TPU v7x, 256 devices: a whole 4x4x8 slice. The times are simulated.
256 devices in a mesh: member: 4 (over y_hi, core), point: 64 (over x, y_lo, z).
Axes of the slice: x: 4, y: 4 (y_hi: 2, y_lo: 2; y = y_hi * 2 + y_lo), z: 8, core: 2. Of those that a mesh axis runs over, the one named last changes fastest.
Arguments:
- final_hidden_states: bfloat16 [16, 49152, 1024], P('member', 'point'), may hold values from -16 to 16
- readout_weights_table: bfloat16 [1024, 100], replicated, may hold values from -0.1875 to 0.1875
- readout_shift: float32 [100], replicated, may hold values from -3 to 3
- observed_truth: float32 [49152, 100], P('point'), may hold values from -6 to 6
- area: float32 [49152], P('point'), may hold values from 0.25 to 4
- quantity_coefficient: float32 [100], replicated, may hold values from 0.25 to 4
Outputs:
- objective_value: float32 [], replicated
- hidden_state_slope: bfloat16 [16, 49152, 1024], P('member', 'point')
- normalised_projection_derivative: float32 [1024, 100], P(('member', 'point'))
- grad_bias: float32 [100], replicated
All inputs are finite; a program needn't handle non-finite values.
Results may differ from a plain program's by a relative error of at most 0.0049.
Values may be sent and summed in bfloat16 or wider, within the bound.
No kernel may reach another device: no remote copies, remote signals or barrier semaphores. Data moves between devices by JAX's collectives and lax.ppermute only.
A program may use at most 128 MiB of HBM per device.

v0:
```python
import jax
import jax.numpy as jnp
from jax import lax
from jax.sharding import PartitionSpec as P

blurring_operator = 0.05
blend_factor_crps = 0.95


def pair_terms(collected_replicas, observed_truth, area, quantity_coefficient):
    drawn_estimates = collected_replicas.shape[0]

    def append_replica(index, carry):
        polarity_slopes_table, blurring_lengths = carry
        other = lax.dynamic_index_in_dim(collected_replicas, index, 0, keepdims=True)
        draw_discrepancy = collected_replicas - other
        blurring_half_width = jnp.sqrt(
            draw_discrepancy * draw_discrepancy + blurring_operator * blurring_operator
        )
        return (
            polarity_slopes_table + draw_discrepancy / blurring_half_width,
            blurring_lengths + blurring_half_width,
        )

    empty_start = jnp.zeros(collected_replicas.shape, jnp.float32)
    polarity_slopes_table, blurring_lengths = lax.fori_loop(
        0, drawn_estimates, append_replica, (empty_start, empty_start)
    )
    draw_discrepancy = collected_replicas - observed_truth[None]
    blurring_half_width = jnp.sqrt(
        draw_discrepancy * draw_discrepancy + blurring_operator * blurring_operator
    )
    corrected_blend_factor = (1.0 - blend_factor_crps) / drawn_estimates
    accuracy_term = jnp.mean(blurring_half_width, axis=0)
    dispersion_term = jnp.sum(blurring_lengths, axis=0) - drawn_estimates * blurring_operator
    continuous_rank_loss = (
        accuracy_term
        - (1.0 - corrected_blend_factor)
        / (2.0 * drawn_estimates * (drawn_estimates - 1))
        * dispersion_term
    )
    cell_factor_table = area[:, None] * quantity_coefficient[None, :]
    loss_part = jnp.sum(cell_factor_table * continuous_rank_loss)
    head_gradients = (
        cell_factor_table[None]
        * (
            draw_discrepancy / blurring_half_width
            - (1.0 - corrected_blend_factor) / (drawn_estimates - 1) * polarity_slopes_table
        )
    ).astype(jnp.bfloat16)
    return (loss_part, head_gradients)


def shards(
    final_hidden_states,
    readout_weights_table,
    readout_shift,
    observed_truth,
    area,
    quantity_coefficient,
):
    local_members, local_points, span_extent = final_hidden_states.shape
    projected_predictions = readout_weights_table.shape[1]
    groups = lax.axis_size("member")
    columns = lax.axis_size("point")
    position = lax.axis_index("member")
    affine_estimate_array = final_hidden_states.reshape(-1, span_extent)
    estimate_layout = (
        jnp.dot(
            affine_estimate_array, readout_weights_table, preferred_element_type=jnp.float32
        ).reshape(local_members, local_points, projected_predictions)
        + readout_shift
    )
    share = local_points // groups
    collected_replicas = lax.all_to_all(
        estimate_layout, "member", split_axis=1, concat_axis=0, tiled=True
    )
    target_share = lax.dynamic_slice_in_dim(observed_truth, position * share, share, 0)
    area_share = lax.dynamic_slice_in_dim(area, position * share, share, 0)
    loss_part, head_gradients = pair_terms(
        collected_replicas, target_share, area_share, quantity_coefficient
    )
    estimate_response = lax.all_to_all(
        head_gradients, "member", split_axis=0, concat_axis=1, tiled=True
    )
    affine_response_array = estimate_response.reshape(-1, projected_predictions)
    total_members = local_members * groups
    total_points = local_points * columns
    scaling_factor = 1.0 / jnp.sqrt(jnp.float32(total_members * total_points))
    normalised_projection_derivative = lax.psum_scatter(
        lax.dot_general(
            affine_estimate_array,
            affine_response_array,
            (((0,), (0,)), ((), ())),
            preferred_element_type=jnp.float32,
        ),
        ("member", "point"),
        scatter_dimension=0,
        tiled=True,
    )
    hidden_state_slope = (
        jnp.dot(affine_response_array, readout_weights_table.T, preferred_element_type=jnp.float32)
        .astype(jnp.bfloat16)
        .reshape(local_members, local_points, span_extent)
    )
    bias_part = jnp.sum(affine_response_array.astype(jnp.float32), axis=0)
    loss_total, bias_total = lax.psum((loss_part, bias_part), ("member", "point"))
    objective_value = loss_total / (total_points * projected_predictions)
    return (
        objective_value,
        hidden_state_slope,
        normalised_projection_derivative * scaling_factor,
        bias_total * scaling_factor,
    )


def solution(mesh):
    placed = (P("member", "point", None), P(), P(), P("point", None), P("point"), P())
    return jax.shard_map(
        shards,
        mesh=mesh,
        in_specs=placed,
        out_specs=(P(), P("member", "point", None), P(("member", "point"), None), P()),
        check_vma=False,
    )
```

profile of v0, /device:TPU:1, one launch (start us, length us, event | category | flops | bytes accessed | tf_op | source)
XLA Modules:
  0.0 411.0 jit_solution(18234872642239653404)
XLA Ops:
  7.2 5.0 %convolution_add_fusion = f32[4,768,100]{1,2,0:T(8,128)S(1)} fusion(bf16[4,768,1024]{2,1,0:T(8,128)(2,1)} %param.8, f32[100]{0:T(128)} %param.10, bf16[1024,100]{0,1:T(8,128)(2,1)} %param.9), kind=kOutput, calls=%fused_computation.12 | convolution fusion | flops 629452800 | bytes 7725456 | tf_op jit(solution)/shard_map/dot_general | solution.py:69
  13.8 6.8 %all-to-all-start = ((f32[4,768,100]{2,0,1:T(4,128)}), f32[4,768,100]{2,0,1:T(4,128)S(1)}, u32[]{:S(2)}, u32[]{:S(2)}) async-start(f32[4,768,100]{2,0,1:T(4,128)} %copy.35), calls=%async_computation | async-start | bytes 3145728 | tf_op jit(solution)/shard_map/all_to_all | solution.py:75
  22.1 1.6 copy.39
  23.7 17.6 %all-to-all-done = f32[4,768,100]{2,0,1:T(4,128)S(1)} async-done(((f32[4,768,100]{2,0,1:T(4,128)}), f32[4,768,100]{2,0,1:T(4,128)S(1)}, u32[]{:S(2)}, u32[]{:S(2)}) %all-to-all-start) | async-done | bytes 1228832 | tf_op jit(solution)/shard_map/all_to_all | solution.py:75
  41.3 2.0 copy.42
  43.3 3.9 fusion.3
  50.4 70.6 %while.16 = (s32[]{:T(128)}, f32[16,192,100]{2,1,0:T(8,128)}, f32[16,192,100]{2,1,0:T(8,128)S(1)}, f32[16,192,100]{2,1,0:T(8,128)S(1)}, s32[]{:T(128)}, /*index=5*/s32[]{:T(128)}) while((s32[]{:T(128)}, f32[16,192,100]{2,1,0:T(8,128)}, f32[16,192,100]{2,1,0:T(8,128)S(1)}, f32[16,192,100]{2,1,0:T(8,128)S(1)}, s32[]{:T(128)}, ...), condition=%wide.region_2.3_spmd.clone, body=%wide.region_1.2_spmd.clone.sunk | while | flops 2457603 | bytes 6374483 | solution.py:26
  51.1 3.2 select_add_fusion.3
  55.0 3.8 select_add_fusion.3
  59.4 3.8 select_add_fusion.3
  63.9 3.8 select_add_fusion.3
  68.3 3.8 select_add_fusion.3
  72.8 3.8 select_add_fusion.3
  77.2 3.8 select_add_fusion.3
  81.7 3.8 select_add_fusion.3
  86.1 3.8 select_add_fusion.3
  90.6 3.8 select_add_fusion.3
  95.0 3.8 select_add_fusion.3
  99.5 3.8 select_add_fusion.3
  103.9 3.8 select_add_fusion.3
  108.4 3.8 select_add_fusion.3
  112.8 3.8 select_add_fusion.3
  117.3 3.8 select_add_fusion.3
  121.8 1.6 broadcast_multiply_fusion
  123.5 2.8 multiply_convert_fusion
  126.2 4.3 %all-to-all-start.1 = ((bf16[16,192,100]{2,1,0:T(8,128)(2,1)}), bf16[16,192,100]{2,1,0:T(8,128)(2,1)S(1)}, u32[]{:S(2)}, u32[]{:S(2)}) async-start(bf16[16,192,100]{2,1,0:T(8,128)(2,1)} %multiply_convert_fusion), calls=%async_computation.1 | async-start | bytes 1572864 | tf_op jit(solution)/shard_map/all_to_all | solution.py:83
  130.5 12.3 %all-to-all-done.1 = bf16[16,192,100]{2,1,0:T(8,128)(2,1)S(1)} async-done(((bf16[16,192,100]{2,1,0:T(8,128)(2,1)}), bf16[16,192,100]{2,1,0:T(8,128)(2,1)S(1)}, u32[]{:S(2)}, u32[]{:S(2)}) %all-to-all-start.1) | async-done | bytes 614432 | tf_op jit(solution)/shard_map/all_to_all | solution.py:83
  144.6 2.4 reshape.48
  147.0 4.6 %convolution_convert_fusion = bf16[3072,1024]{1,0:T(8,128)(2,1)} fusion(bf16[3072,100]{0,1:T(8,128)(2,1)S(1)} %reshape.48, bf16[1024,100]{0,1:T(8,128)(2,1)S(1)} %copy-done.3), kind=kOutput, calls=%fused_computation.4 | convolution fusion | flops 632291328 | bytes 7110656 | tf_op jit(solution)/shard_map/dot_general | solution.py:102
  151.6 1.9 convolution_bitcast_fusion
  153.5 78.5 %all-reduce.1 = (f32[]{:T(128)}, f32[100]{0:T(128)S(1)}) all-reduce(f32[]{:T(128)} %get-tuple-element.138, f32[100]{0:T(128)S(1)} %convert_reduce_fusion), channel_id=1, replica_groups=mesh['member'=4,'point'=64] {'member','point'}, use_global_device_ids=true, to_apply=%region_5.6 | all-reduce | flops 101 | bytes 808 | tf_op jit(solution)/shard_map/psum | solution.py:107
  233.2 168.3 %all-reduce.4.cloned.1.call-done = f32[1024,100]{0,1:T(8,128)} async-done(((f32[1024,100]{0,1:T(8,128)}), f32[1024,100]{0,1:T(8,128)}) %all-reduce.4.cloned.1.call-update) | async-done | bytes 409616
  (46 shorter events, 21.2 us)
Async XLA Ops:
  7.2 14.2 %copy-start = (f32[768,100]{0,1:T(8,128)S(1)}, f32[768,100]{0,1:T(8,128)}, u32[]{:S(2)}) copy-start(f32[768,100]{0,1:T(8,128)} %param.11) | copy-start | bytes 921604
  13.8 27.5 %all-to-all-start = ((f32[4,768,100]{2,0,1:T(4,128)}), f32[4,768,100]{2,0,1:T(4,128)S(1)}, u32[]{:S(2)}, u32[]{:S(2)}) async-start(f32[4,768,100]{2,0,1:T(4,128)} %copy.35), calls=%async_computation | async-start | bytes 3145728 | tf_op jit(solution)/shard_map/all_to_all | solution.py:75
  41.3 2.0 copy-start.1
  121.1 0.8 copy-start.4
  126.2 16.6 %all-to-all-start.1 = ((bf16[16,192,100]{2,1,0:T(8,128)(2,1)}), bf16[16,192,100]{2,1,0:T(8,128)(2,1)S(1)}, u32[]{:S(2)}, u32[]{:S(2)}) async-start(bf16[16,192,100]{2,1,0:T(8,128)(2,1)} %multiply_convert_fusion), calls=%async_computation.1 | async-start | bytes 1572864 | tf_op jit(solution)/shard_map/all_to_all | solution.py:83
  130.5 270.9 %all-reduce.4.cloned.1.call-start = ((), (), s32[]{:S(2)}) async-start(), calls=%async_computation.2 | async-start | bytes 851968
  142.8 4.2 %copy-start.3 = (bf16[1024,100]{0,1:T(8,128)(2,1)S(1)}, bf16[1024,100]{0,1:T(8,128)(2,1)}, u32[]{:S(2)}) copy-start(bf16[1024,100]{0,1:T(8,128)(2,1)} %param.9) | copy-start | bytes 614404
  143.7 0.9 copy-start.2
  144.6 7.0 %slice-start = ((s8[6291456]{0:T(1024)(128)(4,1)}), s8[2097152]{0:T(1024)(128)(4,1)S(1)}, s32[]{:S(2)}) async-start(s8[6291456]{0:T(1024)(128)(4,1)} %bitcast.40), calls=%async_computation.3 | async-start | bytes 4194304
  147.0 4.6 %slice-start.1 = ((s8[6291456]{0:T(1024)(128)(4,1)}), s8[4194304]{0:T(1024)(128)(4,1)S(1)}, s32[]{:S(2)}) async-start(s8[6291456]{0:T(1024)(128)(4,1)} %bitcast.40), calls=%async_computation.4 | async-start | bytes 8388608
Sparse Core Ops, SparseCore 0:
  153.6 247.7 all-reduce.3
where the time goes:
time: 413 us; the launch traced here: 411 us
  waiting for transfers between devices  198 us (48%)
  blocking collectives  78.5 us (19%)
  other arithmetic  71.6 us (17%)
  local copies, waits for them, and re-layouts  24.2 us (6%)
  between operations  15.9 us (4%)
  matrix products  11.5 us (3%)
  starting transfers between devices  11.1 us (3%)
    unnamed x2, waiting for transfers between devices  168 us
    psum x1, blocking collectives, shards(): lax.psum((loss_part, bias_part), ('member', 'point'))  78.5 us
    add x16, other arithmetic, append_replica(): blurring_lengths + blurring_half_width  60.3 us
    all_to_all x1, waiting for transfers between devices, shards(): lax.all_to_all(estimate_layout, 'member', split_axis=1, concat_axis=0, ti...  17.6 us
    all_to_all x1, waiting for transfers between devices, shards(): lax.all_to_all(head_gradients, 'member', split_axis=0, concat_axis=1, til...  12.3 us
    sub x16, local copies, waits for them, and re-layouts, append_replica(): draw_discrepancy = collected_replicas - other  10.4 us
  transfers between devices with their start and end apart: 3, of which 3 were waited for; matrix products, arithmetic and copies ran while one was open for 1% of the time, Pallas kernels for 0%

commit v1 on v0

v1 whole, which is shorter than its diff:
```python
import functools

import jax
import jax.numpy as jnp
from jax import lax
from jax.experimental import pallas as pl
from jax.experimental.pallas import tpu as pltpu
from jax.sharding import PartitionSpec as P

F32 = jnp.float32
BF16 = jnp.bfloat16
LANES = 128
TILES = (6,)
SMOOTH = 0.05 * 0.05
ALPHA = 0.95
VMEM_LIMIT = 48 * 1024 * 1024


def params():
    return pltpu.CompilerParams(vmem_limit_bytes=VMEM_LIMIT)


def round_up(n, k):
    return -(-n // k) * k


def forecast_kernel(x_ref, w_ref, own_ref, sent_ref, wpad, wt):
    members, _, width = x_ref.shape
    rows = own_ref.shape[1]
    fields = w_ref.shape[1]

    @pl.when(pl.program_id(0) == 0)
    def _():
        wpad[...] = jnp.zeros_like(wpad)
        wpad[:, :fields] = w_ref[...]
        wt[...] = wpad[...].T

    x = x_ref[...].reshape(members * LANES, width)
    f = lax.dot_general(
        wt[...], x, (((1,), (1,)), ((), ())), preferred_element_type=F32
    )[:rows]
    own_ref[0] = f
    groups = [
        f[8 * g : 8 * g + 8, m * LANES : (m + 1) * LANES]
        for g in range(rows // 8)
        for m in range(members)
    ]
    sent_ref[0] = jnp.concatenate(groups, axis=0).astype(BF16)


def column(row, rows):
    return jnp.broadcast_to(row, (LANES, LANES)).T[:rows]


def pad_row(ref, scratch, fields):
    scratch[...] = jnp.zeros_like(scratch)
    scratch[:, :fields] = ref[...]
    return scratch[...]


def slope_and_length(d):
    t = d * d + SMOOTH
    r = lax.rsqrt(t)
    return d * r, t * r


def near_kernel(own_ref, sib_ref, truth_ref, area_ref, shift_ref, coef_ref, acc_ref, loss_ref, tpad, rpad, shifts, coefs, *, members, total):
    rows = own_ref.shape[1]
    fields = truth_ref.shape[1]
    c1 = (1.0 - (1.0 - ALPHA) / total) / (total - 1)
    c2 = (1.0 - (1.0 - ALPHA) / total) / (2.0 * total * (total - 1))

    @pl.when(pl.program_id(0) == 0)
    def _():
        shifts[...] = column(pad_row(shift_ref, rpad, fields), rows)
        coefs[...] = column(pad_row(coef_ref, rpad, fields), rows)
        tpad[...] = jnp.zeros_like(tpad)
        loss_ref[...] = jnp.zeros_like(loss_ref)

    tpad[:, :fields] = truth_ref[...]
    truth = tpad[...].T[:rows] - shifts[...]
    loss = jnp.zeros((8, LANES), F32)
    for g in range(rows // 8):
        span = slice(8 * g, 8 * g + 8)
        own = [own_ref[0, span, m * LANES : (m + 1) * LANES] for m in range(members)]
        sib = sib_ref[0, 8 * members * g : 8 * members * (g + 1), :].astype(F32)
        skill = jnp.zeros((8, LANES), F32)
        spread = jnp.zeros((8, LANES), F32)
        inner = jnp.zeros((8, LANES), F32)
        slopes = [jnp.zeros((8, LANES), F32) for _ in range(members)]
        for m in range(members):
            for n in range(m + 1, members):
                a, b = slope_and_length(own[m] - own[n])
                slopes[m] = slopes[m] + a
                slopes[n] = slopes[n] - a
                inner = inner + b
            for n in range(members):
                a, b = slope_and_length(own[m] - sib[8 * n : 8 * n + 8])
                slopes[m] = slopes[m] + a
                spread = spread + b
        for m in range(members):
            a, b = slope_and_length(own[m] - truth[span])
            skill = skill + b
            acc_ref[0, span, m * LANES : (m + 1) * LANES] = a - c1 * slopes[m]
        loss = loss + coefs[span] * (skill * (1.0 / total) - c2 * (spread + 2.0 * inner))
    loss_ref[...] += loss * area_ref[...]


def far_kernel(own_ref, far_ref, fwd_ref, acc_ref, area_ref, coef_ref, x_ref, grad_ref, dw_ref, bias_ref, loss_ref, rpad, coefs, grads, *, members, total):
    rows = own_ref.shape[1]
    fields = coef_ref.shape[1]
    width = x_ref.shape[2]
    c1 = (1.0 - (1.0 - ALPHA) / total) / (total - 1)
    c2 = (1.0 - (1.0 - ALPHA) / total) / (2.0 * total * (total - 1))

    @pl.when(pl.program_id(0) == 0)
    def _():
        coefs[...] = column(pad_row(coef_ref, rpad, fields), rows)
        loss_ref[...] = jnp.zeros_like(loss_ref)
        dw_ref[...] = jnp.zeros_like(dw_ref)
        bias_ref[...] = jnp.zeros_like(bias_ref)
        grads[...] = jnp.zeros_like(grads)

    area = jnp.broadcast_to(area_ref[...], (8, LANES))
    loss = jnp.zeros((8, LANES), F32)
    for g in range(rows // 8):
        span = slice(8 * g, 8 * g + 8)
        part = slice(8 * members * g, 8 * members * (g + 1))
        own = [own_ref[0, span, m * LANES : (m + 1) * LANES] for m in range(members)]
        far = far_ref[0, part, :].astype(F32)
        fwd = fwd_ref[0, part, :].astype(F32)
        spread = jnp.zeros((8, LANES), F32)
        scale = coefs[span] * area
        bias = jnp.zeros((8, LANES), F32)
        for m in range(members):
            slopes = jnp.zeros((8, LANES), F32)
            for other in (far, fwd):
                for n in range(members):
                    a, b = slope_and_length(own[m] - other[8 * n : 8 * n + 8])
                    slopes = slopes + a
                    spread = spread + b
            here = slice(m * LANES, (m + 1) * LANES)
            grad = (scale * (acc_ref[0, span, here] - c1 * slopes)).astype(BF16).astype(F32)
            grads[span, here] = grad
            bias = bias + grad
        bias_ref[span, :] += bias
        loss = loss + coefs[span] * spread
    loss_ref[...] -= c2 * loss * area
    grad = grads[...].astype(BF16)
    grad_ref[0] = grad
    dw_ref[...] += jnp.dot(grad, x_ref[...].reshape(members * LANES, width), preferred_element_type=F32)


def pack_kernel(*refs, chunks, fields):
    dws, biases, losses = refs[:chunks], refs[chunks : 2 * chunks], refs[2 * chunks : 4 * chunks]
    out_ref = refs[4 * chunks]
    padded = refs[4 * chunks + 1]
    dw = sum(r[...] for r in dws)
    padded[...] = jnp.zeros_like(padded)
    padded[: biases[0].shape[0], :] = sum(r[...] for r in biases)
    bias = jnp.sum(padded[...].T, axis=0, keepdims=True)
    loss = sum(r[...] for r in losses)
    loss = jnp.sum(jnp.sum(loss, axis=0, keepdims=True), axis=1, keepdims=True)
    high = loss.astype(BF16).astype(F32)
    low = loss - high
    quarter = fields // 4
    lane = lax.broadcasted_iota(jnp.int32, (8, LANES), 1)
    row = lax.broadcasted_iota(jnp.int32, (8, LANES), 0) % 4
    bias = jnp.broadcast_to(bias, (8, LANES))
    extra = jnp.zeros((8, LANES), F32)
    for r in range(4):
        moved = pltpu.roll(bias, fields - quarter * r, 1)
        extra = jnp.where(row == r, moved, extra)
    extra = jnp.where(lane < fields + quarter, extra, 0.0)
    at = lane == fields + quarter
    extra = jnp.where(at & (row == 0), high, extra)
    extra = jnp.where(at & (row == 1), low, extra)
    table = dw.T.reshape(-1, 8, LANES)
    keep = lax.broadcasted_iota(jnp.int32, table.shape, 2) < fields
    table = jnp.where(keep, table, extra[None])
    out_ref[...] = table.reshape(out_ref.shape).astype(BF16)


def slope_kernel(grad_ref, w_ref, out_ref, wpad):
    fields = w_ref.shape[1]

    @pl.when(pl.program_id(0) == 0)
    def _():
        wpad[...] = jnp.zeros_like(wpad)
        wpad[:, :fields] = w_ref[...]

    s = lax.dot_general(
        grad_ref[0], wpad[...], (((0,), (1,)), ((), ())), preferred_element_type=F32
    )
    out_ref[...] = s.astype(BF16).reshape(out_ref.shape)


def finish_kernel(parts_ref, dw_ref, bias_ref, loss_ref, *, fields, scale, count):
    parts = parts_ref[...].astype(F32).reshape(-1, 8, LANES)
    total = jnp.sum(parts, axis=0)
    total = total[:4] + total[4:]
    dw_ref[...] = total[:, :fields] * scale
    quarter = fields // 4
    lane = lax.broadcasted_iota(jnp.int32, (1, LANES), 1)
    bias = jnp.zeros((1, LANES), F32)
    for r in range(4):
        moved = pltpu.roll(total, (quarter * r - fields) % LANES, 1)[r : r + 1]
        bias = jnp.where((lane >= quarter * r) & (lane < quarter * (r + 1)), moved, bias)
    bias_ref[...] = bias[:, :fields] * scale
    at = fields + quarter
    loss_ref[...] = (total[0:1, at : at + 1] + total[1:2, at : at + 1]) * (1.0 / count)


def shards(hidden, weights, shift, truth, area, coef):
    members, points, width = hidden.shape
    fields = weights.shape[1]
    total = members * lax.axis_size("member")
    all_points = points * lax.axis_size("point")
    rows = round_up(fields, 8)
    depth = round_up(fields, 16)
    span = members * LANES
    shift, coef, area = shift[None], coef[None], area[None]
    fixed = lambda shape: pl.BlockSpec(shape, lambda i: (0,) * len(shape))
    tile = lambda shape: pl.BlockSpec((1,) + shape, lambda i: (i, 0, 0))
    shape = jax.ShapeDtypeStruct
    core_swap = [(0, 1), (1, 0), (2, 3), (3, 2)]
    chip_swap = [(0, 2), (1, 3), (2, 0), (3, 1)]

    sent = []
    first = 0
    for n in TILES:
        at = lambda i, first=first: (0, first + i, 0)
        own, out = pl.pallas_call(
            forecast_kernel,
            grid=(n,),
            in_specs=[pl.BlockSpec((members, LANES, width), at), fixed((width, fields))],
            out_specs=[tile((rows, span)), tile((rows * members, LANES))],
            out_shape=[shape((n, rows, span), F32), shape((n, rows * members, LANES), BF16)],
            scratch_shapes=[pltpu.VMEM((width, LANES), BF16), pltpu.VMEM((LANES, width), BF16)],
            compiler_params=params(),
            name="forecast",
        )(hidden, weights)
        far = lax.ppermute(out, "member", chip_swap)
        sib = lax.ppermute(out, "member", core_swap)
        sent.append((n, first, own, far, sib))
        first += n

    near = []
    for n, first, own, far, sib in sent:
        at = lambda i, first=first: (first + i, 0)
        along = lambda i, first=first: (0, first + i)
        acc, loss = pl.pallas_call(
            functools.partial(near_kernel, members=members, total=total),
            grid=(n,),
            in_specs=[
                tile((rows, span)),
                tile((rows * members, LANES)),
                pl.BlockSpec((LANES, fields), at),
                pl.BlockSpec((1, LANES), along),
                fixed((1, fields)),
                fixed((1, fields)),
            ],
            out_specs=[tile((rows, span)), fixed((8, LANES))],
            out_shape=[shape((n, rows, span), F32), shape((8, LANES), F32)],
            scratch_shapes=[
                pltpu.VMEM((LANES, LANES), F32),
                pltpu.VMEM((1, LANES), F32),
                pltpu.VMEM((rows, LANES), F32),
                pltpu.VMEM((rows, LANES), F32),
            ],
            compiler_params=params(),
            name="near",
        )(own, sib, truth, area, shift, coef)
        near.append((acc, loss))

    grads, dws, biases, losses = [], [], [], []
    for (n, first, own, far, _), (acc, loss) in zip(sent, near):
        fwd = lax.ppermute(far, "member", core_swap)
        at = lambda i, first=first: (0, first + i, 0)
        along = lambda i, first=first: (0, first + i)
        grad, dw, bias, far_loss = pl.pallas_call(
            functools.partial(far_kernel, members=members, total=total),
            grid=(n,),
            in_specs=[
                tile((rows, span)),
                tile((rows * members, LANES)),
                tile((rows * members, LANES)),
                tile((rows, span)),
                pl.BlockSpec((1, LANES), along),
                fixed((1, fields)),
                pl.BlockSpec((members, LANES, width), at),
            ],
            out_specs=[tile((LANES, span)), fixed((LANES, width)), fixed((rows, LANES)), fixed((8, LANES))],
            out_shape=[
                shape((n, LANES, span), BF16),
                shape((LANES, width), F32),
                shape((rows, LANES), F32),
                shape((8, LANES), F32),
            ],
            scratch_shapes=[
                pltpu.VMEM((1, LANES), F32),
                pltpu.VMEM((rows, LANES), F32),
                pltpu.VMEM((LANES, span), F32),
            ],
            compiler_params=params(),
            name="far",
        )(own, far, fwd, acc, area, coef, hidden)
        grads.append(grad)
        dws.append(dw)
        biases.append(bias)
        losses += [loss, far_loss]

    packed = pl.pallas_call(
        functools.partial(pack_kernel, chunks=len(TILES), fields=fields),
        out_shape=shape((width, LANES), BF16),
        scratch_shapes=[pltpu.VMEM((LANES, LANES), F32)],
        compiler_params=params(),
        name="pack",
    )(*dws, *biases, *losses)
    parts = lax.all_to_all(packed, ("member", "point"), split_axis=0, concat_axis=0, tiled=True)

    grad = grads[0] if len(grads) == 1 else jnp.concatenate(grads, axis=0)
    slope = pl.pallas_call(
        slope_kernel,
        grid=(points // LANES,),
        in_specs=[tile((LANES, span)), fixed((width, fields))],
        out_specs=pl.BlockSpec((members, LANES, width), lambda i: (0, i, 0)),
        out_shape=shape(hidden.shape, BF16),
        scratch_shapes=[pltpu.VMEM((width, LANES), BF16)],
        compiler_params=params(),
        cost_estimate=pl.CostEstimate(flops=2 * members * points * width * LANES, bytes_accessed=4 * members * points * width, transcendentals=0),
        name="slope",
    )(grad, weights)

    own_rows = width // (lax.axis_size("member") * lax.axis_size("point"))
    dw, bias, loss = pl.pallas_call(
        functools.partial(
            finish_kernel, fields=fields, scale=float((total * all_points) ** -0.5), count=float(all_points * fields)
        ),
        out_shape=[shape((own_rows, fields), F32), shape((1, fields), F32), shape((1, 1), F32)],
        compiler_params=params(),
        name="finish",
    )(parts)
    return loss.reshape(()), slope, dw, bias.reshape(fields)


def solution(mesh):
    placed = (P("member", "point", None), P(), P(), P("point", None), P("point"), P())
    return jax.shard_map(
        shards,
        mesh=mesh,
        in_specs=placed,
        out_specs=(P(), P("member", "point", None), P(("member", "point"), None), P()),
        check_vma=False,
    )
```

time: 413 us -> 71.9 us (0.17)
  waiting for transfers between devices: 198 us -> 22.9 us
  blocking collectives: 78.5 us -> 0 us
  other arithmetic: 71.6 us -> 0 us
  Pallas kernels: 0 us -> 25.2 us
  local copies, waits for them, and re-layouts: 24.2 us -> 1.35 us
  between operations: 15.9 us -> 0.73 us
  matrix products: 11.5 us -> 0 us
  starting transfers between devices: 11.1 us -> 21.2 us
    unnamed x2 -> x0, waiting for transfers between devices: 168 us -> none
    psum x1 -> x0, blocking collectives: 78.5 us -> none  [shards(): lax.psum((loss_part, bias_part), ('member', 'point'))]
    add x16 -> x0, other arithmetic: 60.3 us -> none  [append_replica(): blurring_lengths + blurring_half_width]
    pallas_call x0 -> x6, Pallas kernels: none -> 25.2 us  [the longest x1 7.41 us: shards(): pl.pallas_call(functools.partial(far_kernel, members=members, total=total...]
    all_to_all x2 -> x1, waiting for transfers between devices: 29.9 us -> 10.5 us  [shards(): lax.all_to_all(packed, ('member', 'point'), split_axis=0, concat_axis=0,...]
    ppermute x0 -> x3, waiting for transfers between devices: none -> 12.4 us  [the longest x1 12.4 us: shards(): far = lax.ppermute(out, 'member', chip_swap)]
    dot_general x3 -> x0, matrix products: 11.5 us -> none  [the longest x1 5.04 us: shards(): jnp.dot(affine_estimate_array, readout_weights_table, preferred_element_t...]
    sub x16 -> x0, local copies, waits for them, and re-layouts: 10.4 us -> none  [append_replica(): draw_discrepancy = collected_replicas - other]
  transfers between devices with their start and end apart: 3 -> 4, of which waited for: 3 -> 2; matrix products, arithmetic and copies ran while one was open for 1% -> 0% of each run, Pallas kernels for 0% -> 13%
where the time goes in v1:
time: 71.9 us; the launch traced here: 71.4 us
  Pallas kernels  25.2 us (35%)
  waiting for transfers between devices  22.9 us (32%)
  starting transfers between devices  21.2 us (29%)
  local copies, waits for them, and re-layouts  1.35 us (2%)
  between operations  0.73 us (1%)
    all_to_all x1, starting transfers between devices, shards(): lax.all_to_all(packed, ('member', 'point'), split_axis=0, concat_axis=0,...  14.3 us
    ppermute x1, waiting for transfers between devices, shards(): far = lax.ppermute(out, 'member', chip_swap)  12.4 us
    all_to_all x1, waiting for transfers between devices, shards(): lax.all_to_all(packed, ('member', 'point'), split_axis=0, concat_axis=0,...  10.5 us
    pallas_call x1, Pallas kernels, shards(): pl.pallas_call(functools.partial(far_kernel, members=members, total=total...  7.41 us
    pallas_call x1, Pallas kernels, shards(): pl.pallas_call(forecast_kernel, grid=(n,), in_specs=[pl.BlockSpec((member...  6.8 us
    pallas_call x1, Pallas kernels, shards(): pl.pallas_call(slope_kernel, grid=(points // LANES,), in_specs=[tile((LAN...  4.84 us
    pallas_call x1, Pallas kernels, shards(): pl.pallas_call(functools.partial(near_kernel, members=members, total=tota...  4.49 us
    ppermute x1, starting transfers between devices, shards(): far = lax.ppermute(out, 'member', chip_swap)  3.74 us
  transfers between devices with their start and end apart: 4, of which 2 were waited for; matrix products, arithmetic and copies ran while one was open for 0% of the time, Pallas kernels for 13%

profile of v1, /device:TPU:1, one launch (start us, length us, event | category | flops | bytes accessed | tf_op | source)
XLA Modules:
  0.0 71.4 jit_solution(6352280252349924315)
XLA Ops:
  0.6 0.0 copy-start.3
  0.6 0.0 copy-start.2
  0.7 0.0 copy-start
  0.7 0.0 copy-start.1
  0.7 1.2 %copy.10.w_ref = bf16[1024,100]{1,0:T(8,128)(2,1)S(1)} copy(bf16[1024,100]{0,1:T(8,128)(2,1)} %param.7) | data formatting | bytes 409600 | tf_op args[1]
  1.8 6.8 %forecast.1 = (f32[6,104,512]{2,1,0:T(8,128)S(1)}, bf16[6,416,128]{2,1,0:T(8,128)(2,1)}) custom-call(bf16[4,768,1024]{2,1,0:T(8,128)(2,1)} %x_ref.3, bf16[1024,100]{1,0:T(8,128)(2,1)S(1)} %copy.10.w_ref), custom_call_target="tpu_custom_call" | custom-call | tf_op jit(solution)/shard_map/forecast/pallas_call | solution.py:233
  8.6 3.7 %collective-permute-start = (bf16[6,416,128]{2,1,0:T(8,128)(2,1)}, bf16[6,416,128]{2,1,0:T(8,128)(2,1)S(1)}, u32[]{:S(2)}, u32[]{:S(2)}) collective-permute-start(bf16[6,416,128]{2,1,0:T(8,128)(2,1)} %get-tuple-element.16), channel_id=1, source_target_pairs={{0,128},{64,192},{128,0},{192,64},{1,129},{65,193},{129,1},{193,65... | collective-permute-start | bytes 1916936 | tf_op jit(solution)/shard_map/ppermute | solution.py:243
  12.4 1.0 %collective-permute-start.2 = (bf16[6,416,128]{2,1,0:T(8,128)(2,1)}, bf16[6,416,128]{2,1,0:T(8,128)(2,1)}, u32[]{:S(2)}, u32[]{:S(2)}) collective-permute-start(bf16[6,416,128]{2,1,0:T(8,128)(2,1)} %get-tuple-element.16), channel_id=1, source_target_pairs={{0,64},{64,0},{128,192},{192,128},{1,65},{65,1},{129,193},{193,129... | collective-permute-start | bytes 1916936 | tf_op jit(solution)/shard_map/ppermute | solution.py:244
  13.3 12.4 %collective-permute-done.far_ref = bf16[6,416,128]{2,1,0:T(8,128)(2,1)S(1)} collective-permute-done((bf16[6,416,128]{2,1,0:T(8,128)(2,1)}, bf16[6,416,128]{2,1,0:T(8,128)(2,1)S(1)}, u32[]{:S(2)}, u32[]{:S(2)}) %collective-permute-start) | collective-permute-done | bytes 639008 | tf_op jit(solution)/shard_map/ppermute | solution.py:243
  25.7 2.2 %collective-permute-start.1 = (bf16[6,416,128]{2,1,0:T(8,128)(2,1)S(1)}, bf16[6,416,128]{2,1,0:T(8,128)(2,1)}, u32[]{:S(2)}, u32[]{:S(2)}) collective-permute-start(bf16[6,416,128]{2,1,0:T(8,128)(2,1)S(1)} %collective-permute-done.far_ref), channel_id=1, source_target_pairs={{0,64},{64,0},{128,192},{192,128},{1,65},{65,1},{129,193},{193,129... | collective-permute-start | bytes 1916936 | tf_op jit(solution)/shard_map/ppermute | solution.py:278
  27.9 0.0 copy-done.3
  27.9 0.0 copy-done.2
  27.9 0.2 copy.11.truth_ref
  28.1 0.0 collective-permute-done.2.sib_ref
  28.1 0.0 copy-done
  28.1 0.0 copy-done.1
  28.1 4.5 %near.1 = (f32[6,104,512]{2,1,0:T(8,128)S(1)}, f32[8,128]{1,0:T(8,128)S(1)}) custom-call(f32[6,104,512]{2,1,0:T(8,128)S(1)} %get-tuple-element.15.own_ref, bf16[6,416,128]{2,1,0:T(8,128)(2,1)} %collective-permute-done.2.sib_ref, f32[768,100]{1,0:T(8,128)S(1)} %copy.11.truth_ref, f32[1,768]{1,0:T(1,128)S(1)} %broadcast_in_dim.9.area_ref, ...), custom_call_target="tpu_custom_call" | custom-call | tf_op jit(solution)/shard_map/near/pallas_call | solution.py:252
  32.6 0.0 collective-permute-done.1.fwd_ref
  32.7 7.4 %far.1 = (bf16[6,128,512]{2,1,0:T(8,128)(2,1)S(1)}, f32[128,1024]{1,0:T(8,128)S(1)}, f32[104,128]{1,0:T(8,128)S(1)}, f32[8,128]{1,0:T(8,128)S(1)}) custom-call(f32[6,104,512]{2,1,0:T(8,128)S(1)} %get-tuple-element.15.own_ref, bf16[6,416,128]{2,1,0:T(8,128)(2,1)S(1)} %collective-permute-done.far_ref, bf16[6,416,128]{2,1,0:T(8,128)(2,1)} %collective-permute-done.1.fwd_ref, ...), custom_call_target="tpu_custom_call" | custom-call | tf_op jit(solution)/shard_map/far/pallas_call | solution.py:281
  40.1 1.0 %pack.1 = bf16[1024,128]{1,0:T(8,128)(2,1)} custom-call(f32[128,1024]{1,0:T(8,128)S(1)} %get-tuple-element.18.refs_0_, f32[104,128]{1,0:T(8,128)S(1)} %get-tuple-element.19.refs_1_, f32[8,128]{1,0:T(8,128)S(1)} %get-tuple-element.20.refs_2_, f32[8,128]{1,0:T(8,128)S(1)} %get-tuple-element.21.refs_3_), custom_call_target="tpu_custom_call" | custom-call | tf_op jit(solution)/shard_map/pack/pallas_call | solution.py:313
  41.0 14.3 %all-to-all-start = ((bf16[256,4,128]{2,1,0:T(4,128)(2,1)}), bf16[256,4,128]{2,1,0:T(4,128)(2,1)S(1)}, u32[]{:S(2)}, u32[]{:S(2)}) async-start(bf16[256,4,128]{2,1,0:T(4,128)(2,1)} %bitcast.2), calls=%async_computation | async-start | bytes 524288 | tf_op jit(solution)/shard_map/all_to_all | solution.py:320
  55.4 4.8 %slope.1 = bf16[4,768,1024]{2,1,0:T(8,128)(2,1)} custom-call(bf16[6,128,512]{2,1,0:T(8,128)(2,1)S(1)} %get-tuple-element.23.grad_ref, bf16[1024,100]{1,0:T(8,128)(2,1)S(1)} %copy.10.w_ref), custom_call_target="tpu_custom_call" | custom-call | flops 805306368 | bytes 12582912 | tf_op jit(solution)/shard_map/slope/pallas_call | solution.py:323
  60.2 10.5 %all-to-all-done = bf16[256,4,128]{2,1,0:T(4,128)(2,1)S(1)} async-done(((bf16[256,4,128]{2,1,0:T(4,128)(2,1)}), bf16[256,4,128]{2,1,0:T(4,128)(2,1)S(1)}, u32[]{:S(2)}, u32[]{:S(2)}) %all-to-all-start) | async-done | bytes 262176 | tf_op jit(solution)/shard_map/all_to_all | solution.py:320
  70.7 0.7 %finish.1 = (f32[4,100]{1,0:T(4,128)}, f32[1,100]{1,0:T(1,128)}, f32[1,1]{1,0:T(1,128)}) custom-call(bf16[1024,128]{1,0:T(8,128)(2,1)S(1)} %bitcast.6), custom_call_target="tpu_custom_call" | custom-call | tf_op jit(solution)/shard_map/finish/pallas_call | solution.py:336
  (1 shorter events, 0.0 us)
Async XLA Ops:
  0.6 27.3 %copy-start.3 = (f32[768]{0:T(1024)S(1)}, f32[768]{0:T(1024)}, u32[]{:S(2)}) copy-start(f32[768]{0:T(1024)} %param.10) | copy-start | bytes 9220
  0.6 27.3 %copy-start.2 = (f32[768,100]{0,1:T(8,128)S(1)}, f32[768,100]{0,1:T(8,128)}, u32[]{:S(2)}) copy-start(f32[768,100]{0,1:T(8,128)} %param.9) | copy-start | bytes 921604
  0.7 27.5 %copy-start = (f32[100]{0:T(128)S(1)}, f32[100]{0:T(128)}, u32[]{:S(2)}) copy-start(f32[100]{0:T(128)} %param.11) | copy-start | bytes 1204
  0.7 27.5 %copy-start.1 = (f32[100]{0:T(128)S(1)}, f32[100]{0:T(128)}, u32[]{:S(2)}) copy-start(f32[100]{0:T(128)} %param.8) | copy-start | bytes 1204
  8.6 17.1 %collective-permute-start = (bf16[6,416,128]{2,1,0:T(8,128)(2,1)}, bf16[6,416,128]{2,1,0:T(8,128)(2,1)S(1)}, u32[]{:S(2)}, u32[]{:S(2)}) collective-permute-start(bf16[6,416,128]{2,1,0:T(8,128)(2,1)} %get-tuple-element.16), channel_id=1, source_target_pairs={{0,128},{64,192},{128,0},{192,64},{1,129},{65,193},{129,1},{193,65... | collective-permute-start | bytes 1916936 | tf_op jit(solution)/shard_map/ppermute | solution.py:243
  12.4 15.7 %collective-permute-start.2 = (bf16[6,416,128]{2,1,0:T(8,128)(2,1)}, bf16[6,416,128]{2,1,0:T(8,128)(2,1)}, u32[]{:S(2)}, u32[]{:S(2)}) collective-permute-start(bf16[6,416,128]{2,1,0:T(8,128)(2,1)} %get-tuple-element.16), channel_id=1, source_target_pairs={{0,64},{64,0},{128,192},{192,128},{1,65},{65,1},{129,193},{193,129... | collective-permute-start | bytes 1916936 | tf_op jit(solution)/shard_map/ppermute | solution.py:244
  25.7 6.9 %collective-permute-start.1 = (bf16[6,416,128]{2,1,0:T(8,128)(2,1)S(1)}, bf16[6,416,128]{2,1,0:T(8,128)(2,1)}, u32[]{:S(2)}, u32[]{:S(2)}) collective-permute-start(bf16[6,416,128]{2,1,0:T(8,128)(2,1)S(1)} %collective-permute-done.far_ref), channel_id=1, source_target_pairs={{0,64},{64,0},{128,192},{192,128},{1,65},{65,1},{129,193},{193,129... | collective-permute-start | bytes 1916936 | tf_op jit(solution)/shard_map/ppermute | solution.py:278
  41.0 29.7 %all-to-all-start = ((bf16[256,4,128]{2,1,0:T(4,128)(2,1)}), bf16[256,4,128]{2,1,0:T(4,128)(2,1)S(1)}, u32[]{:S(2)}, u32[]{:S(2)}) async-start(bf16[256,4,128]{2,1,0:T(4,128)(2,1)} %bitcast.2), calls=%async_computation | async-start | bytes 524288 | tf_op jit(solution)/shard_map/all_to_all | solution.py:320

commit v2 on v1

v2 whole, which is shorter than its diff:
```python
import functools

import jax
import jax.numpy as jnp
from jax import lax
from jax.experimental import pallas as pl
from jax.experimental.pallas import tpu as pltpu
from jax.sharding import PartitionSpec as P

F32 = jnp.float32
BF16 = jnp.bfloat16
LANES = 128
TILES = (2, 2, 2)
US = (.01,.01,.01,.01,8,8,.01,8,.01)
SMOOTH = 0.05 * 0.05
ALPHA = 0.95


def params(mib=48):
    return pltpu.CompilerParams(vmem_limit_bytes=mib * 1024 * 1024)


def round_up(n, k):
    return -(-n // k) * k


def forecast_kernel(x_hbm, w_hbm, own_ref, sent_ref, x, w, x_sems, w_sem, *, first):
    tiles, members, _, width = x.shape
    rows = own_ref.shape[1]
    fields = w.shape[0]
    w_copy = pltpu.make_async_copy(w_hbm, w, w_sem)
    w_copy.start()

    def fetch(t):
        points = pl.ds((first + t) * LANES, LANES)
        return pltpu.make_async_copy(x_hbm.at[:, points], x.at[t], x_sems.at[t])

    for t in range(tiles):
        fetch(t).start()
    w_copy.wait()

    def step(t, carry):
        fetch(t).wait()
        f = lax.dot_general(
            x[t].reshape(members * LANES, width),
            w[...],
            (((1,), (1,)), ((), ())),
            preferred_element_type=F32,
        )
        f = jnp.concatenate([f, jnp.zeros((members * LANES, LANES - fields), F32)], axis=1)
        f = f.T[:rows]
        own_ref[t] = f
        groups = [
            f[8 * g : 8 * g + 8, m * LANES : (m + 1) * LANES]
            for g in range(rows // 8)
            for m in range(members)
        ]
        sent_ref[t] = jnp.concatenate(groups, axis=0).astype(BF16)
        return carry

    lax.fori_loop(0, tiles, step, 0)


def column(row, rows):
    return jnp.broadcast_to(row, (LANES, LANES)).T[:rows]


def pad_row(ref, scratch, fields):
    scratch[...] = jnp.zeros_like(scratch)
    scratch[:, :fields] = ref[...]
    return scratch[...]


def slope_and_length(d):
    t = d * d + SMOOTH
    r = lax.rsqrt(t)
    return d * r, t * r


def near_kernel(own_ref, sib_ref, truth_ref, area_ref, shift_ref, coef_ref, acc_ref, loss_ref, goal, rpad, coefs, *, first, members, total):
    tiles, rows, _ = own_ref.shape
    fields = truth_ref.shape[0]
    c1 = (1.0 - (1.0 - ALPHA) / total) / (total - 1)
    c2 = (1.0 - (1.0 - ALPHA) / total) / (2.0 * total * (total - 1))

    here = slice(first * LANES, (first + tiles) * LANES)
    coefs[...] = column(pad_row(coef_ref, rpad, fields), rows)
    shifts = column(pad_row(shift_ref, rpad, fields), rows)
    goal[...] = jnp.zeros_like(goal)
    for t in range(tiles):
        at = slice((first + t) * LANES, (first + t + 1) * LANES)
        goal[t, :fields, :] = truth_ref[:, at] - shifts[:fields]
    loss_ref[...] = jnp.zeros_like(loss_ref)

    def step(t, carry):
        loss = jnp.zeros((8, LANES), F32)
        for g in range(rows // 8):
            span = slice(8 * g, 8 * g + 8)
            own = [own_ref[t, span, m * LANES : (m + 1) * LANES] for m in range(members)]
            sib = sib_ref[t, 8 * members * g : 8 * members * (g + 1), :].astype(F32)
            skill = jnp.zeros((8, LANES), F32)
            spread = jnp.zeros((8, LANES), F32)
            inner = jnp.zeros((8, LANES), F32)
            slopes = [jnp.zeros((8, LANES), F32) for _ in range(members)]
            for m in range(members):
                for n in range(m + 1, members):
                    a, b = slope_and_length(own[m] - own[n])
                    slopes[m] = slopes[m] + a
                    slopes[n] = slopes[n] - a
                    inner = inner + b
                for n in range(members):
                    a, b = slope_and_length(own[m] - sib[8 * n : 8 * n + 8])
                    slopes[m] = slopes[m] + a
                    spread = spread + b
            for m in range(members):
                a, b = slope_and_length(own[m] - goal[t, span, :])
                skill = skill + b
                acc_ref[t, span, m * LANES : (m + 1) * LANES] = a - c1 * slopes[m]
            loss = loss + coefs[span] * (skill * (1.0 / total) - c2 * (spread + 2.0 * inner))
        at = pl.multiple_of((first + t) * LANES, LANES)
        loss_ref[...] += loss * area_ref[:, pl.ds(at, LANES)]
        return carry

    lax.fori_loop(0, tiles, step, 0)


def far_kernel(*refs, first, before, members, total, fields):
    own_ref, far_ref, fwd_ref, acc_ref, area_ref, coef_ref, near_loss, x_hbm = refs[:8]
    earlier, refs = refs[8 : 8 + before], refs[8 + before :]
    grad_ref, dw_ref, bias_ref, loss_ref, rpad, coefs, grads, x, x_sem = refs
    tiles, rows, _ = own_ref.shape
    width = x.shape[3]
    span_all = members * LANES
    c1 = (1.0 - (1.0 - ALPHA) / total) / (total - 1)
    c2 = (1.0 - (1.0 - ALPHA) / total) / (2.0 * total * (total - 1))

    def fetch(t):
        points = pl.ds((first + t) * LANES, LANES)
        return pltpu.make_async_copy(x_hbm.at[:, points], x.at[t], x_sem.at[t])

    for t in range(tiles):
        fetch(t).start()
    coefs[...] = column(pad_row(coef_ref, rpad, fields), rows)
    grads[...] = jnp.zeros_like(grads)
    if before:
        bias_ref[...] = earlier[1][...]
        loss_ref[...] = earlier[2][...] + near_loss[...]
    else:
        bias_ref[...] = jnp.zeros_like(bias_ref)
        loss_ref[...] = near_loss[...]

    def step(t, carry):
        at = pl.multiple_of((first + t) * LANES, LANES)
        area = jnp.broadcast_to(area_ref[:, pl.ds(at, LANES)], (8, LANES))
        loss = jnp.zeros((8, LANES), F32)
        for g in range(rows // 8):
            span = slice(8 * g, 8 * g + 8)
            part = slice(8 * members * g, 8 * members * (g + 1))
            own = [own_ref[t, span, m * LANES : (m + 1) * LANES] for m in range(members)]
            far = far_ref[t, part, :].astype(F32)
            fwd = fwd_ref[t, part, :].astype(F32)
            spread = jnp.zeros((8, LANES), F32)
            scale = coefs[span] * area
            bias = jnp.zeros((8, LANES), F32)
            for m in range(members):
                slopes = jnp.zeros((8, LANES), F32)
                for other in (far, fwd):
                    for n in range(members):
                        a, b = slope_and_length(own[m] - other[8 * n : 8 * n + 8])
                        slopes = slopes + a
                        spread = spread + b
                here = slice(m * LANES, (m + 1) * LANES)
                grad = (scale * (acc_ref[t, span, here] - c1 * slopes)).astype(BF16).astype(F32)
                grads[t, span, here] = grad
                bias = bias + grad
            bias_ref[span, :] += bias
            loss = loss + coefs[span] * spread
        loss_ref[...] -= c2 * loss * area
        grad_ref[t] = grads[t].astype(BF16)
        return carry

    lax.fori_loop(0, tiles, step, 0)

    dw = earlier[0][...] if before else jnp.zeros(dw_ref.shape, F32)
    for t in range(tiles):
        fetch(t).wait()
        dw = dw + jnp.dot(grad_ref[t], x[t].reshape(span_all, width), preferred_element_type=F32)
    dw_ref[...] = dw


def pack_kernel(dw_ref, bias_ref, loss_ref, out_ref, padded, *, fields):
    padded[...] = jnp.zeros_like(padded)
    padded[: bias_ref.shape[0], :] = bias_ref[...]
    bias = jnp.sum(padded[...].T, axis=0, keepdims=True)
    loss = jnp.sum(jnp.sum(loss_ref[...], axis=0, keepdims=True), axis=1, keepdims=True)
    high = loss.astype(BF16).astype(F32)
    low = loss - high
    quarter = fields // 4
    lane = lax.broadcasted_iota(jnp.int32, (8, LANES), 1)
    row = lax.broadcasted_iota(jnp.int32, (8, LANES), 0) % 4
    bias = jnp.broadcast_to(bias, (8, LANES))
    extra = jnp.zeros((8, LANES), F32)
    for r in range(4):
        moved = pltpu.roll(bias, fields - quarter * r, 1)
        extra = jnp.where(row == r, moved, extra)
    extra = jnp.where(lane < fields + quarter, extra, 0.0)
    at = lane == fields + quarter
    extra = jnp.where(at & (row == 0), high, extra)
    extra = jnp.where(at & (row == 1), low, extra)
    table = dw_ref[...].T.reshape(-1, 8, LANES)
    keep = lax.broadcasted_iota(jnp.int32, table.shape, 2) < fields
    table = jnp.where(keep, table, extra[None])
    out_ref[...] = table.reshape(out_ref.shape).astype(BF16)


def slope_kernel(grad_ref, w_ref, out_ref):
    fields = w_ref.shape[0]
    s = lax.dot_general(
        grad_ref[0, :fields, :], w_ref[...], (((0,), (0,)), ((), ())), preferred_element_type=F32
    )
    out_ref[...] = s.astype(BF16).reshape(out_ref.shape)


def finish_kernel(parts_ref, dw_ref, bias_ref, loss_ref, *, fields, scale, count):
    parts = parts_ref[...].astype(F32).reshape(-1, 8, LANES)
    total = jnp.sum(parts, axis=0)
    total = total[:4] + total[4:]
    dw_ref[...] = total[:, :fields] * scale
    quarter = fields // 4
    lane = lax.broadcasted_iota(jnp.int32, (1, LANES), 1)
    bias = jnp.zeros((1, LANES), F32)
    for r in range(4):
        moved = pltpu.roll(total, (quarter * r - fields) % LANES, 1)[r : r + 1]
        bias = jnp.where((lane >= quarter * r) & (lane < quarter * (r + 1)), moved, bias)
    bias_ref[...] = bias[:, :fields] * scale
    at = fields + quarter
    loss_ref[...] = (total[0:1, at : at + 1] + total[1:2, at : at + 1]) * (1.0 / count)


def cost(us):
    return pl.CostEstimate(flops=int(us * 1e9), bytes_accessed=int(us * 3.5e6), transcendentals=0)


def shards(hidden, weights, shift, truth, area, coef):
    members, points, width = hidden.shape
    fields = weights.shape[1]
    total = members * lax.axis_size("member")
    all_points = points * lax.axis_size("point")
    rows = round_up(fields, 8)
    span = members * LANES
    weights, truth = weights.T, truth.T
    shift, coef, area = shift[None], coef[None], area[None]
    tile = lambda shape: pl.BlockSpec((1,) + shape, lambda i: (i, 0, 0))
    shape = jax.ShapeDtypeStruct
    vmem = pl.BlockSpec(memory_space=pltpu.VMEM)
    hbm = pl.BlockSpec(memory_space=pltpu.HBM)
    core_swap = [(0, 1), (1, 0), (2, 3), (3, 2)]
    chip_swap = [(0, 2), (1, 3), (2, 0), (3, 1)]

    def forecast(n, first, us):
        return pl.pallas_call(
            functools.partial(forecast_kernel, first=first),
            in_specs=[hbm, hbm],
            out_specs=[vmem, vmem],
            out_shape=[shape((n, rows, span), F32), shape((n, rows * members, LANES), BF16)],
            scratch_shapes=[
                pltpu.VMEM((n, members, LANES, width), BF16),
                pltpu.VMEM((fields, width), BF16),
                pltpu.SemaphoreType.DMA((n,)),
                pltpu.SemaphoreType.DMA,
            ],
            compiler_params=params(48 if first else 60),
            cost_estimate=cost(us),
            name="forecast",
        )(hidden, weights)

    def near(n, first, us, own, sib):
        return pl.pallas_call(
            functools.partial(near_kernel, first=first, members=members, total=total),
            in_specs=[vmem] * 6,
            out_specs=[vmem] * 2,
            out_shape=[shape((n, rows, span), F32), shape((8, LANES), F32)],
            scratch_shapes=[
                pltpu.VMEM((n, rows, LANES), F32),
                pltpu.VMEM((1, LANES), F32),
                pltpu.VMEM((rows, LANES), F32),
            ],
            compiler_params=params(),
            cost_estimate=cost(us),
            name="near",
        )(own, sib, truth, area, shift, coef)

    def far(n, first, us, own, away, fwd, acc, loss, *sums):
        return pl.pallas_call(
            functools.partial(
                far_kernel, first=first, before=len(sums), members=members, total=total, fields=fields
            ),
            in_specs=[vmem] * 7 + [hbm] + [vmem] * len(sums),
            out_specs=[vmem] * 4,
            out_shape=[
                shape((n, LANES, span), BF16),
                shape((LANES, width), F32),
                shape((rows, LANES), F32),
                shape((8, LANES), F32),
            ],
            scratch_shapes=[
                pltpu.VMEM((1, LANES), F32),
                pltpu.VMEM((rows, LANES), F32),
                pltpu.VMEM((n, LANES, span), F32),
                pltpu.VMEM((n, members, LANES, width), BF16),
                pltpu.SemaphoreType.DMA((n,)),
            ],
            compiler_params=params(),
            cost_estimate=cost(us),
            name="far",
        )(own, away, fwd, acc, area, coef, loss, hidden, *sums)

    across = lambda a: lax.ppermute(a, "member", chip_swap)
    beside = lambda a: lax.ppermute(a, "member", core_swap)
    hold = lax.optimization_barrier
    n0, n1, n2 = TILES
    a1, a2 = n0, n0 + n1
    own0, out0 = forecast(n0, 0, US[0])
    away0 = across(out0)
    own1, out1 = forecast(n1, a1, US[1])
    away1 = across(out1)
    own2, out2 = forecast(n2, a2, US[2])
    own0, out2 = hold((own0, out2))
    away2 = across(out2)
    sib0, sib1, sib2 = beside(out0), beside(out1), beside(out2)
    acc0, loss0 = near(n0, 0, US[3], own0, sib0)
    away0, acc0, own1 = hold((away0, acc0, own1))
    fwd0 = beside(away0)
    acc1, loss1 = near(n1, a1, US[4], own1, sib1)
    away1, acc1, acc0 = hold((away1, acc1, acc0))
    fwd1 = beside(away1)
    grad0, *sums = far(n0, 0, US[5], own0, away0, fwd0, acc0, loss0)
    grad1, *sums = far(n1, a1, US[6], own1, away1, fwd1, acc1, loss1, *sums)
    away2, own2, *sums = hold((away2, own2, *sums))
    fwd2 = beside(away2)
    acc2, loss2 = near(n2, a2, US[7], own2, sib2)
    grad2, *sums = far(n2, a2, US[8], own2, away2, fwd2, acc2, loss2, *sums)
    grads = [grad0, grad1, grad2]

    packed = pl.pallas_call(
        functools.partial(pack_kernel, fields=fields),
        out_shape=shape((width, LANES), BF16),
        scratch_shapes=[pltpu.VMEM((LANES, LANES), F32)],
        compiler_params=params(),
        name="pack",
    )(*sums)
    parts = lax.all_to_all(packed, ("member", "point"), split_axis=0, concat_axis=0, tiled=True)

    grad = grads[0] if len(grads) == 1 else jnp.concatenate(grads, axis=0)
    slope = pl.pallas_call(
        slope_kernel,
        grid=(points // LANES,),
        in_specs=[tile((LANES, span)), pl.BlockSpec((fields, width), lambda i: (0, 0))],
        out_specs=pl.BlockSpec((members, LANES, width), lambda i: (0, i, 0)),
        out_shape=shape(hidden.shape, BF16),
        compiler_params=params(),
        cost_estimate=cost(5),
        name="slope",
    )(grad, weights)

    own_rows = width // (lax.axis_size("member") * lax.axis_size("point"))
    dw, bias, loss = pl.pallas_call(
        functools.partial(
            finish_kernel, fields=fields, scale=float((total * all_points) ** -0.5), count=float(all_points * fields)
        ),
        out_shape=[shape((own_rows, fields), F32), shape((1, fields), F32), shape((1, 1), F32)],
        compiler_params=params(),
        name="finish",
    )(parts)
    return loss.reshape(()), slope, dw, bias.reshape(fields)


def solution(mesh):
    placed = (P("member", "point", None), P(), P(), P("point", None), P("point"), P())
    return jax.shard_map(
        shards,
        mesh=mesh,
        in_specs=placed,
        out_specs=(P(), P("member", "point", None), P(("member", "point"), None), P()),
        check_vma=False,
    )
```

time: 71.9 us -> 58.9 us (0.82)
  waiting for transfers between devices: 22.9 us -> 11.3 us
  Pallas kernels: 25.2 us -> 23.2 us
  starting transfers between devices: 21.2 us -> 23.2 us
  local copies, waits for them, and re-layouts: 1.35 us -> 0.04 us
    ppermute x3 -> x9, waiting for transfers between devices: 12.4 us -> 0.83 us  [the longest x3 0.59 us: shards(): across = lambda a: lax.ppermute(a, 'member', chip_swap)]
    ppermute x3 -> x9, starting transfers between devices: 6.88 us -> 10.5 us  [the longest x6 6.23 us: shards(): beside = lambda a: lax.ppermute(a, 'member', core_swap)]
    pallas_call x4 -> x10, Pallas kernels: 19.7 us -> 17.7 us  [the longest x3 8.28 us: forecast(): pl.pallas_call(functools.partial(forecast_kernel, first=first), in_specs=...]
    all_to_all x1, starting transfers between devices: 14.3 us -> 12.7 us  [shards(): lax.all_to_all(packed, ('member', 'point'), split_axis=0, concat_axis=0,...]
    unnamed x10 -> x12, local copies, waits for them, and re-layouts: 1.34 us -> 0.04 us
  transfers between devices with their start and end apart: 4 -> 10, of which waited for: 2 -> 3; matrix products, arithmetic and copies ran while one was open for 0% -> 0% of each run, Pallas kernels for 13% -> 28%
where the time goes in v2:
time: 58.9 us; the launch traced here: 58.7 us
  Pallas kernels  23.2 us (39%)
  starting transfers between devices  23.2 us (39%)
  waiting for transfers between devices  11.3 us (19%)
  between operations  0.8 us (1%)
    all_to_all x1, starting transfers between devices, shards(): lax.all_to_all(packed, ('member', 'point'), split_axis=0, concat_axis=0,...  12.7 us
    all_to_all x1, waiting for transfers between devices, shards(): lax.all_to_all(packed, ('member', 'point'), split_axis=0, concat_axis=0,...  10.4 us
    pallas_call x3, Pallas kernels, forecast(): pl.pallas_call(functools.partial(forecast_kernel, first=first), in_specs=...  8.28 us
    ppermute x6, starting transfers between devices, shards(): beside = lambda a: lax.ppermute(a, 'member', core_swap)  6.23 us
    pallas_call x3, Pallas kernels, far(): pl.pallas_call(functools.partial(far_kernel, first=first, before=len(sums...  5.76 us
    pallas_call x1, Pallas kernels, shards(): pl.pallas_call(slope_kernel, grid=(points // LANES,), in_specs=[tile((LAN...  4.79 us
    ppermute x3, starting transfers between devices, shards(): across = lambda a: lax.ppermute(a, 'member', chip_swap)  4.25 us
    pallas_call x3, Pallas kernels, near(): pl.pallas_call(functools.partial(near_kernel, first=first, members=member...  2.71 us
  transfers between devices with their start and end apart: 10, of which 3 were waited for; matrix products, arithmetic and copies ran while one was open for 0% of the time, Pallas kernels for 28%

profile of v2, /device:TPU:1, one launch (start us, length us, event | category | flops | bytes accessed | tf_op | source)
XLA Modules:
  0.0 58.7 jit_solution(12594564135850572208)
XLA Ops:
  0.6 3.3 %forecast.3 = (f32[2,104,512]{2,1,0:T(8,128)}, bf16[2,416,128]{2,1,0:T(8,128)(2,1)}) custom-call(bf16[4,768,1024]{2,1,0:T(8,128)(2,1)} %refs_7_.5, bf16[100,1024]{1,0:T(8,128)(2,1)} %bitcast.8), custom_call_target="tpu_custom_call" | custom-call | flops 10000000 | bytes 35000 | tf_op jit(solution)/shard_map/forecast/pallas_call | solution.py:261
  3.9 0.0 copy-start.5
  4.0 0.0 copy-start.1
  4.0 0.0 copy-start.2
  4.0 0.0 copy-start.3
  4.0 0.0 copy-start.4
  4.0 3.3 %collective-permute-start.2 = (bf16[2,416,128]{2,1,0:T(8,128)(2,1)}, bf16[2,416,128]{2,1,0:T(8,128)(2,1)S(1)}, u32[]{:S(2)}, u32[]{:S(2)}) collective-permute-start(bf16[2,416,128]{2,1,0:T(8,128)(2,1)} %get-tuple-element.48), channel_id=1, source_target_pairs={{0,64},{64,0},{128,192},{192,128},{1,65},{65,1},{129,193},{193,129... | collective-permute-start | bytes 638984 | tf_op jit(solution)/shard_map/ppermute | solution.py:319
  7.3 1.2 %collective-permute-start.1 = (bf16[2,416,128]{2,1,0:T(8,128)(2,1)}, bf16[2,416,128]{2,1,0:T(8,128)(2,1)S(1)}, u32[]{:S(2)}, u32[]{:S(2)}) collective-permute-start(bf16[2,416,128]{2,1,0:T(8,128)(2,1)} %get-tuple-element.48), channel_id=1, source_target_pairs={{0,128},{64,192},{128,0},{192,64},{1,129},{65,193},{129,1},{193,65... | collective-permute-start | bytes 638984 | tf_op jit(solution)/shard_map/ppermute | solution.py:318
  8.5 2.5 %forecast.5 = (f32[2,104,512]{2,1,0:T(8,128)S(1)}, bf16[2,416,128]{2,1,0:T(8,128)(2,1)S(1)}) custom-call(bf16[4,768,1024]{2,1,0:T(8,128)(2,1)} %refs_7_.5, bf16[100,1024]{1,0:T(8,128)(2,1)S(1)} %bitcast.9), custom_call_target="tpu_custom_call" | custom-call | flops 10000000 | bytes 35000 | tf_op jit(solution)/shard_map/forecast/pallas_call | solution.py:261
  11.0 0.4 collective-permute-start.4
  11.5 1.8 %collective-permute-start.3 = (bf16[2,416,128]{2,1,0:T(8,128)(2,1)S(1)}, bf16[2,416,128]{2,1,0:T(8,128)(2,1)S(1)}, u32[]{:S(2)}, u32[]{:S(2)}) collective-permute-start(bf16[2,416,128]{2,1,0:T(8,128)(2,1)S(1)} %get-tuple-element.53), channel_id=1, source_target_pairs={{0,128},{64,192},{128,0},{192,64},{1,129},{65,193},{129,1},{193,65... | collective-permute-start | bytes 638984 | tf_op jit(solution)/shard_map/ppermute | solution.py:318
  13.3 2.5 %forecast.4 = (f32[2,104,512]{2,1,0:T(8,128)S(1)}, bf16[2,416,128]{2,1,0:T(8,128)(2,1)S(1)}) custom-call(bf16[4,768,1024]{2,1,0:T(8,128)(2,1)} %refs_7_.5, bf16[100,1024]{1,0:T(8,128)(2,1)S(1)} %bitcast.10), custom_call_target="tpu_custom_call" | custom-call | flops 10000000 | bytes 35000 | tf_op jit(solution)/shard_map/forecast/pallas_call | solution.py:261
  15.8 0.5 collective-permute-start.8
  16.3 0.0 collective-permute-done.2.sib_ref
  16.3 1.3 %collective-permute-start = (bf16[2,416,128]{2,1,0:T(8,128)(2,1)S(1)}, bf16[2,416,128]{2,1,0:T(8,128)(2,1)S(1)}, u32[]{:S(2)}, u32[]{:S(2)}) collective-permute-start(bf16[2,416,128]{2,1,0:T(8,128)(2,1)S(1)} %get-tuple-element.46), channel_id=1, source_target_pairs={{0,128},{64,192},{128,0},{192,64},{1,129},{65,193},{129,1},{193,65... | collective-permute-start | bytes 638984 | tf_op jit(solution)/shard_map/ppermute | solution.py:318
  17.6 0.9 %near.3 = (f32[2,104,512]{2,1,0:T(8,128)S(1)}, f32[8,128]{1,0:T(8,128)S(1)}) custom-call(f32[2,104,512]{2,1,0:T(8,128)S(1)} %copy-done.1, bf16[2,416,128]{2,1,0:T(8,128)(2,1)S(1)} %collective-permute-done.2.sib_ref, f32[100,768]{1,0:T(8,128)S(1)} %bitcast.13, f32[1,768]{1,0:T(1,128)S(1)} %broadcast_in_dim.9.area_ref.refs_4_, f32[1,100]{1,0:T(1,128)S(1)} %bitcast.22, ...), custom_call_target="tpu_custom_call" | custom-call | flops 10000000 | bytes 35000 | tf_op jit(solution)/shard_map/near/pallas_call | solution.py:278
  18.5 0.4 collective-permute-start.6
  18.9 0.9 %near.4 = (f32[2,104,512]{2,1,0:T(8,128)S(1)}, f32[8,128]{1,0:T(8,128)S(1)}) custom-call(f32[2,104,512]{2,1,0:T(8,128)S(1)} %get-tuple-element.52.own_ref.refs_0_, bf16[2,416,128]{2,1,0:T(8,128)(2,1)S(1)} %collective-permute-done.4.sib_ref, f32[100,768]{1,0:T(8,128)S(1)} %bitcast.14, f32[1,768]{1,0:T(1,128)S(1)} %broadcast_in_dim.9.area_ref.refs_4_, ...), custom_call_target="tpu_custom_call" | custom-call | flops 8000000000 | bytes 28000000 | tf_op jit(solution)/shard_map/near/pallas_call | solution.py:278
  19.8 0.6 collective-permute-done.3.refs_1_
  20.4 1.1 %collective-permute-start.5 = (bf16[2,416,128]{2,1,0:T(8,128)(2,1)S(1)}, bf16[2,416,128]{2,1,0:T(8,128)(2,1)S(1)}, u32[]{:S(2)}, u32[]{:S(2)}) collective-permute-start(bf16[2,416,128]{2,1,0:T(8,128)(2,1)S(1)} %collective-permute-done.3.refs_1_), channel_id=1, source_target_pairs={{0,64},{64,0},{128,192},{192,128},{1,65},{65,1},{129,193},{193,129... | collective-permute-start | bytes 638984 | tf_op jit(solution)/shard_map/ppermute | solution.py:319
  21.5 2.0 %far.3 = (bf16[2,128,512]{2,1,0:T(8,128)(2,1)S(1)}, f32[128,1024]{1,0:T(8,128)S(1)}, f32[104,128]{1,0:T(8,128)S(1)}, f32[8,128]{1,0:T(8,128)S(1)}) custom-call(f32[2,104,512]{2,1,0:T(8,128)S(1)} %copy-done.1, bf16[2,416,128]{2,1,0:T(8,128)(2,1)S(1)} %collective-permute-done.1.refs_1_, bf16[2,416,128]{2,1,0:T(8,128)(2,1)S(1)} %collective-permute-done.6.refs_2_, ...), custom_call_target="tpu_custom_call" | custom-call | flops 8000000000 | bytes 28000000 | tf_op jit(solution)/shard_map/far/pallas_call | solution.py:294
  23.6 1.9 %far.4 = (bf16[2,128,512]{2,1,0:T(8,128)(2,1)S(1)}, f32[128,1024]{1,0:T(8,128)S(1)}, f32[104,128]{1,0:T(8,128)S(1)}, f32[8,128]{1,0:T(8,128)S(1)}) custom-call(f32[2,104,512]{2,1,0:T(8,128)S(1)} %get-tuple-element.52.own_ref.refs_0_, bf16[2,416,128]{2,1,0:T(8,128)(2,1)S(1)} %collective-permute-done.3.refs_1_, ...), custom_call_target="tpu_custom_call" | custom-call | flops 10000000 | bytes 35000 | tf_op jit(solution)/shard_map/far/pallas_call | solution.py:294
  25.5 0.4 collective-permute-start.7
  25.9 0.9 %near.5 = (f32[2,104,512]{2,1,0:T(8,128)S(1)}, f32[8,128]{1,0:T(8,128)S(1)}) custom-call(f32[2,104,512]{2,1,0:T(8,128)S(1)} %get-tuple-element.68.own_ref.refs_0_, bf16[2,416,128]{2,1,0:T(8,128)(2,1)S(1)} %collective-permute-done.8.sib_ref, f32[100,768]{1,0:T(8,128)S(1)} %bitcast.15, f32[1,768]{1,0:T(1,128)S(1)} %broadcast_in_dim.9.area_ref.refs_4_, ...), custom_call_target="tpu_custom_call" | custom-call | flops 8000000000 | bytes 28000000 | tf_op jit(solution)/shard_map/near/pallas_call | solution.py:278
  26.8 0.2 collective-permute-done.7.refs_2_
  27.0 1.9 %far.5 = (bf16[2,128,512]{2,1,0:T(8,128)(2,1)S(1)}, f32[128,1024]{1,0:T(8,128)S(1)}, f32[104,128]{1,0:T(8,128)S(1)}, f32[8,128]{1,0:T(8,128)S(1)}) custom-call(f32[2,104,512]{2,1,0:T(8,128)S(1)} %get-tuple-element.68.own_ref.refs_0_, bf16[2,416,128]{2,1,0:T(8,128)(2,1)S(1)} %collective-permute-done.refs_1_, ...), custom_call_target="tpu_custom_call" | custom-call | flops 10000000 | bytes 35000 | tf_op jit(solution)/shard_map/far/pallas_call | solution.py:294
  28.9 1.0 %pack.1 = bf16[1024,128]{1,0:T(8,128)(2,1)} custom-call(f32[128,1024]{1,0:T(8,128)S(1)} %get-tuple-element.75.dw_ref, f32[104,128]{1,0:T(8,128)S(1)} %get-tuple-element.76.bias_ref, f32[8,128]{1,0:T(8,128)S(1)} %get-tuple-element.77.loss_ref), custom_call_target="tpu_custom_call" | custom-call | tf_op jit(solution)/shard_map/pack/pallas_call | solution.py:345
  29.8 12.7 %all-to-all-start = ((bf16[256,4,128]{2,1,0:T(4,128)(2,1)}), bf16[256,4,128]{2,1,0:T(4,128)(2,1)S(1)}, u32[]{:S(2)}, u32[]{:S(2)}) async-start(bf16[256,4,128]{2,1,0:T(4,128)(2,1)} %bitcast.4), calls=%async_computation | async-start | bytes 524288 | tf_op jit(solution)/shard_map/all_to_all | solution.py:352
  42.6 0.1 pad_maximum_fusion.grad_ref
  42.7 4.8 %slope.1 = bf16[4,768,1024]{2,1,0:T(8,128)(2,1)} custom-call(bf16[6,128,512]{2,1,0:T(8,128)(2,1)S(1)} %pad_maximum_fusion.grad_ref, bf16[100,1024]{1,0:T(8,128)(2,1)S(1)} %bitcast.11), custom_call_target="tpu_custom_call" | custom-call | flops 5000000000 | bytes 17500000 | tf_op jit(solution)/shard_map/slope/pallas_call | solution.py:355
  47.5 10.4 %all-to-all-done = bf16[256,4,128]{2,1,0:T(4,128)(2,1)S(1)} async-done(((bf16[256,4,128]{2,1,0:T(4,128)(2,1)}), bf16[256,4,128]{2,1,0:T(4,128)(2,1)S(1)}, u32[]{:S(2)}, u32[]{:S(2)}) %all-to-all-start) | async-done | bytes 262176 | tf_op jit(solution)/shard_map/all_to_all | solution.py:352
  57.9 0.7 %finish.1 = (f32[4,100]{1,0:T(4,128)}, f32[1,100]{1,0:T(1,128)}, f32[1,1]{1,0:T(1,128)}) custom-call(bf16[1024,128]{1,0:T(8,128)(2,1)S(1)} %bitcast.12), custom_call_target="tpu_custom_call" | custom-call | tf_op jit(solution)/shard_map/finish/pallas_call | solution.py:367
  (14 shorter events, 0.0 us)
Async XLA Ops:
  0.6 7.9 %copy-start = (bf16[1024,100]{0,1:T(8,128)(2,1)S(1)}, bf16[1024,100]{0,1:T(8,128)(2,1)}, u32[]{:S(2)}) copy-start(bf16[1024,100]{0,1:T(8,128)(2,1)} %param.7) | copy-start | bytes 614404
  3.9 12.3 %copy-start.5 = (f32[768]{0:T(1024)S(1)}, f32[768]{0:T(1024)}, u32[]{:S(2)}) copy-start(f32[768]{0:T(1024)} %param.10) | copy-start | bytes 9220
  4.0 13.6 %copy-start.1 = (f32[2,104,512]{2,1,0:T(8,128)S(1)}, f32[2,104,512]{2,1,0:T(8,128)}, u32[]{:S(2)}) copy-start(f32[2,104,512]{2,1,0:T(8,128)} %get-tuple-element.49.own_ref.refs_0_) | copy-start | bytes 1277956
  4.0 13.6 %copy-start.2 = (f32[768,100]{0,1:T(8,128)S(1)}, f32[768,100]{0,1:T(8,128)}, u32[]{:S(2)}) copy-start(f32[768,100]{0,1:T(8,128)} %param.9) | copy-start | bytes 921604
  4.0 13.6 %copy-start.3 = (f32[100]{0:T(128)S(1)}, f32[100]{0:T(128)}, u32[]{:S(2)}) copy-start(f32[100]{0:T(128)} %param.11) | copy-start | bytes 1204
  4.0 13.6 %copy-start.4 = (f32[100]{0:T(128)S(1)}, f32[100]{0:T(128)}, u32[]{:S(2)}) copy-start(f32[100]{0:T(128)} %param.8) | copy-start | bytes 1204
  4.0 12.3 %collective-permute-start.2 = (bf16[2,416,128]{2,1,0:T(8,128)(2,1)}, bf16[2,416,128]{2,1,0:T(8,128)(2,1)S(1)}, u32[]{:S(2)}, u32[]{:S(2)}) collective-permute-start(bf16[2,416,128]{2,1,0:T(8,128)(2,1)} %get-tuple-element.48), channel_id=1, source_target_pairs={{0,64},{64,0},{128,192},{192,128},{1,65},{65,1},{129,193},{193,129... | collective-permute-start | bytes 638984 | tf_op jit(solution)/shard_map/ppermute | solution.py:319
  7.3 11.2 %collective-permute-start.1 = (bf16[2,416,128]{2,1,0:T(8,128)(2,1)}, bf16[2,416,128]{2,1,0:T(8,128)(2,1)S(1)}, u32[]{:S(2)}, u32[]{:S(2)}) collective-permute-start(bf16[2,416,128]{2,1,0:T(8,128)(2,1)} %get-tuple-element.48), channel_id=1, source_target_pairs={{0,128},{64,192},{128,0},{192,64},{1,129},{65,193},{129,1},{193,65... | collective-permute-start | bytes 638984 | tf_op jit(solution)/shard_map/ppermute | solution.py:318
  11.0 7.9 %collective-permute-start.4 = (bf16[2,416,128]{2,1,0:T(8,128)(2,1)S(1)}, bf16[2,416,128]{2,1,0:T(8,128)(2,1)S(1)}, u32[]{:S(2)}, u32[]{:S(2)}) collective-permute-start(bf16[2,416,128]{2,1,0:T(8,128)(2,1)S(1)} %get-tuple-element.53), channel_id=1, source_target_pairs={{0,64},{64,0},{128,192},{192,128},{1,65},{65,1},{129,193},{193,129... | collective-permute-start | bytes 638984 | tf_op jit(solution)/shard_map/ppermute | solution.py:319
  11.5 9.0 %collective-permute-start.3 = (bf16[2,416,128]{2,1,0:T(8,128)(2,1)S(1)}, bf16[2,416,128]{2,1,0:T(8,128)(2,1)S(1)}, u32[]{:S(2)}, u32[]{:S(2)}) collective-permute-start(bf16[2,416,128]{2,1,0:T(8,128)(2,1)S(1)} %get-tuple-element.53), channel_id=1, source_target_pairs={{0,128},{64,192},{128,0},{192,64},{1,129},{65,193},{129,1},{193,65... | collective-permute-start | bytes 638984 | tf_op jit(solution)/shard_map/ppermute | solution.py:318
  15.8 10.1 %collective-permute-start.8 = (bf16[2,416,128]{2,1,0:T(8,128)(2,1)S(1)}, bf16[2,416,128]{2,1,0:T(8,128)(2,1)S(1)}, u32[]{:S(2)}, u32[]{:S(2)}) collective-permute-start(bf16[2,416,128]{2,1,0:T(8,128)(2,1)S(1)} %get-tuple-element.46), channel_id=1, source_target_pairs={{0,64},{64,0},{128,192},{192,128},{1,65},{65,1},{129,193},{193,129... | collective-permute-start | bytes 638984 | tf_op jit(solution)/shard_map/ppermute | solution.py:319
  16.3 9.2 %collective-permute-start = (bf16[2,416,128]{2,1,0:T(8,128)(2,1)S(1)}, bf16[2,416,128]{2,1,0:T(8,128)(2,1)S(1)}, u32[]{:S(2)}, u32[]{:S(2)}) collective-permute-start(bf16[2,416,128]{2,1,0:T(8,128)(2,1)S(1)} %get-tuple-element.46), channel_id=1, source_target_pairs={{0,128},{64,192},{128,0},{192,64},{1,129},{65,193},{129,1},{193,65... | collective-permute-start | bytes 638984 | tf_op jit(solution)/shard_map/ppermute | solution.py:318
  18.5 3.0 %collective-permute-start.6 = (bf16[2,416,128]{2,1,0:T(8,128)(2,1)S(1)}, bf16[2,416,128]{2,1,0:T(8,128)(2,1)S(1)}, u32[]{:S(2)}, u32[]{:S(2)}) collective-permute-start(bf16[2,416,128]{2,1,0:T(8,128)(2,1)S(1)} %collective-permute-done.1.refs_1_), channel_id=1, source_target_pairs={{0,64},{64,0},{128,192},{192,128},{1,65},{65,1},{129,193},{193,129... | collective-permute-start | bytes 638984 | tf_op jit(solution)/shard_map/ppermute | solution.py:319
  20.4 3.1 %collective-permute-start.5 = (bf16[2,416,128]{2,1,0:T(8,128)(2,1)S(1)}, bf16[2,416,128]{2,1,0:T(8,128)(2,1)S(1)}, u32[]{:S(2)}, u32[]{:S(2)}) collective-permute-start(bf16[2,416,128]{2,1,0:T(8,128)(2,1)S(1)} %collective-permute-done.3.refs_1_), channel_id=1, source_target_pairs={{0,64},{64,0},{128,192},{192,128},{1,65},{65,1},{129,193},{193,129... | collective-permute-start | bytes 638984 | tf_op jit(solution)/shard_map/ppermute | solution.py:319
  25.5 1.6 %collective-permute-start.7 = (bf16[2,416,128]{2,1,0:T(8,128)(2,1)S(1)}, bf16[2,416,128]{2,1,0:T(8,128)(2,1)S(1)}, u32[]{:S(2)}, u32[]{:S(2)}) collective-permute-start(bf16[2,416,128]{2,1,0:T(8,128)(2,1)S(1)} %collective-permute-done.refs_1_), channel_id=1, source_target_pairs={{0,64},{64,0},{128,192},{192,128},{1,65},{65,1},{129,193},{193,129... | collective-permute-start | bytes 638984 | tf_op jit(solution)/shard_map/ppermute | solution.py:319
  29.8 28.1 %all-to-all-start = ((bf16[256,4,128]{2,1,0:T(4,128)(2,1)}), bf16[256,4,128]{2,1,0:T(4,128)(2,1)S(1)}, u32[]{:S(2)}, u32[]{:S(2)}) async-start(bf16[256,4,128]{2,1,0:T(4,128)(2,1)} %bitcast.4), calls=%async_computation | async-start | bytes 524288 | tf_op jit(solution)/shard_map/all_to_all | solution.py:352

commit v3 on v2

--- a/solution.py
+++ b/solution.py
@@ -24,7 +24,7 @@
     return -(-n // k) * k
 
 
-def forecast_kernel(x_hbm, w_hbm, own_ref, sent_ref, x, w, x_sems, w_sem, *, first):
+def forecast_kernel(x_hbm, w_hbm, x, own_ref, sent_ref, w, x_sems, w_sem, *, first):
     tiles, members, _, width = x.shape
     rows = own_ref.shape[1]
     fields = w.shape[0]
@@ -124,22 +124,44 @@
     lax.fori_loop(0, tiles, step, 0)
 
 
-def far_kernel(*refs, first, before, members, total, fields):
-    own_ref, far_ref, fwd_ref, acc_ref, area_ref, coef_ref, near_loss, x_hbm = refs[:8]
+def pack(dw, bias_ref, loss_ref, padded, fields):
+    padded[...] = jnp.zeros_like(padded)
+    padded[: bias_ref.shape[0], :] = bias_ref[...]
+    bias = jnp.sum(padded[...].T, axis=0, keepdims=True)
+    loss = jnp.sum(jnp.sum(loss_ref[...], axis=0, keepdims=True), axis=1, keepdims=True)
+    high = loss.astype(BF16).astype(F32)
+    low = loss - high
+    quarter = fields // 4
+    lane = lax.broadcasted_iota(jnp.int32, (8, LANES), 1)
+    row = lax.broadcasted_iota(jnp.int32, (8, LANES), 0) % 4
+    bias = jnp.broadcast_to(bias, (8, LANES))
+    extra = jnp.zeros((8, LANES), F32)
+    for r in range(4):
+        moved = pltpu.roll(bias, fields - quarter * r, 1)
+        extra = jnp.where(row == r, moved, extra)
+    extra = jnp.where(lane < fields + quarter, extra, 0.0)
+    at = lane == fields + quarter
+    extra = jnp.where(at & (row == 0), high, extra)
+    extra = jnp.where(at & (row == 1), low, extra)
+    table = dw.T.reshape(-1, 8, LANES)
+    keep = lax.broadcasted_iota(jnp.int32, table.shape, 2) < fields
+    table = jnp.where(keep, table, extra[None])
+    return table.reshape(-1, LANES).astype(BF16)
+
+
+def far_kernel(*refs, first, before, last, members, total, fields):
+    own_ref, far_ref, fwd_ref, acc_ref, area_ref, coef_ref, near_loss, x = refs[:8]
     earlier, refs = refs[8 : 8 + before], refs[8 + before :]
-    grad_ref, dw_ref, bias_ref, loss_ref, rpad, coefs, grads, x, x_sem = refs
+    if last:
+        grad_ref, out_ref, rpad, coefs, grads, bias_ref, loss_ref, padded = refs
+    else:
+        grad_ref, dw_ref, bias_ref, loss_ref, rpad, coefs, grads = refs
     tiles, rows, _ = own_ref.shape
     width = x.shape[3]
     span_all = members * LANES
     c1 = (1.0 - (1.0 - ALPHA) / total) / (total - 1)
     c2 = (1.0 - (1.0 - ALPHA) / total) / (2.0 * total * (total - 1))
 
-    def fetch(t):
-        points = pl.ds((first + t) * LANES, LANES)
-        return pltpu.make_async_copy(x_hbm.at[:, points], x.at[t], x_sem.at[t])
-
-    for t in range(tiles):
-        fetch(t).start()
     coefs[...] = column(pad_row(coef_ref, rpad, fields), rows)
     grads[...] = jnp.zeros_like(grads)
     if before:
@@ -181,36 +203,13 @@
 
     lax.fori_loop(0, tiles, step, 0)
 
-    dw = earlier[0][...] if before else jnp.zeros(dw_ref.shape, F32)
+    dw = earlier[0][...] if before else jnp.zeros((LANES, width), F32)
     for t in range(tiles):
-        fetch(t).wait()
         dw = dw + jnp.dot(grad_ref[t], x[t].reshape(span_all, width), preferred_element_type=F32)
-    dw_ref[...] = dw
-
-
-def pack_kernel(dw_ref, bias_ref, loss_ref, out_ref, padded, *, fields):
-    padded[...] = jnp.zeros_like(padded)
-    padded[: bias_ref.shape[0], :] = bias_ref[...]
-    bias = jnp.sum(padded[...].T, axis=0, keepdims=True)
-    loss = jnp.sum(jnp.sum(loss_ref[...], axis=0, keepdims=True), axis=1, keepdims=True)
-    high = loss.astype(BF16).astype(F32)
-    low = loss - high
-    quarter = fields // 4
-    lane = lax.broadcasted_iota(jnp.int32, (8, LANES), 1)
-    row = lax.broadcasted_iota(jnp.int32, (8, LANES), 0) % 4
-    bias = jnp.broadcast_to(bias, (8, LANES))
-    extra = jnp.zeros((8, LANES), F32)
-    for r in range(4):
-        moved = pltpu.roll(bias, fields - quarter * r, 1)
-        extra = jnp.where(row == r, moved, extra)
-    extra = jnp.where(lane < fields + quarter, extra, 0.0)
-    at = lane == fields + quarter
-    extra = jnp.where(at & (row == 0), high, extra)
-    extra = jnp.where(at & (row == 1), low, extra)
-    table = dw_ref[...].T.reshape(-1, 8, LANES)
-    keep = lax.broadcasted_iota(jnp.int32, table.shape, 2) < fields
-    table = jnp.where(keep, table, extra[None])
-    out_ref[...] = table.reshape(out_ref.shape).astype(BF16)
+    if last:
+        out_ref[...] = pack(dw, bias_ref, loss_ref, padded, fields)
+    else:
+        dw_ref[...] = dw
 
 
 def slope_kernel(grad_ref, w_ref, out_ref):
@@ -261,18 +260,21 @@
         return pl.pallas_call(
             functools.partial(forecast_kernel, first=first),
             in_specs=[hbm, hbm],
-            out_specs=[vmem, vmem],
-            out_shape=[shape((n, rows, span), F32), shape((n, rows * members, LANES), BF16)],
+            out_specs=[vmem] * 3,
+            out_shape=[
+                shape((n, members, LANES, width), BF16),
+                shape((n, rows, span), F32),
+                shape((n, rows * members, LANES), BF16),
+            ],
             scratch_shapes=[
-                pltpu.VMEM((n, members, LANES, width), BF16),
                 pltpu.VMEM((fields, width), BF16),
                 pltpu.SemaphoreType.DMA((n,)),
                 pltpu.SemaphoreType.DMA,
             ],
-            compiler_params=params(48 if first else 60),
+            compiler_params=params(),
             cost_estimate=cost(us),
             name="forecast",
-        )(hidden, weights)
+        )(hidden, pltpu.with_memory_space_constraint(weights, pltpu.HBM))
 
     def near(n, first, us, own, sib):
         return pl.pallas_call(
@@ -290,41 +292,42 @@
             name="near",
         )(own, sib, truth, area, shift, coef)
 
-    def far(n, first, us, own, away, fwd, acc, loss, *sums):
+    def far(n, first, us, own, away, fwd, acc, loss, x, *sums, last=False):
+        sums_shapes = [((rows, LANES), F32), ((8, LANES), F32)]
+        if last:
+            outs = [shape((width, LANES), BF16)]
+            extra = [pltpu.VMEM(*i) for i in sums_shapes] + [pltpu.VMEM((LANES, LANES), F32)]
+        else:
+            outs = [shape((LANES, width), F32)] + [shape(*i) for i in sums_shapes]
+            extra = []
         return pl.pallas_call(
             functools.partial(
-                far_kernel, first=first, before=len(sums), members=members, total=total, fields=fields
+                far_kernel, first=first, before=len(sums), last=last, members=members, total=total, fields=fields
             ),
-            in_specs=[vmem] * 7 + [hbm] + [vmem] * len(sums),
-            out_specs=[vmem] * 4,
-            out_shape=[
-                shape((n, LANES, span), BF16),
-                shape((LANES, width), F32),
-                shape((rows, LANES), F32),
-                shape((8, LANES), F32),
-            ],
+            in_specs=[vmem] * (8 + len(sums)),
+            out_specs=[vmem] * (1 + len(outs)),
+            out_shape=[shape((n, LANES, span), BF16)] + outs,
             scratch_shapes=[
                 pltpu.VMEM((1, LANES), F32),
                 pltpu.VMEM((rows, LANES), F32),
                 pltpu.VMEM((n, LANES, span), F32),
-                pltpu.VMEM((n, members, LANES, width), BF16),
-                pltpu.SemaphoreType.DMA((n,)),
-            ],
+            ]
+            + extra,
             compiler_params=params(),
             cost_estimate=cost(us),
             name="far",
-        )(own, away, fwd, acc, area, coef, loss, hidden, *sums)
+        )(own, away, fwd, acc, area, coef, loss, x, *sums)
 
     across = lambda a: lax.ppermute(a, "member", chip_swap)
     beside = lambda a: lax.ppermute(a, "member", core_swap)
     hold = lax.optimization_barrier
     n0, n1, n2 = TILES
     a1, a2 = n0, n0 + n1
-    own0, out0 = forecast(n0, 0, US[0])
+    x0, own0, out0 = forecast(n0, 0, US[0])
     away0 = across(out0)
-    own1, out1 = forecast(n1, a1, US[1])
+    x1, own1, out1 = forecast(n1, a1, US[1])
     away1 = across(out1)
-    own2, out2 = forecast(n2, a2, US[2])
+    x2, own2, out2 = forecast(n2, a2, US[2])
     own0, out2 = hold((own0, out2))
     away2 = across(out2)
     sib0, sib1, sib2 = beside(out0), beside(out1), beside(out2)
@@ -334,21 +337,14 @@
     acc1, loss1 = near(n1, a1, US[4], own1, sib1)
     away1, acc1, acc0 = hold((away1, acc1, acc0))
     fwd1 = beside(away1)
-    grad0, *sums = far(n0, 0, US[5], own0, away0, fwd0, acc0, loss0)
-    grad1, *sums = far(n1, a1, US[6], own1, away1, fwd1, acc1, loss1, *sums)
+    grad0, *sums = far(n0, 0, US[5], own0, away0, fwd0, acc0, loss0, x0)
+    grad1, *sums = far(n1, a1, US[6], own1, away1, fwd1, acc1, loss1, x1, *sums)
     away2, own2, *sums = hold((away2, own2, *sums))
     fwd2 = beside(away2)
     acc2, loss2 = near(n2, a2, US[7], own2, sib2)
-    grad2, *sums = far(n2, a2, US[8], own2, away2, fwd2, acc2, loss2, *sums)
+    grad2, packed = far(n2, a2, US[8], own2, away2, fwd2, acc2, loss2, x2, *sums, last=True)
     grads = [grad0, grad1, grad2]
 
-    packed = pl.pallas_call(
-        functools.partial(pack_kernel, fields=fields),
-        out_shape=shape((width, LANES), BF16),
-        scratch_shapes=[pltpu.VMEM((LANES, LANES), F32)],
-        compiler_params=params(),
-        name="pack",
-    )(*sums)
     parts = lax.all_to_all(packed, ("member", "point"), split_axis=0, concat_axis=0, tiled=True)
 
     grad = grads[0] if len(grads) == 1 else jnp.concatenate(grads, axis=0)

time: 58.9 us -> 57.1 us (0.969)
  Pallas kernels: 23.2 us -> 20.6 us
  starting transfers between devices: 23.2 us -> 23.9 us
    pallas_call x3, Pallas kernels: 8.28 us -> 6.81 us  [forecast(): pl.pallas_call(functools.partial(forecast_kernel, first=first), in_specs=...]
    pallas_call x1 -> x0, Pallas kernels: 0.96 us -> none  [shards(): pl.pallas_call(functools.partial(pack_kernel, fields=fields), out_shape=s...]
    ppermute x6, starting transfers between devices: 6.23 us -> 6.9 us  [shards(): beside = lambda a: lax.ppermute(a, 'member', core_swap)]
  transfers between devices with their start and end apart: 10 -> 10, of which waited for: 3 -> 3; matrix products, arithmetic and copies ran while one was open for 0% -> 0% of each run, Pallas kernels for 28% -> 27%
where the time goes in v3:
time: 57.1 us; the launch traced here: 56.9 us
  starting transfers between devices  23.9 us (42%)
  Pallas kernels  20.6 us (36%)
  waiting for transfers between devices  11.4 us (20%)
  between operations  0.78 us (1%)
    all_to_all x1, starting transfers between devices, shards(): lax.all_to_all(packed, ('member', 'point'), split_axis=0, concat_axis=0,...  12.8 us
    all_to_all x1, waiting for transfers between devices, shards(): lax.all_to_all(packed, ('member', 'point'), split_axis=0, concat_axis=0,...  10.4 us
    ppermute x6, starting transfers between devices, shards(): beside = lambda a: lax.ppermute(a, 'member', core_swap)  6.9 us
    pallas_call x3, Pallas kernels, forecast(): pl.pallas_call(functools.partial(forecast_kernel, first=first), in_specs=...  6.81 us
    pallas_call x3, Pallas kernels, far(): pl.pallas_call(functools.partial(far_kernel, first=first, before=len(sums...  5.59 us
    pallas_call x1, Pallas kernels, shards(): pl.pallas_call(slope_kernel, grid=(points // LANES,), in_specs=[tile((LAN...  4.79 us
    ppermute x3, starting transfers between devices, shards(): across = lambda a: lax.ppermute(a, 'member', chip_swap)  4.26 us
    pallas_call x3, Pallas kernels, near(): pl.pallas_call(functools.partial(near_kernel, first=first, members=member...  2.71 us
  transfers between devices with their start and end apart: 10, of which 3 were waited for; matrix products, arithmetic and copies ran while one was open for 0% of the time, Pallas kernels for 27%

profile of v3, /device:TPU:1, one launch (start us, length us, event | category | flops | bytes accessed | tf_op | source)
XLA Modules:
  0.0 56.9 jit_solution(16677149683914537454)
XLA Ops:
  0.6 2.3 %forecast.3 = (bf16[2,4,128,1024]{3,2,1,0:T(8,128)(2,1)S(1)}, f32[2,104,512]{2,1,0:T(8,128)S(1)}, bf16[2,416,128]{2,1,0:T(8,128)(2,1)S(1)}) custom-call(bf16[4,768,1024]{2,1,0:T(8,128)(2,1)} %x_hbm.5, bf16[100,1024]{1,0:T(8,128)(2,1)} %bitcast.8), custom_call_target="tpu_custom_call" | custom-call | flops 10000000 | bytes 35000 | tf_op jit(solution)/shard_map/forecast/pallas_call | solution.py:260
  2.9 3.3 %collective-permute-start.2 = (bf16[2,416,128]{2,1,0:T(8,128)(2,1)S(1)}, bf16[2,416,128]{2,1,0:T(8,128)(2,1)S(1)}, u32[]{:S(2)}, u32[]{:S(2)}) collective-permute-start(bf16[2,416,128]{2,1,0:T(8,128)(2,1)S(1)} %get-tuple-element.49), channel_id=1, source_target_pairs={{0,64},{64,0},{128,192},{192,128},{1,65},{65,1},{129,193},{193,129... | collective-permute-start | bytes 638984 | tf_op jit(solution)/shard_map/ppermute | solution.py:322
  6.2 1.2 %collective-permute-start.1 = (bf16[2,416,128]{2,1,0:T(8,128)(2,1)S(1)}, bf16[2,416,128]{2,1,0:T(8,128)(2,1)S(1)}, u32[]{:S(2)}, u32[]{:S(2)}) collective-permute-start(bf16[2,416,128]{2,1,0:T(8,128)(2,1)S(1)} %get-tuple-element.49), channel_id=1, source_target_pairs={{0,128},{64,192},{128,0},{192,64},{1,129},{65,193},{129,1},{193,65... | collective-permute-start | bytes 638984 | tf_op jit(solution)/shard_map/ppermute | solution.py:321
  7.4 2.3 %forecast.5 = (bf16[2,4,128,1024]{3,2,1,0:T(8,128)(2,1)S(1)}, f32[2,104,512]{2,1,0:T(8,128)S(1)}, bf16[2,416,128]{2,1,0:T(8,128)(2,1)S(1)}) custom-call(bf16[4,768,1024]{2,1,0:T(8,128)(2,1)} %x_hbm.5, bf16[100,1024]{1,0:T(8,128)(2,1)} %bitcast.9), custom_call_target="tpu_custom_call" | custom-call | flops 10000000 | bytes 35000 | tf_op jit(solution)/shard_map/forecast/pallas_call | solution.py:260
  9.7 0.0 copy-start.4
  9.7 0.0 copy-start.1
  9.7 0.0 copy-start.2
  9.7 0.0 copy-start.3
  9.8 0.4 collective-permute-start.4
  10.2 1.8 %collective-permute-start.3 = (bf16[2,416,128]{2,1,0:T(8,128)(2,1)S(1)}, bf16[2,416,128]{2,1,0:T(8,128)(2,1)S(1)}, u32[]{:S(2)}, u32[]{:S(2)}) collective-permute-start(bf16[2,416,128]{2,1,0:T(8,128)(2,1)S(1)} %get-tuple-element.54), channel_id=1, source_target_pairs={{0,128},{64,192},{128,0},{192,64},{1,129},{65,193},{129,1},{193,65... | collective-permute-start | bytes 638984 | tf_op jit(solution)/shard_map/ppermute | solution.py:321
  12.0 2.3 %forecast.4 = (bf16[2,4,128,1024]{3,2,1,0:T(8,128)(2,1)S(1)}, f32[2,104,512]{2,1,0:T(8,128)S(1)}, bf16[2,416,128]{2,1,0:T(8,128)(2,1)S(1)}) custom-call(bf16[4,768,1024]{2,1,0:T(8,128)(2,1)} %x_hbm.5, bf16[100,1024]{1,0:T(8,128)(2,1)} %bitcast.10), custom_call_target="tpu_custom_call" | custom-call | flops 10000000 | bytes 35000 | tf_op jit(solution)/shard_map/forecast/pallas_call | solution.py:260
  14.3 1.3 %collective-permute-start = (bf16[2,416,128]{2,1,0:T(8,128)(2,1)S(1)}, bf16[2,416,128]{2,1,0:T(8,128)(2,1)S(1)}, u32[]{:S(2)}, u32[]{:S(2)}) collective-permute-start(bf16[2,416,128]{2,1,0:T(8,128)(2,1)S(1)} %get-tuple-element.47), channel_id=1, source_target_pairs={{0,128},{64,192},{128,0},{192,64},{1,129},{65,193},{129,1},{193,65... | collective-permute-start | bytes 638984 | tf_op jit(solution)/shard_map/ppermute | solution.py:321
  15.6 0.0 collective-permute-done.2.sib_ref
  15.6 0.8 %collective-permute-start.8 = (bf16[2,416,128]{2,1,0:T(8,128)(2,1)S(1)}, bf16[2,416,128]{2,1,0:T(8,128)(2,1)S(1)}, u32[]{:S(2)}, u32[]{:S(2)}) collective-permute-start(bf16[2,416,128]{2,1,0:T(8,128)(2,1)S(1)} %get-tuple-element.47), channel_id=1, source_target_pairs={{0,64},{64,0},{128,192},{192,128},{1,65},{65,1},{129,193},{193,129... | collective-permute-start | bytes 638984 | tf_op jit(solution)/shard_map/ppermute | solution.py:322
  16.4 0.9 %near.3 = (f32[2,104,512]{2,1,0:T(8,128)S(1)}, f32[8,128]{1,0:T(8,128)S(1)}) custom-call(f32[2,104,512]{2,1,0:T(8,128)S(1)} %get-tuple-element.50.own_ref.refs_0_, bf16[2,416,128]{2,1,0:T(8,128)(2,1)S(1)} %collective-permute-done.2.sib_ref, f32[100,768]{1,0:T(8,128)S(1)} %bitcast.13, f32[1,768]{1,0:T(1,128)S(1)} %broadcast_in_dim.9.area_ref.refs_4_, ...), custom_call_target="tpu_custom_call" | custom-call | flops 10000000 | bytes 35000 | tf_op jit(solution)/shard_map/near/pallas_call | solution.py:280
  17.3 0.0 collective-permute-done.1.refs_1_
  17.3 0.1 collective-permute-start.6
  17.4 0.0 collective-permute-done.4.sib_ref
  17.4 0.9 %near.4 = (f32[2,104,512]{2,1,0:T(8,128)S(1)}, f32[8,128]{1,0:T(8,128)S(1)}) custom-call(f32[2,104,512]{2,1,0:T(8,128)S(1)} %get-tuple-element.53.own_ref.refs_0_, bf16[2,416,128]{2,1,0:T(8,128)(2,1)S(1)} %collective-permute-done.4.sib_ref, f32[100,768]{1,0:T(8,128)S(1)} %bitcast.14, f32[1,768]{1,0:T(1,128)S(1)} %broadcast_in_dim.9.area_ref.refs_4_, ...), custom_call_target="tpu_custom_call" | custom-call | flops 8000000000 | bytes 28000000 | tf_op jit(solution)/shard_map/near/pallas_call | solution.py:280
  18.3 0.8 %collective-permute-done.3.refs_1_ = bf16[2,416,128]{2,1,0:T(8,128)(2,1)S(1)} collective-permute-done((bf16[2,416,128]{2,1,0:T(8,128)(2,1)S(1)}, bf16[2,416,128]{2,1,0:T(8,128)(2,1)S(1)}, u32[]{:S(2)}, u32[]{:S(2)}) %collective-permute-start.3) | collective-permute-done | bytes 213024 | tf_op jit(solution)/shard_map/ppermute | solution.py:321
  19.1 1.3 %collective-permute-start.5 = (bf16[2,416,128]{2,1,0:T(8,128)(2,1)S(1)}, bf16[2,416,128]{2,1,0:T(8,128)(2,1)S(1)}, u32[]{:S(2)}, u32[]{:S(2)}) collective-permute-start(bf16[2,416,128]{2,1,0:T(8,128)(2,1)S(1)} %collective-permute-done.3.refs_1_), channel_id=1, source_target_pairs={{0,64},{64,0},{128,192},{192,128},{1,65},{65,1},{129,193},{193,129... | collective-permute-start | bytes 638984 | tf_op jit(solution)/shard_map/ppermute | solution.py:322
  20.5 1.6 %far.3 = (bf16[2,128,512]{2,1,0:T(8,128)(2,1)S(1)}, f32[128,1024]{1,0:T(8,128)S(1)}, f32[104,128]{1,0:T(8,128)S(1)}, f32[8,128]{1,0:T(8,128)S(1)}) custom-call(f32[2,104,512]{2,1,0:T(8,128)S(1)} %get-tuple-element.50.own_ref.refs_0_, bf16[2,416,128]{2,1,0:T(8,128)(2,1)S(1)} %collective-permute-done.1.refs_1_, ...), custom_call_target="tpu_custom_call" | custom-call | flops 8000000000 | bytes 28000000 | tf_op jit(solution)/shard_map/far/pallas_call | solution.py:303
  22.1 1.6 %far.4 = (bf16[2,128,512]{2,1,0:T(8,128)(2,1)S(1)}, f32[128,1024]{1,0:T(8,128)S(1)}, f32[104,128]{1,0:T(8,128)S(1)}, f32[8,128]{1,0:T(8,128)S(1)}) custom-call(f32[2,104,512]{2,1,0:T(8,128)S(1)} %get-tuple-element.53.own_ref.refs_0_, bf16[2,416,128]{2,1,0:T(8,128)(2,1)S(1)} %collective-permute-done.3.refs_1_, ...), custom_call_target="tpu_custom_call" | custom-call | flops 10000000 | bytes 35000 | tf_op jit(solution)/shard_map/far/pallas_call | solution.py:303
  23.7 0.8 %collective-permute-start.7 = (bf16[2,416,128]{2,1,0:T(8,128)(2,1)S(1)}, bf16[2,416,128]{2,1,0:T(8,128)(2,1)S(1)}, u32[]{:S(2)}, u32[]{:S(2)}) collective-permute-start(bf16[2,416,128]{2,1,0:T(8,128)(2,1)S(1)} %collective-permute-done.refs_1_), channel_id=1, source_target_pairs={{0,64},{64,0},{128,192},{192,128},{1,65},{65,1},{129,193},{193,129... | collective-permute-start | bytes 638984 | tf_op jit(solution)/shard_map/ppermute | solution.py:322
  24.6 0.9 %near.5 = (f32[2,104,512]{2,1,0:T(8,128)S(1)}, f32[8,128]{1,0:T(8,128)S(1)}) custom-call(f32[2,104,512]{2,1,0:T(8,128)S(1)} %get-tuple-element.71.own_ref.refs_0_, bf16[2,416,128]{2,1,0:T(8,128)(2,1)S(1)} %collective-permute-done.8.sib_ref, f32[100,768]{1,0:T(8,128)S(1)} %bitcast.15, f32[1,768]{1,0:T(1,128)S(1)} %broadcast_in_dim.9.area_ref.refs_4_, ...), custom_call_target="tpu_custom_call" | custom-call | flops 8000000000 | bytes 28000000 | tf_op jit(solution)/shard_map/near/pallas_call | solution.py:280
  25.5 0.2 collective-permute-done.7.refs_2_
  25.7 2.4 %far.5 = (bf16[2,128,512]{2,1,0:T(8,128)(2,1)S(1)}, bf16[1024,128]{1,0:T(8,128)(2,1)}) custom-call(f32[2,104,512]{2,1,0:T(8,128)S(1)} %get-tuple-element.71.own_ref.refs_0_, bf16[2,416,128]{2,1,0:T(8,128)(2,1)S(1)} %collective-permute-done.refs_1_, bf16[2,416,128]{2,1,0:T(8,128)(2,1)S(1)} %collective-permute-done.7.refs_2_, ...), custom_call_target="tpu_custom_call" | custom-call | flops 10000000 | bytes 35000 | tf_op jit(solution)/shard_map/far/pallas_call | solution.py:303
  28.0 12.8 %all-to-all-start = ((bf16[256,4,128]{2,1,0:T(4,128)(2,1)}), bf16[256,4,128]{2,1,0:T(4,128)(2,1)S(1)}, u32[]{:S(2)}, u32[]{:S(2)}) async-start(bf16[256,4,128]{2,1,0:T(4,128)(2,1)} %bitcast.4), calls=%async_computation | async-start | bytes 524288 | tf_op jit(solution)/shard_map/all_to_all | solution.py:348
  40.8 0.1 pad_maximum_fusion.grad_ref
  40.9 4.8 %slope.1 = bf16[4,768,1024]{2,1,0:T(8,128)(2,1)} custom-call(bf16[6,128,512]{2,1,0:T(8,128)(2,1)S(1)} %pad_maximum_fusion.grad_ref, bf16[100,1024]{1,0:T(8,128)(2,1)S(1)} %bitcast.11), custom_call_target="tpu_custom_call" | custom-call | flops 5000000000 | bytes 17500000 | tf_op jit(solution)/shard_map/slope/pallas_call | solution.py:351
  45.7 10.4 %all-to-all-done = bf16[256,4,128]{2,1,0:T(4,128)(2,1)S(1)} async-done(((bf16[256,4,128]{2,1,0:T(4,128)(2,1)}), bf16[256,4,128]{2,1,0:T(4,128)(2,1)S(1)}, u32[]{:S(2)}, u32[]{:S(2)}) %all-to-all-start) | async-done | bytes 262176 | tf_op jit(solution)/shard_map/all_to_all | solution.py:348
  56.2 0.7 %finish.1 = (f32[4,100]{1,0:T(4,128)}, f32[1,100]{1,0:T(1,128)}, f32[1,1]{1,0:T(1,128)}) custom-call(bf16[1024,128]{1,0:T(8,128)(2,1)S(1)} %bitcast.12), custom_call_target="tpu_custom_call" | custom-call | tf_op jit(solution)/shard_map/finish/pallas_call | solution.py:363
  (11 shorter events, 0.0 us)
Async XLA Ops:
  2.9 12.6 %collective-permute-start.2 = (bf16[2,416,128]{2,1,0:T(8,128)(2,1)S(1)}, bf16[2,416,128]{2,1,0:T(8,128)(2,1)S(1)}, u32[]{:S(2)}, u32[]{:S(2)}) collective-permute-start(bf16[2,416,128]{2,1,0:T(8,128)(2,1)S(1)} %get-tuple-element.49), channel_id=1, source_target_pairs={{0,64},{64,0},{128,192},{192,128},{1,65},{65,1},{129,193},{193,129... | collective-permute-start | bytes 638984 | tf_op jit(solution)/shard_map/ppermute | solution.py:322
  6.2 11.1 %collective-permute-start.1 = (bf16[2,416,128]{2,1,0:T(8,128)(2,1)S(1)}, bf16[2,416,128]{2,1,0:T(8,128)(2,1)S(1)}, u32[]{:S(2)}, u32[]{:S(2)}) collective-permute-start(bf16[2,416,128]{2,1,0:T(8,128)(2,1)S(1)} %get-tuple-element.49), channel_id=1, source_target_pairs={{0,128},{64,192},{128,0},{192,64},{1,129},{65,193},{129,1},{193,65... | collective-permute-start | bytes 638984 | tf_op jit(solution)/shard_map/ppermute | solution.py:321
  9.7 5.8 %copy-start.4 = (f32[768]{0:T(1024)S(1)}, f32[768]{0:T(1024)}, u32[]{:S(2)}) copy-start(f32[768]{0:T(1024)} %param.10) | copy-start | bytes 9220
  9.7 6.6 %copy-start.1 = (f32[768,100]{0,1:T(8,128)S(1)}, f32[768,100]{0,1:T(8,128)}, u32[]{:S(2)}) copy-start(f32[768,100]{0,1:T(8,128)} %param.9) | copy-start | bytes 921604
  9.7 6.6 %copy-start.2 = (f32[100]{0:T(128)S(1)}, f32[100]{0:T(128)}, u32[]{:S(2)}) copy-start(f32[100]{0:T(128)} %param.11) | copy-start | bytes 1204
  9.7 6.6 %copy-start.3 = (f32[100]{0:T(128)S(1)}, f32[100]{0:T(128)}, u32[]{:S(2)}) copy-start(f32[100]{0:T(128)} %param.8) | copy-start | bytes 1204
  9.8 7.7 %collective-permute-start.4 = (bf16[2,416,128]{2,1,0:T(8,128)(2,1)S(1)}, bf16[2,416,128]{2,1,0:T(8,128)(2,1)S(1)}, u32[]{:S(2)}, u32[]{:S(2)}) collective-permute-start(bf16[2,416,128]{2,1,0:T(8,128)(2,1)S(1)} %get-tuple-element.54), channel_id=1, source_target_pairs={{0,64},{64,0},{128,192},{192,128},{1,65},{65,1},{129,193},{193,129... | collective-permute-start | bytes 638984 | tf_op jit(solution)/shard_map/ppermute | solution.py:322
  10.2 8.9 %collective-permute-start.3 = (bf16[2,416,128]{2,1,0:T(8,128)(2,1)S(1)}, bf16[2,416,128]{2,1,0:T(8,128)(2,1)S(1)}, u32[]{:S(2)}, u32[]{:S(2)}) collective-permute-start(bf16[2,416,128]{2,1,0:T(8,128)(2,1)S(1)} %get-tuple-element.54), channel_id=1, source_target_pairs={{0,128},{64,192},{128,0},{192,64},{1,129},{65,193},{129,1},{193,65... | collective-permute-start | bytes 638984 | tf_op jit(solution)/shard_map/ppermute | solution.py:321
  14.3 9.4 %collective-permute-start = (bf16[2,416,128]{2,1,0:T(8,128)(2,1)S(1)}, bf16[2,416,128]{2,1,0:T(8,128)(2,1)S(1)}, u32[]{:S(2)}, u32[]{:S(2)}) collective-permute-start(bf16[2,416,128]{2,1,0:T(8,128)(2,1)S(1)} %get-tuple-element.47), channel_id=1, source_target_pairs={{0,128},{64,192},{128,0},{192,64},{1,129},{65,193},{129,1},{193,65... | collective-permute-start | bytes 638984 | tf_op jit(solution)/shard_map/ppermute | solution.py:321
  15.6 9.0 %collective-permute-start.8 = (bf16[2,416,128]{2,1,0:T(8,128)(2,1)S(1)}, bf16[2,416,128]{2,1,0:T(8,128)(2,1)S(1)}, u32[]{:S(2)}, u32[]{:S(2)}) collective-permute-start(bf16[2,416,128]{2,1,0:T(8,128)(2,1)S(1)} %get-tuple-element.47), channel_id=1, source_target_pairs={{0,64},{64,0},{128,192},{192,128},{1,65},{65,1},{129,193},{193,129... | collective-permute-start | bytes 638984 | tf_op jit(solution)/shard_map/ppermute | solution.py:322
  17.3 3.2 %collective-permute-start.6 = (bf16[2,416,128]{2,1,0:T(8,128)(2,1)S(1)}, bf16[2,416,128]{2,1,0:T(8,128)(2,1)S(1)}, u32[]{:S(2)}, u32[]{:S(2)}) collective-permute-start(bf16[2,416,128]{2,1,0:T(8,128)(2,1)S(1)} %collective-permute-done.1.refs_1_), channel_id=1, source_target_pairs={{0,64},{64,0},{128,192},{192,128},{1,65},{65,1},{129,193},{193,129... | collective-permute-start | bytes 638984 | tf_op jit(solution)/shard_map/ppermute | solution.py:322
  19.1 3.0 %collective-permute-start.5 = (bf16[2,416,128]{2,1,0:T(8,128)(2,1)S(1)}, bf16[2,416,128]{2,1,0:T(8,128)(2,1)S(1)}, u32[]{:S(2)}, u32[]{:S(2)}) collective-permute-start(bf16[2,416,128]{2,1,0:T(8,128)(2,1)S(1)} %collective-permute-done.3.refs_1_), channel_id=1, source_target_pairs={{0,64},{64,0},{128,192},{192,128},{1,65},{65,1},{129,193},{193,129... | collective-permute-start | bytes 638984 | tf_op jit(solution)/shard_map/ppermute | solution.py:322
  23.7 1.9 %collective-permute-start.7 = (bf16[2,416,128]{2,1,0:T(8,128)(2,1)S(1)}, bf16[2,416,128]{2,1,0:T(8,128)(2,1)S(1)}, u32[]{:S(2)}, u32[]{:S(2)}) collective-permute-start(bf16[2,416,128]{2,1,0:T(8,128)(2,1)S(1)} %collective-permute-done.refs_1_), channel_id=1, source_target_pairs={{0,64},{64,0},{128,192},{192,128},{1,65},{65,1},{129,193},{193,129... | collective-permute-start | bytes 638984 | tf_op jit(solution)/shard_map/ppermute | solution.py:322
  25.6 15.3 %copy-start = (bf16[1024,100]{0,1:T(8,128)(2,1)S(1)}, bf16[1024,100]{0,1:T(8,128)(2,1)}, u32[]{:S(2)}) copy-start(bf16[1024,100]{0,1:T(8,128)(2,1)} %param.7) | copy-start | bytes 614404
  28.0 28.1 %all-to-all-start = ((bf16[256,4,128]{2,1,0:T(4,128)(2,1)}), bf16[256,4,128]{2,1,0:T(4,128)(2,1)S(1)}, u32[]{:S(2)}, u32[]{:S(2)}) async-start(bf16[256,4,128]{2,1,0:T(4,128)(2,1)} %bitcast.4), calls=%async_computation | async-start | bytes 524288 | tf_op jit(solution)/shard_map/all_to_all | solution.py:348

commit v4 on v3

--- a/solution.py
+++ b/solution.py
@@ -11,7 +11,7 @@
 BF16 = jnp.bfloat16
 LANES = 128
 TILES = (2, 2, 2)
-US = (.01,.01,.01,.01,8,8,.01,8,.01)
+US = (.01,.01,.01,.01,8,8,.01,.01,.01,8)
 SMOOTH = 0.05 * 0.05
 ALPHA = 0.95
 
@@ -22,6 +22,24 @@
 
 def round_up(n, k):
     return -(-n // k) * k
+
+
+def half_turn(a):
+    return pltpu.roll(a, 4, 0)
+
+
+def interleaved(f, members, fields):
+    parts = lambda g: [f[8 * g : 8 * g + 8, m * LANES : (m + 1) * LANES] for m in range(members)]
+    groups = [p for g in range(fields // 8) for p in parts(g)]
+    ends = parts(fields // 8)
+    groups += [ends[m] + half_turn(ends[m + 1]) for m in range(0, members, 2)]
+    return jnp.concatenate(groups, axis=0).astype(BF16)
+
+
+def others(ref, t, g, members, fields):
+    count = members if 8 * g + 8 <= fields else members // 2
+    block = ref[t, 8 * members * g : 8 * members * g + 8 * count, :].astype(F32)
+    return [block[8 * n : 8 * n + 8] for n in range(count)]
 
 
 def forecast_kernel(x_hbm, w_hbm, x, own_ref, sent_ref, w, x_sems, w_sem, *, first):
@@ -50,12 +68,7 @@
         f = jnp.concatenate([f, jnp.zeros((members * LANES, LANES - fields), F32)], axis=1)
         f = f.T[:rows]
         own_ref[t] = f
-        groups = [
-            f[8 * g : 8 * g + 8, m * LANES : (m + 1) * LANES]
-            for g in range(rows // 8)
-            for m in range(members)
-        ]
-        sent_ref[t] = jnp.concatenate(groups, axis=0).astype(BF16)
+        sent_ref[t] = interleaved(f, members, fields)
         return carry
 
     lax.fori_loop(0, tiles, step, 0)
@@ -97,21 +110,28 @@
         for g in range(rows // 8):
             span = slice(8 * g, 8 * g + 8)
             own = [own_ref[t, span, m * LANES : (m + 1) * LANES] for m in range(members)]
-            sib = sib_ref[t, 8 * members * g : 8 * members * (g + 1), :].astype(F32)
+            sib = others(sib_ref, t, g, members, fields)
+            folded = len(sib) < members
             skill = jnp.zeros((8, LANES), F32)
             spread = jnp.zeros((8, LANES), F32)
             inner = jnp.zeros((8, LANES), F32)
             slopes = [jnp.zeros((8, LANES), F32) for _ in range(members)]
+            for m in range(members):
+                mine = own[m] + half_turn(own[m]) if folded else own[m]
+                for other in sib:
+                    a, b = slope_and_length(mine - other)
+                    slopes[m] = slopes[m] + a
+                    spread = spread + b
+                if folded:
+                    slopes[m] = slopes[m] + half_turn(slopes[m])
+            if folded:
+                spread = spread + half_turn(spread)
             for m in range(members):
                 for n in range(m + 1, members):
                     a, b = slope_and_length(own[m] - own[n])
                     slopes[m] = slopes[m] + a
                     slopes[n] = slopes[n] - a
                     inner = inner + b
-                for n in range(members):
-                    a, b = slope_and_length(own[m] - sib[8 * n : 8 * n + 8])
-                    slopes[m] = slopes[m] + a
-                    spread = spread + b
             for m in range(members):
                 a, b = slope_and_length(own[m] - goal[t, span, :])
                 skill = skill + b
@@ -119,6 +139,43 @@
             loss = loss + coefs[span] * (skill * (1.0 / total) - c2 * (spread + 2.0 * inner))
         at = pl.multiple_of((first + t) * LANES, LANES)
         loss_ref[...] += loss * area_ref[:, pl.ds(at, LANES)]
+        return carry
+
+    lax.fori_loop(0, tiles, step, 0)
+
+
+def direct_kernel(own_ref, far_ref, acc_ref, loss_in, area_ref, coef_ref, out_ref, loss_ref, rpad, coefs, *, first, members, total):
+    tiles, rows, _ = own_ref.shape
+    fields = coef_ref.shape[1]
+    c1 = (1.0 - (1.0 - ALPHA) / total) / (total - 1)
+    c2 = (1.0 - (1.0 - ALPHA) / total) / (2.0 * total * (total - 1))
+    coefs[...] = column(pad_row(coef_ref, rpad, fields), rows)
+    loss_ref[...] = loss_in[...]
+
+    def step(t, carry):
+        loss = jnp.zeros((8, LANES), F32)
+        for g in range(rows // 8):
+            span = slice(8 * g, 8 * g + 8)
+            own = [own_ref[t, span, m * LANES : (m + 1) * LANES] for m in range(members)]
+            remote = others(far_ref, t, g, members, fields)
+            folded = len(remote) < members
+            spread = jnp.zeros((8, LANES), F32)
+            for m in range(members):
+                mine = own[m] + half_turn(own[m]) if folded else own[m]
+                slopes = jnp.zeros((8, LANES), F32)
+                for other in remote:
+                    a, b = slope_and_length(mine - other)
+                    slopes = slopes + a
+                    spread = spread + b
+                if folded:
+                    slopes = slopes + half_turn(slopes)
+                here = slice(m * LANES, (m + 1) * LANES)
+                out_ref[t, span, here] = acc_ref[t, span, here] - c1 * slopes
+            if folded:
+                spread = spread + half_turn(spread)
+            loss = loss + coefs[span] * spread
+        at = pl.multiple_of((first + t) * LANES, LANES)
+        loss_ref[...] -= c2 * loss * area_ref[:, pl.ds(at, LANES)]
         return carry
 
     lax.fori_loop(0, tiles, step, 0)
@@ -149,9 +206,10 @@
     return table.reshape(-1, LANES).astype(BF16)
 
 
-def far_kernel(*refs, first, before, last, members, total, fields):
-    own_ref, far_ref, fwd_ref, acc_ref, area_ref, coef_ref, near_loss, x = refs[:8]
-    earlier, refs = refs[8 : 8 + before], refs[8 + before :]
+def far_kernel(*refs, first, before, received, last, members, total, fields):
+    own_ref, acc_ref, area_ref, coef_ref, near_loss, x = refs[:6]
+    earlier, refs = refs[6 : 6 + before], refs[6 + before :]
+    sources, refs = refs[:received], refs[received:]
     if last:
         grad_ref, out_ref, rpad, coefs, grads, bias_ref, loss_ref, padded = refs
     else:
@@ -177,24 +235,27 @@
         loss = jnp.zeros((8, LANES), F32)
         for g in range(rows // 8):
             span = slice(8 * g, 8 * g + 8)
-            part = slice(8 * members * g, 8 * members * (g + 1))
             own = [own_ref[t, span, m * LANES : (m + 1) * LANES] for m in range(members)]
-            far = far_ref[t, part, :].astype(F32)
-            fwd = fwd_ref[t, part, :].astype(F32)
+            remote = [o for ref in sources for o in others(ref, t, g, members, fields)]
+            folded = len(remote) < received * members
             spread = jnp.zeros((8, LANES), F32)
             scale = coefs[span] * area
             bias = jnp.zeros((8, LANES), F32)
             for m in range(members):
+                mine = own[m] + half_turn(own[m]) if folded else own[m]
                 slopes = jnp.zeros((8, LANES), F32)
-                for other in (far, fwd):
-                    for n in range(members):
-                        a, b = slope_and_length(own[m] - other[8 * n : 8 * n + 8])
-                        slopes = slopes + a
-                        spread = spread + b
+                for other in remote:
+                    a, b = slope_and_length(mine - other)
+                    slopes = slopes + a
+                    spread = spread + b
+                if folded:
+                    slopes = slopes + half_turn(slopes)
                 here = slice(m * LANES, (m + 1) * LANES)
                 grad = (scale * (acc_ref[t, span, here] - c1 * slopes)).astype(BF16).astype(F32)
                 grads[t, span, here] = grad
                 bias = bias + grad
+            if folded:
+                spread = spread + half_turn(spread)
             bias_ref[span, :] += bias
             loss = loss + coefs[span] * spread
         loss_ref[...] -= c2 * loss * area
@@ -247,6 +308,7 @@
     all_points = points * lax.axis_size("point")
     rows = round_up(fields, 8)
     span = members * LANES
+    sent_rows = members * fields
     weights, truth = weights.T, truth.T
     shift, coef, area = shift[None], coef[None], area[None]
     tile = lambda shape: pl.BlockSpec((1,) + shape, lambda i: (i, 0, 0))
@@ -264,7 +326,7 @@
             out_shape=[
                 shape((n, members, LANES, width), BF16),
                 shape((n, rows, span), F32),
-                shape((n, rows * members, LANES), BF16),
+                shape((n, sent_rows, LANES), BF16),
             ],
             scratch_shapes=[
                 pltpu.VMEM((fields, width), BF16),
@@ -292,7 +354,19 @@
             name="near",
         )(own, sib, truth, area, shift, coef)
 
-    def far(n, first, us, own, away, fwd, acc, loss, x, *sums, last=False):
+    def direct(n, first, us, own, away, acc, loss):
+        return pl.pallas_call(
+            functools.partial(direct_kernel, first=first, members=members, total=total),
+            in_specs=[vmem] * 6,
+            out_specs=[vmem] * 2,
+            out_shape=[shape((n, rows, span), F32), shape((8, LANES), F32)],
+            scratch_shapes=[pltpu.VMEM((1, LANES), F32), pltpu.VMEM((rows, LANES), F32)],
+            compiler_params=params(),
+            cost_estimate=cost(us),
+            name="direct",
+        )(own, away, acc, loss, area, coef)
+
+    def far(n, first, us, own, acc, loss, x, *sums, received, last=False):
         sums_shapes = [((rows, LANES), F32), ((8, LANES), F32)]
         if last:
             outs = [shape((width, LANES), BF16)]
@@ -302,9 +376,9 @@
             extra = []
         return pl.pallas_call(
             functools.partial(
-                far_kernel, first=first, before=len(sums), last=last, members=members, total=total, fields=fields
+                far_kernel, first=first, before=len(sums), received=len(received), last=last, members=members, total=total, fields=fields
             ),
-            in_specs=[vmem] * (8 + len(sums)),
+            in_specs=[vmem] * (6 + len(sums) + len(received)),
             out_specs=[vmem] * (1 + len(outs)),
             out_shape=[shape((n, LANES, span), BF16)] + outs,
             scratch_shapes=[
@@ -316,7 +390,7 @@
             compiler_params=params(),
             cost_estimate=cost(us),
             name="far",
-        )(own, away, fwd, acc, area, coef, loss, x, *sums)
+        )(own, acc, area, coef, loss, x, *sums, *received)
 
     across = lambda a: lax.ppermute(a, "member", chip_swap)
     beside = lambda a: lax.ppermute(a, "member", core_swap)
@@ -332,17 +406,18 @@
     away2 = across(out2)
     sib0, sib1, sib2 = beside(out0), beside(out1), beside(out2)
     acc0, loss0 = near(n0, 0, US[3], own0, sib0)
-    away0, acc0, own1 = hold((away0, acc0, own1))
+    away0, acc0, own1, own2 = hold((away0, acc0, own1, own2))
     fwd0 = beside(away0)
     acc1, loss1 = near(n1, a1, US[4], own1, sib1)
-    away1, acc1, acc0 = hold((away1, acc1, acc0))
+    acc2, loss2 = near(n2, a2, US[7], own2, sib2)
+    away1, acc1, acc0, acc2 = hold((away1, acc1, acc0, acc2))
     fwd1 = beside(away1)
-    grad0, *sums = far(n0, 0, US[5], own0, away0, fwd0, acc0, loss0, x0)
-    grad1, *sums = far(n1, a1, US[6], own1, away1, fwd1, acc1, loss1, x1, *sums)
-    away2, own2, *sums = hold((away2, own2, *sums))
+    grad0, *sums = far(n0, 0, US[5], own0, acc0, loss0, x0, received=(away0, fwd0))
+    grad1, *sums = far(n1, a1, US[6], own1, acc1, loss1, x1, *sums, received=(away1, fwd1))
+    away2, acc2, *sums = hold((away2, acc2, *sums))
     fwd2 = beside(away2)
-    acc2, loss2 = near(n2, a2, US[7], own2, sib2)
-    grad2, packed = far(n2, a2, US[8], own2, away2, fwd2, acc2, loss2, x2, *sums, last=True)
+    acc2, loss2 = direct(n2, a2, US[9], own2, away2, acc2, loss2)
+    grad2, packed = far(n2, a2, US[8], own2, acc2, loss2, x2, *sums, received=(fwd2,), last=True)
     grads = [grad0, grad1, grad2]
 
     parts = lax.all_to_all(packed, ("member", "point"), split_axis=0, concat_axis=0, tiled=True)

time: 57.1 us -> 56.1 us (0.982)
  starting transfers between devices: 23.9 us -> 22.9 us
    ppermute x6, starting transfers between devices: 6.9 us -> 5.92 us  [shards(): beside = lambda a: lax.ppermute(a, 'member', core_swap)]
    pallas_call x0 -> x1, Pallas kernels: none -> 0.58 us  [direct(): pl.pallas_call(functools.partial(direct_kernel, first=first, members=memb...]
  transfers between devices with their start and end apart: 10 -> 10, of which waited for: 3 -> 3; matrix products, arithmetic and copies ran while one was open for 0% -> 0% of each run, Pallas kernels for 27% -> 28%
where the time goes in v4:
time: 56.1 us; the launch traced here: 55.9 us
  starting transfers between devices  22.9 us (41%)
  Pallas kernels  20.6 us (37%)
  waiting for transfers between devices  11.4 us (20%)
  between operations  0.8 us (1%)
    all_to_all x1, starting transfers between devices, shards(): lax.all_to_all(packed, ('member', 'point'), split_axis=0, concat_axis=0,...  12.8 us
    all_to_all x1, waiting for transfers between devices, shards(): lax.all_to_all(packed, ('member', 'point'), split_axis=0, concat_axis=0,...  10.4 us
    pallas_call x3, Pallas kernels, forecast(): pl.pallas_call(functools.partial(forecast_kernel, first=first), in_specs=...  6.84 us
    ppermute x6, starting transfers between devices, shards(): beside = lambda a: lax.ppermute(a, 'member', core_swap)  5.92 us
    pallas_call x3, Pallas kernels, far(): pl.pallas_call(functools.partial(far_kernel, first=first, before=len(sums...  5.05 us
    pallas_call x1, Pallas kernels, shards(): pl.pallas_call(slope_kernel, grid=(points // LANES,), in_specs=[tile((LAN...  4.79 us
    ppermute x3, starting transfers between devices, shards(): across = lambda a: lax.ppermute(a, 'member', chip_swap)  4.24 us
    pallas_call x3, Pallas kernels, near(): pl.pallas_call(functools.partial(near_kernel, first=first, members=member...  2.65 us
  transfers between devices with their start and end apart: 10, of which 3 were waited for; matrix products, arithmetic and copies ran while one was open for 0% of the time, Pallas kernels for 28%

profile of v4, /device:TPU:1, one launch (start us, length us, event | category | flops | bytes accessed | tf_op | source)
XLA Modules:
  0.0 55.9 jit_solution(7194738834206193997)
XLA Ops:
  0.6 2.3 %forecast.3 = (bf16[2,4,128,1024]{3,2,1,0:T(8,128)(2,1)S(1)}, f32[2,104,512]{2,1,0:T(8,128)S(1)}, bf16[2,400,128]{2,1,0:T(8,128)(2,1)S(1)}) custom-call(bf16[4,768,1024]{2,1,0:T(8,128)(2,1)} %x_hbm.5, bf16[100,1024]{1,0:T(8,128)(2,1)} %bitcast.8), custom_call_target="tpu_custom_call" | custom-call | flops 10000000 | bytes 35000 | tf_op jit(solution)/shard_map/forecast/pallas_call | solution.py:322
  2.9 3.3 %collective-permute-start.1 = (bf16[2,400,128]{2,1,0:T(8,128)(2,1)S(1)}, bf16[2,400,128]{2,1,0:T(8,128)(2,1)S(1)}, u32[]{:S(2)}, u32[]{:S(2)}) collective-permute-start(bf16[2,400,128]{2,1,0:T(8,128)(2,1)S(1)} %get-tuple-element.49), channel_id=1, source_target_pairs={{0,64},{64,0},{128,192},{192,128},{1,65},{65,1},{129,193},{193,129... | collective-permute-start | bytes 614408 | tf_op jit(solution)/shard_map/ppermute | solution.py:396
  6.2 1.2 %collective-permute-start = (bf16[2,400,128]{2,1,0:T(8,128)(2,1)S(1)}, bf16[2,400,128]{2,1,0:T(8,128)(2,1)S(1)}, u32[]{:S(2)}, u32[]{:S(2)}) collective-permute-start(bf16[2,400,128]{2,1,0:T(8,128)(2,1)S(1)} %get-tuple-element.49), channel_id=1, source_target_pairs={{0,128},{64,192},{128,0},{192,64},{1,129},{65,193},{129,1},{193,65... | collective-permute-start | bytes 614408 | tf_op jit(solution)/shard_map/ppermute | solution.py:395
  7.4 2.3 %forecast.5 = (bf16[2,4,128,1024]{3,2,1,0:T(8,128)(2,1)S(1)}, f32[2,104,512]{2,1,0:T(8,128)S(1)}, bf16[2,400,128]{2,1,0:T(8,128)(2,1)S(1)}) custom-call(bf16[4,768,1024]{2,1,0:T(8,128)(2,1)} %x_hbm.5, bf16[100,1024]{1,0:T(8,128)(2,1)} %bitcast.9), custom_call_target="tpu_custom_call" | custom-call | flops 10000000 | bytes 35000 | tf_op jit(solution)/shard_map/forecast/pallas_call | solution.py:322
  9.7 0.0 copy-start.4
  9.7 0.0 copy-start.1
  9.8 0.0 copy-start.2
  9.8 0.0 copy-start.3
  9.8 0.4 collective-permute-start.4
  10.2 1.8 %collective-permute-start.3 = (bf16[2,400,128]{2,1,0:T(8,128)(2,1)S(1)}, bf16[2,400,128]{2,1,0:T(8,128)(2,1)S(1)}, u32[]{:S(2)}, u32[]{:S(2)}) collective-permute-start(bf16[2,400,128]{2,1,0:T(8,128)(2,1)S(1)} %get-tuple-element.58), channel_id=1, source_target_pairs={{0,128},{64,192},{128,0},{192,64},{1,129},{65,193},{129,1},{193,65... | collective-permute-start | bytes 614408 | tf_op jit(solution)/shard_map/ppermute | solution.py:395
  12.0 2.3 %forecast.4 = (bf16[2,4,128,1024]{3,2,1,0:T(8,128)(2,1)S(1)}, f32[2,104,512]{2,1,0:T(8,128)S(1)}, bf16[2,400,128]{2,1,0:T(8,128)(2,1)S(1)}) custom-call(bf16[4,768,1024]{2,1,0:T(8,128)(2,1)} %x_hbm.5, bf16[100,1024]{1,0:T(8,128)(2,1)} %bitcast.10), custom_call_target="tpu_custom_call" | custom-call | flops 10000000 | bytes 35000 | tf_op jit(solution)/shard_map/forecast/pallas_call | solution.py:322
  14.3 0.5 collective-permute-start.5
  14.9 1.3 %collective-permute-start.2 = (bf16[2,400,128]{2,1,0:T(8,128)(2,1)S(1)}, bf16[2,400,128]{2,1,0:T(8,128)(2,1)S(1)}, u32[]{:S(2)}, u32[]{:S(2)}) collective-permute-start(bf16[2,400,128]{2,1,0:T(8,128)(2,1)S(1)} %get-tuple-element.57), channel_id=1, source_target_pairs={{0,128},{64,192},{128,0},{192,64},{1,129},{65,193},{129,1},{193,65... | collective-permute-start | bytes 614408 | tf_op jit(solution)/shard_map/ppermute | solution.py:395
  16.1 0.9 %near.3 = (f32[2,104,512]{2,1,0:T(8,128)S(1)}, f32[8,128]{1,0:T(8,128)S(1)}) custom-call(f32[2,104,512]{2,1,0:T(8,128)S(1)} %get-tuple-element.52.own_ref.refs_0_, bf16[2,400,128]{2,1,0:T(8,128)(2,1)S(1)} %collective-permute-done.1.sib_ref, f32[100,768]{1,0:T(8,128)S(1)} %bitcast.12, f32[1,768]{1,0:T(1,128)S(1)} %broadcast_in_dim.9.area_ref.refs_2_, ...), custom_call_target="tpu_custom_call" | custom-call | flops 10000000 | bytes 35000 | tf_op jit(solution)/shard_map/near/pallas_call | solution.py:342
  17.0 0.0 collective-permute-done.refs_6_
  17.0 0.4 collective-permute-start.6
  17.5 0.9 %near.4 = (f32[2,104,512]{2,1,0:T(8,128)S(1)}, f32[8,128]{1,0:T(8,128)S(1)}) custom-call(f32[2,104,512]{2,1,0:T(8,128)S(1)} %get-tuple-element.59.own_ref.refs_0_, bf16[2,400,128]{2,1,0:T(8,128)(2,1)S(1)} %collective-permute-done.4.sib_ref, f32[100,768]{1,0:T(8,128)S(1)} %bitcast.13, f32[1,768]{1,0:T(1,128)S(1)} %broadcast_in_dim.9.area_ref.refs_2_, ...), custom_call_target="tpu_custom_call" | custom-call | flops 8000000000 | bytes 28000000 | tf_op jit(solution)/shard_map/near/pallas_call | solution.py:342
  18.3 0.0 collective-permute-done.5.sib_ref
  18.4 0.9 %near.5 = (f32[2,104,512]{2,1,0:T(8,128)S(1)}, f32[8,128]{1,0:T(8,128)S(1)}) custom-call(f32[2,104,512]{2,1,0:T(8,128)S(1)} %get-tuple-element.56.own_ref.refs_0_, bf16[2,400,128]{2,1,0:T(8,128)(2,1)S(1)} %collective-permute-done.5.sib_ref, f32[100,768]{1,0:T(8,128)S(1)} %bitcast.14, f32[1,768]{1,0:T(1,128)S(1)} %broadcast_in_dim.9.area_ref.refs_2_, ...), custom_call_target="tpu_custom_call" | custom-call | flops 10000000 | bytes 35000 | tf_op jit(solution)/shard_map/near/pallas_call | solution.py:342
  19.3 0.4 collective-permute-start.7
  19.7 1.6 %far.3 = (bf16[2,128,512]{2,1,0:T(8,128)(2,1)S(1)}, f32[128,1024]{1,0:T(8,128)S(1)}, f32[104,128]{1,0:T(8,128)S(1)}, f32[8,128]{1,0:T(8,128)S(1)}) custom-call(f32[2,104,512]{2,1,0:T(8,128)S(1)} %get-tuple-element.52.own_ref.refs_0_, f32[2,104,512]{2,1,0:T(8,128)S(1)} %get-tuple-element.67.refs_1_, f32[1,768]{1,0:T(1,128)S(1)} %broadcast_in_dim.9.area_ref.refs_2_, ...), custom_call_target="tpu_custom_call" | custom-call | flops 8000000000 | bytes 28000000 | tf_op jit(solution)/shard_map/far/pallas_call | solution.py:377
  21.3 1.6 %far.4 = (bf16[2,128,512]{2,1,0:T(8,128)(2,1)S(1)}, f32[128,1024]{1,0:T(8,128)S(1)}, f32[104,128]{1,0:T(8,128)S(1)}, f32[8,128]{1,0:T(8,128)S(1)}) custom-call(f32[2,104,512]{2,1,0:T(8,128)S(1)} %get-tuple-element.59.own_ref.refs_0_, f32[2,104,512]{2,1,0:T(8,128)S(1)} %get-tuple-element.64.refs_1_, f32[1,768]{1,0:T(1,128)S(1)} %broadcast_in_dim.9.area_ref.refs_2_, ...), custom_call_target="tpu_custom_call" | custom-call | flops 10000000 | bytes 35000 | tf_op jit(solution)/shard_map/far/pallas_call | solution.py:377
  22.8 0.5 collective-permute-done.2.far_ref
  23.3 0.7 %collective-permute-start.8 = (bf16[2,400,128]{2,1,0:T(8,128)(2,1)S(1)}, bf16[2,400,128]{2,1,0:T(8,128)(2,1)S(1)}, u32[]{:S(2)}, u32[]{:S(2)}) collective-permute-start(bf16[2,400,128]{2,1,0:T(8,128)(2,1)S(1)} %collective-permute-done.2.far_ref), channel_id=1, source_target_pairs={{0,64},{64,0},{128,192},{192,128},{1,65},{65,1},{129,193},{193,129... | collective-permute-start | bytes 614408 | tf_op jit(solution)/shard_map/ppermute | solution.py:396
  24.0 0.6 %direct.1 = (f32[2,104,512]{2,1,0:T(8,128)S(1)}, f32[8,128]{1,0:T(8,128)S(1)}) custom-call(f32[2,104,512]{2,1,0:T(8,128)S(1)} %get-tuple-element.56.own_ref.refs_0_, bf16[2,400,128]{2,1,0:T(8,128)(2,1)S(1)} %collective-permute-done.2.far_ref, f32[2,104,512]{2,1,0:T(8,128)S(1)} %get-tuple-element.79.acc_ref, f32[8,128]{1,0:T(8,128)S(1)} %get-tuple-element.80.loss_in, ...), custom_call_target="tpu_custom_call" | custom-call | flops 8000000000 | bytes 28000000 | tf_op jit(solution)/shard_map/direct/pallas_call | solution.py:358
  24.6 0.5 collective-permute-done.8.refs_9_
  25.1 1.9 %far.5 = (bf16[2,128,512]{2,1,0:T(8,128)(2,1)S(1)}, bf16[1024,128]{1,0:T(8,128)(2,1)}) custom-call(f32[2,104,512]{2,1,0:T(8,128)S(1)} %get-tuple-element.56.own_ref.refs_0_, f32[2,104,512]{2,1,0:T(8,128)S(1)} %get-tuple-element.81.refs_1_, f32[1,768]{1,0:T(1,128)S(1)} %broadcast_in_dim.9.area_ref.refs_2_, f32[1,100]{1,0:T(1,128)S(1)} %bitcast.22, ...), custom_call_target="tpu_custom_call" | custom-call | flops 10000000 | bytes 35000 | tf_op jit(solution)/shard_map/far/pallas_call | solution.py:377
  27.0 12.8 %all-to-all-start = ((bf16[256,4,128]{2,1,0:T(4,128)(2,1)}), bf16[256,4,128]{2,1,0:T(4,128)(2,1)S(1)}, u32[]{:S(2)}, u32[]{:S(2)}) async-start(bf16[256,4,128]{2,1,0:T(4,128)(2,1)} %bitcast.4), calls=%async_computation | async-start | bytes 524288 | tf_op jit(solution)/shard_map/all_to_all | solution.py:423
  39.8 0.1 pad_maximum_fusion.grad_ref
  39.9 4.8 %slope.1 = bf16[4,768,1024]{2,1,0:T(8,128)(2,1)} custom-call(bf16[6,128,512]{2,1,0:T(8,128)(2,1)S(1)} %pad_maximum_fusion.grad_ref, bf16[100,1024]{1,0:T(8,128)(2,1)S(1)} %bitcast.11), custom_call_target="tpu_custom_call" | custom-call | flops 5000000000 | bytes 17500000 | tf_op jit(solution)/shard_map/slope/pallas_call | solution.py:426
  44.7 10.4 %all-to-all-done = bf16[256,4,128]{2,1,0:T(4,128)(2,1)S(1)} async-done(((bf16[256,4,128]{2,1,0:T(4,128)(2,1)}), bf16[256,4,128]{2,1,0:T(4,128)(2,1)S(1)}, u32[]{:S(2)}, u32[]{:S(2)}) %all-to-all-start) | async-done | bytes 262176 | tf_op jit(solution)/shard_map/all_to_all | solution.py:423
  55.2 0.7 %finish.1 = (f32[4,100]{1,0:T(4,128)}, f32[1,100]{1,0:T(1,128)}, f32[1,1]{1,0:T(1,128)}) custom-call(bf16[1024,128]{1,0:T(8,128)(2,1)S(1)} %bitcast.15), custom_call_target="tpu_custom_call" | custom-call | tf_op jit(solution)/shard_map/finish/pallas_call | solution.py:438
  (12 shorter events, 0.0 us)
Async XLA Ops:
  2.9 11.9 %collective-permute-start.1 = (bf16[2,400,128]{2,1,0:T(8,128)(2,1)S(1)}, bf16[2,400,128]{2,1,0:T(8,128)(2,1)S(1)}, u32[]{:S(2)}, u32[]{:S(2)}) collective-permute-start(bf16[2,400,128]{2,1,0:T(8,128)(2,1)S(1)} %get-tuple-element.49), channel_id=1, source_target_pairs={{0,64},{64,0},{128,192},{192,128},{1,65},{65,1},{129,193},{193,129... | collective-permute-start | bytes 614408 | tf_op jit(solution)/shard_map/ppermute | solution.py:396
  6.2 10.8 %collective-permute-start = (bf16[2,400,128]{2,1,0:T(8,128)(2,1)S(1)}, bf16[2,400,128]{2,1,0:T(8,128)(2,1)S(1)}, u32[]{:S(2)}, u32[]{:S(2)}) collective-permute-start(bf16[2,400,128]{2,1,0:T(8,128)(2,1)S(1)} %get-tuple-element.49), channel_id=1, source_target_pairs={{0,128},{64,192},{128,0},{192,64},{1,129},{65,193},{129,1},{193,65... | collective-permute-start | bytes 614408 | tf_op jit(solution)/shard_map/ppermute | solution.py:395
  9.7 5.1 %copy-start.4 = (f32[768]{0:T(1024)S(1)}, f32[768]{0:T(1024)}, u32[]{:S(2)}) copy-start(f32[768]{0:T(1024)} %param.10) | copy-start | bytes 9220
  9.7 6.4 %copy-start.1 = (f32[768,100]{0,1:T(8,128)S(1)}, f32[768,100]{0,1:T(8,128)}, u32[]{:S(2)}) copy-start(f32[768,100]{0,1:T(8,128)} %param.9) | copy-start | bytes 921604
  9.8 6.4 %copy-start.2 = (f32[100]{0:T(128)S(1)}, f32[100]{0:T(128)}, u32[]{:S(2)}) copy-start(f32[100]{0:T(128)} %param.11) | copy-start | bytes 1204
  9.8 6.3 %copy-start.3 = (f32[100]{0:T(128)S(1)}, f32[100]{0:T(128)}, u32[]{:S(2)}) copy-start(f32[100]{0:T(128)} %param.8) | copy-start | bytes 1204
  9.8 7.7 %collective-permute-start.4 = (bf16[2,400,128]{2,1,0:T(8,128)(2,1)S(1)}, bf16[2,400,128]{2,1,0:T(8,128)(2,1)S(1)}, u32[]{:S(2)}, u32[]{:S(2)}) collective-permute-start(bf16[2,400,128]{2,1,0:T(8,128)(2,1)S(1)} %get-tuple-element.58), channel_id=1, source_target_pairs={{0,64},{64,0},{128,192},{192,128},{1,65},{65,1},{129,193},{193,129... | collective-permute-start | bytes 614408 | tf_op jit(solution)/shard_map/ppermute | solution.py:396
  10.2 9.0 %collective-permute-start.3 = (bf16[2,400,128]{2,1,0:T(8,128)(2,1)S(1)}, bf16[2,400,128]{2,1,0:T(8,128)(2,1)S(1)}, u32[]{:S(2)}, u32[]{:S(2)}) collective-permute-start(bf16[2,400,128]{2,1,0:T(8,128)(2,1)S(1)} %get-tuple-element.58), channel_id=1, source_target_pairs={{0,128},{64,192},{128,0},{192,64},{1,129},{65,193},{129,1},{193,65... | collective-permute-start | bytes 614408 | tf_op jit(solution)/shard_map/ppermute | solution.py:395
  14.3 4.0 %collective-permute-start.5 = (bf16[2,400,128]{2,1,0:T(8,128)(2,1)S(1)}, bf16[2,400,128]{2,1,0:T(8,128)(2,1)S(1)}, u32[]{:S(2)}, u32[]{:S(2)}) collective-permute-start(bf16[2,400,128]{2,1,0:T(8,128)(2,1)S(1)} %get-tuple-element.57), channel_id=1, source_target_pairs={{0,64},{64,0},{128,192},{192,128},{1,65},{65,1},{129,193},{193,129... | collective-permute-start | bytes 614408 | tf_op jit(solution)/shard_map/ppermute | solution.py:396
  14.9 8.4 %collective-permute-start.2 = (bf16[2,400,128]{2,1,0:T(8,128)(2,1)S(1)}, bf16[2,400,128]{2,1,0:T(8,128)(2,1)S(1)}, u32[]{:S(2)}, u32[]{:S(2)}) collective-permute-start(bf16[2,400,128]{2,1,0:T(8,128)(2,1)S(1)} %get-tuple-element.57), channel_id=1, source_target_pairs={{0,128},{64,192},{128,0},{192,64},{1,129},{65,193},{129,1},{193,65... | collective-permute-start | bytes 614408 | tf_op jit(solution)/shard_map/ppermute | solution.py:395
  17.0 2.7 %collective-permute-start.6 = (bf16[2,400,128]{2,1,0:T(8,128)(2,1)S(1)}, bf16[2,400,128]{2,1,0:T(8,128)(2,1)S(1)}, u32[]{:S(2)}, u32[]{:S(2)}) collective-permute-start(bf16[2,400,128]{2,1,0:T(8,128)(2,1)S(1)} %collective-permute-done.refs_6_), channel_id=1, source_target_pairs={{0,64},{64,0},{128,192},{192,128},{1,65},{65,1},{129,193},{193,129... | collective-permute-start | bytes 614408 | tf_op jit(solution)/shard_map/ppermute | solution.py:396
  19.3 2.0 %collective-permute-start.7 = (bf16[2,400,128]{2,1,0:T(8,128)(2,1)S(1)}, bf16[2,400,128]{2,1,0:T(8,128)(2,1)S(1)}, u32[]{:S(2)}, u32[]{:S(2)}) collective-permute-start(bf16[2,400,128]{2,1,0:T(8,128)(2,1)S(1)} %collective-permute-done.3.refs_9_), channel_id=1, source_target_pairs={{0,64},{64,0},{128,192},{192,128},{1,65},{65,1},{129,193},{193,129... | collective-permute-start | bytes 614408 | tf_op jit(solution)/shard_map/ppermute | solution.py:396
  23.3 1.8 %collective-permute-start.8 = (bf16[2,400,128]{2,1,0:T(8,128)(2,1)S(1)}, bf16[2,400,128]{2,1,0:T(8,128)(2,1)S(1)}, u32[]{:S(2)}, u32[]{:S(2)}) collective-permute-start(bf16[2,400,128]{2,1,0:T(8,128)(2,1)S(1)} %collective-permute-done.2.far_ref), channel_id=1, source_target_pairs={{0,64},{64,0},{128,192},{192,128},{1,65},{65,1},{129,193},{193,129... | collective-permute-start | bytes 614408 | tf_op jit(solution)/shard_map/ppermute | solution.py:396
  25.1 14.8 %copy-start = (bf16[1024,100]{0,1:T(8,128)(2,1)S(1)}, bf16[1024,100]{0,1:T(8,128)(2,1)}, u32[]{:S(2)}) copy-start(bf16[1024,100]{0,1:T(8,128)(2,1)} %param.7) | copy-start | bytes 614404
  27.0 28.1 %all-to-all-start = ((bf16[256,4,128]{2,1,0:T(4,128)(2,1)}), bf16[256,4,128]{2,1,0:T(4,128)(2,1)S(1)}, u32[]{:S(2)}, u32[]{:S(2)}) async-start(bf16[256,4,128]{2,1,0:T(4,128)(2,1)} %bitcast.4), calls=%async_computation | async-start | bytes 524288 | tf_op jit(solution)/shard_map/all_to_all | solution.py:423

commit v5 on v4

--- a/solution.py
+++ b/solution.py
@@ -90,7 +90,7 @@
     return d * r, t * r
 
 
-def near_kernel(own_ref, sib_ref, truth_ref, area_ref, shift_ref, coef_ref, acc_ref, loss_ref, goal, rpad, coefs, *, first, members, total):
+def near_kernel(own_ref, sib_ref, truth_ref, area_ref, shift_ref, coef_ref, acc_ref, loss_ref, coefs, goal, rpad, *, first, members, total):
     tiles, rows, _ = own_ref.shape
     fields = truth_ref.shape[0]
     c1 = (1.0 - (1.0 - ALPHA) / total) / (total - 1)
@@ -144,12 +144,10 @@
     lax.fori_loop(0, tiles, step, 0)
 
 
-def direct_kernel(own_ref, far_ref, acc_ref, loss_in, area_ref, coef_ref, out_ref, loss_ref, rpad, coefs, *, first, members, total):
+def direct_kernel(own_ref, far_ref, acc_ref, loss_in, area_ref, coefs, out_ref, loss_ref, *, first, members, total, fields):
     tiles, rows, _ = own_ref.shape
-    fields = coef_ref.shape[1]
     c1 = (1.0 - (1.0 - ALPHA) / total) / (total - 1)
     c2 = (1.0 - (1.0 - ALPHA) / total) / (2.0 * total * (total - 1))
-    coefs[...] = column(pad_row(coef_ref, rpad, fields), rows)
     loss_ref[...] = loss_in[...]
 
     def step(t, carry):
@@ -207,21 +205,20 @@
 
 
 def far_kernel(*refs, first, before, received, last, members, total, fields):
-    own_ref, acc_ref, area_ref, coef_ref, near_loss, x = refs[:6]
+    own_ref, acc_ref, area_ref, coefs, near_loss, x = refs[:6]
     earlier, refs = refs[6 : 6 + before], refs[6 + before :]
     sources, refs = refs[:received], refs[received:]
     if last:
-        grad_ref, out_ref, rpad, coefs, grads, bias_ref, loss_ref, padded = refs
+        grad_ref, out_ref, grads, bias_ref, loss_ref, padded = refs
     else:
-        grad_ref, dw_ref, bias_ref, loss_ref, rpad, coefs, grads = refs
+        grad_ref, dw_ref, bias_ref, loss_ref, grads = refs
     tiles, rows, _ = own_ref.shape
     width = x.shape[3]
     span_all = members * LANES
     c1 = (1.0 - (1.0 - ALPHA) / total) / (total - 1)
     c2 = (1.0 - (1.0 - ALPHA) / total) / (2.0 * total * (total - 1))
 
-    coefs[...] = column(pad_row(coef_ref, rpad, fields), rows)
-    grads[...] = jnp.zeros_like(grads)
+    grads[:, rows:, :] = jnp.zeros((tiles, LANES - rows, span_all), F32)
     if before:
         bias_ref[...] = earlier[1][...]
         loss_ref[...] = earlier[2][...] + near_loss[...]
@@ -342,31 +339,28 @@
         return pl.pallas_call(
             functools.partial(near_kernel, first=first, members=members, total=total),
             in_specs=[vmem] * 6,
-            out_specs=[vmem] * 2,
-            out_shape=[shape((n, rows, span), F32), shape((8, LANES), F32)],
-            scratch_shapes=[
-                pltpu.VMEM((n, rows, LANES), F32),
-                pltpu.VMEM((1, LANES), F32),
-                pltpu.VMEM((rows, LANES), F32),
-            ],
+            out_specs=[vmem] * (2 if first else 3),
+            out_shape=[shape((n, rows, span), F32), shape((8, LANES), F32)]
+            + ([] if first else [shape((rows, LANES), F32)]),
+            scratch_shapes=([pltpu.VMEM((rows, LANES), F32)] if first else [])
+            + [pltpu.VMEM((n, rows, LANES), F32), pltpu.VMEM((1, LANES), F32)],
             compiler_params=params(),
             cost_estimate=cost(us),
             name="near",
         )(own, sib, truth, area, shift, coef)
 
-    def direct(n, first, us, own, away, acc, loss):
+    def direct(n, first, us, coefs, own, away, acc, loss):
         return pl.pallas_call(
-            functools.partial(direct_kernel, first=first, members=members, total=total),
+            functools.partial(direct_kernel, first=first, members=members, total=total, fields=fields),
             in_specs=[vmem] * 6,
             out_specs=[vmem] * 2,
             out_shape=[shape((n, rows, span), F32), shape((8, LANES), F32)],
-            scratch_shapes=[pltpu.VMEM((1, LANES), F32), pltpu.VMEM((rows, LANES), F32)],
             compiler_params=params(),
             cost_estimate=cost(us),
             name="direct",
-        )(own, away, acc, loss, area, coef)
-
-    def far(n, first, us, own, acc, loss, x, *sums, received, last=False):
+        )(own, away, acc, loss, area, coefs)
+
+    def far(n, first, us, coefs, own, acc, loss, x, *sums, received, last=False):
         sums_shapes = [((rows, LANES), F32), ((8, LANES), F32)]
         if last:
             outs = [shape((width, LANES), BF16)]
@@ -381,16 +375,11 @@
             in_specs=[vmem] * (6 + len(sums) + len(received)),
             out_specs=[vmem] * (1 + len(outs)),
             out_shape=[shape((n, LANES, span), BF16)] + outs,
-            scratch_shapes=[
-                pltpu.VMEM((1, LANES), F32),
-                pltpu.VMEM((rows, LANES), F32),
-                pltpu.VMEM((n, LANES, span), F32),
-            ]
-            + extra,
+            scratch_shapes=[pltpu.VMEM((n, LANES, span), F32)] + extra,
             compiler_params=params(),
             cost_estimate=cost(us),
             name="far",
-        )(own, acc, area, coef, loss, x, *sums, *received)
+        )(own, acc, area, coefs, loss, x, *sums, *received)
 
     across = lambda a: lax.ppermute(a, "member", chip_swap)
     beside = lambda a: lax.ppermute(a, "member", core_swap)
@@ -405,19 +394,19 @@
     own0, out2 = hold((own0, out2))
     away2 = across(out2)
     sib0, sib1, sib2 = beside(out0), beside(out1), beside(out2)
-    acc0, loss0 = near(n0, 0, US[3], own0, sib0)
+    acc0, loss0, coefs = near(n0, 0, US[3], own0, sib0)
     away0, acc0, own1, own2 = hold((away0, acc0, own1, own2))
     fwd0 = beside(away0)
     acc1, loss1 = near(n1, a1, US[4], own1, sib1)
     acc2, loss2 = near(n2, a2, US[7], own2, sib2)
     away1, acc1, acc0, acc2 = hold((away1, acc1, acc0, acc2))
     fwd1 = beside(away1)
-    grad0, *sums = far(n0, 0, US[5], own0, acc0, loss0, x0, received=(away0, fwd0))
-    grad1, *sums = far(n1, a1, US[6], own1, acc1, loss1, x1, *sums, received=(away1, fwd1))
+    grad0, *sums = far(n0, 0, US[5], coefs, own0, acc0, loss0, x0, received=(away0, fwd0))
+    grad1, *sums = far(n1, a1, US[6], coefs, own1, acc1, loss1, x1, *sums, received=(away1, fwd1))
     away2, acc2, *sums = hold((away2, acc2, *sums))
     fwd2 = beside(away2)
-    acc2, loss2 = direct(n2, a2, US[9], own2, away2, acc2, loss2)
-    grad2, packed = far(n2, a2, US[8], own2, acc2, loss2, x2, *sums, received=(fwd2,), last=True)
+    acc2, loss2 = direct(n2, a2, US[9], coefs, own2, away2, acc2, loss2)
+    grad2, packed = far(n2, a2, US[8], coefs, own2, acc2, loss2, x2, *sums, received=(fwd2,), last=True)
     grads = [grad0, grad1, grad2]
 
     parts = lax.all_to_all(packed, ("member", "point"), split_axis=0, concat_axis=0, tiled=True)

time: 56.1 us -> 56 us (level)
  no operation moved by 1% of the time
where the time goes in v5:
time: 56 us; the launch traced here: 55.8 us
  starting transfers between devices  23 us (41%)
  Pallas kernels  20.2 us (36%)
  waiting for transfers between devices  11.8 us (21%)
  between operations  0.8 us (1%)
    all_to_all x1, starting transfers between devices, shards(): lax.all_to_all(packed, ('member', 'point'), split_axis=0, concat_axis=0,...  12.8 us
    all_to_all x1, waiting for transfers between devices, shards(): lax.all_to_all(packed, ('member', 'point'), split_axis=0, concat_axis=0,...  10.4 us
    pallas_call x3, Pallas kernels, forecast(): pl.pallas_call(functools.partial(forecast_kernel, first=first), in_specs=...  6.84 us
    ppermute x6, starting transfers between devices, shards(): beside = lambda a: lax.ppermute(a, 'member', core_swap)  5.92 us
    pallas_call x1, Pallas kernels, shards(): pl.pallas_call(slope_kernel, grid=(points // LANES,), in_specs=[tile((LAN...  4.79 us
    pallas_call x3, Pallas kernels, far(): pl.pallas_call(functools.partial(far_kernel, first=first, before=len(sums...  4.67 us
    ppermute x3, starting transfers between devices, shards(): across = lambda a: lax.ppermute(a, 'member', chip_swap)  4.24 us
    pallas_call x3, Pallas kernels, near(): pl.pallas_call(functools.partial(near_kernel, first=first, members=member...  2.64 us
  transfers between devices with their start and end apart: 10, of which 3 were waited for; matrix products, arithmetic and copies ran while one was open for 0% of the time, Pallas kernels for 28%

profile of v5, /device:TPU:1, one launch (start us, length us, event | category | flops | bytes accessed | tf_op | source)
XLA Modules:
  0.0 55.8 jit_solution(13167881670719549849)
XLA Ops:
  0.6 2.3 %forecast.3 = (bf16[2,4,128,1024]{3,2,1,0:T(8,128)(2,1)S(1)}, f32[2,104,512]{2,1,0:T(8,128)S(1)}, bf16[2,400,128]{2,1,0:T(8,128)(2,1)S(1)}) custom-call(bf16[4,768,1024]{2,1,0:T(8,128)(2,1)} %x_hbm.5, bf16[100,1024]{1,0:T(8,128)(2,1)} %bitcast.8), custom_call_target="tpu_custom_call" | custom-call | flops 10000000 | bytes 35000 | tf_op jit(solution)/shard_map/forecast/pallas_call | solution.py:319
  2.9 3.3 %collective-permute-start.1 = (bf16[2,400,128]{2,1,0:T(8,128)(2,1)S(1)}, bf16[2,400,128]{2,1,0:T(8,128)(2,1)S(1)}, u32[]{:S(2)}, u32[]{:S(2)}) collective-permute-start(bf16[2,400,128]{2,1,0:T(8,128)(2,1)S(1)} %get-tuple-element.50), channel_id=1, source_target_pairs={{0,64},{64,0},{128,192},{192,128},{1,65},{65,1},{129,193},{193,129... | collective-permute-start | bytes 614408 | tf_op jit(solution)/shard_map/ppermute | solution.py:385
  6.2 1.2 %collective-permute-start = (bf16[2,400,128]{2,1,0:T(8,128)(2,1)S(1)}, bf16[2,400,128]{2,1,0:T(8,128)(2,1)S(1)}, u32[]{:S(2)}, u32[]{:S(2)}) collective-permute-start(bf16[2,400,128]{2,1,0:T(8,128)(2,1)S(1)} %get-tuple-element.50), channel_id=1, source_target_pairs={{0,128},{64,192},{128,0},{192,64},{1,129},{65,193},{129,1},{193,65... | collective-permute-start | bytes 614408 | tf_op jit(solution)/shard_map/ppermute | solution.py:384
  7.4 2.3 %forecast.5 = (bf16[2,4,128,1024]{3,2,1,0:T(8,128)(2,1)S(1)}, f32[2,104,512]{2,1,0:T(8,128)S(1)}, bf16[2,400,128]{2,1,0:T(8,128)(2,1)S(1)}) custom-call(bf16[4,768,1024]{2,1,0:T(8,128)(2,1)} %x_hbm.5, bf16[100,1024]{1,0:T(8,128)(2,1)} %bitcast.9), custom_call_target="tpu_custom_call" | custom-call | flops 10000000 | bytes 35000 | tf_op jit(solution)/shard_map/forecast/pallas_call | solution.py:319
  9.7 0.0 copy-start.4
  9.7 0.0 copy-start.1
  9.8 0.0 copy-start.2
  9.8 0.0 copy-start.3
  9.8 0.4 collective-permute-start.4
  10.2 1.8 %collective-permute-start.3 = (bf16[2,400,128]{2,1,0:T(8,128)(2,1)S(1)}, bf16[2,400,128]{2,1,0:T(8,128)(2,1)S(1)}, u32[]{:S(2)}, u32[]{:S(2)}) collective-permute-start(bf16[2,400,128]{2,1,0:T(8,128)(2,1)S(1)} %get-tuple-element.59), channel_id=1, source_target_pairs={{0,128},{64,192},{128,0},{192,64},{1,129},{65,193},{129,1},{193,65... | collective-permute-start | bytes 614408 | tf_op jit(solution)/shard_map/ppermute | solution.py:384
  12.0 2.3 %forecast.4 = (bf16[2,4,128,1024]{3,2,1,0:T(8,128)(2,1)S(1)}, f32[2,104,512]{2,1,0:T(8,128)S(1)}, bf16[2,400,128]{2,1,0:T(8,128)(2,1)S(1)}) custom-call(bf16[4,768,1024]{2,1,0:T(8,128)(2,1)} %x_hbm.5, bf16[100,1024]{1,0:T(8,128)(2,1)} %bitcast.10), custom_call_target="tpu_custom_call" | custom-call | flops 10000000 | bytes 35000 | tf_op jit(solution)/shard_map/forecast/pallas_call | solution.py:319
  14.3 0.5 collective-permute-start.5
  14.9 1.3 %collective-permute-start.2 = (bf16[2,400,128]{2,1,0:T(8,128)(2,1)S(1)}, bf16[2,400,128]{2,1,0:T(8,128)(2,1)S(1)}, u32[]{:S(2)}, u32[]{:S(2)}) collective-permute-start(bf16[2,400,128]{2,1,0:T(8,128)(2,1)S(1)} %get-tuple-element.58), channel_id=1, source_target_pairs={{0,128},{64,192},{128,0},{192,64},{1,129},{65,193},{129,1},{193,65... | collective-permute-start | bytes 614408 | tf_op jit(solution)/shard_map/ppermute | solution.py:384
  16.1 0.9 %near.3 = (f32[2,104,512]{2,1,0:T(8,128)S(1)}, f32[8,128]{1,0:T(8,128)S(1)}, f32[104,128]{1,0:T(8,128)S(1)}) custom-call(f32[2,104,512]{2,1,0:T(8,128)S(1)} %get-tuple-element.53.own_ref.refs_0_, bf16[2,400,128]{2,1,0:T(8,128)(2,1)S(1)} %collective-permute-done.1.sib_ref, f32[100,768]{1,0:T(8,128)S(1)} %bitcast.12, ...), custom_call_target="tpu_custom_call" | custom-call | flops 10000000 | bytes 35000 | tf_op jit(solution)/shard_map/near/pallas_call | solution.py:339
  17.0 0.0 collective-permute-done.refs_6_
  17.0 0.4 collective-permute-start.6
  17.5 0.0 collective-permute-done.4.sib_ref
  17.5 0.9 %near.4 = (f32[2,104,512]{2,1,0:T(8,128)S(1)}, f32[8,128]{1,0:T(8,128)S(1)}) custom-call(f32[2,104,512]{2,1,0:T(8,128)S(1)} %get-tuple-element.60.own_ref.refs_0_, bf16[2,400,128]{2,1,0:T(8,128)(2,1)S(1)} %collective-permute-done.4.sib_ref, f32[100,768]{1,0:T(8,128)S(1)} %bitcast.13, f32[1,768]{1,0:T(1,128)S(1)} %broadcast_in_dim.9.area_ref.refs_2_, ...), custom_call_target="tpu_custom_call" | custom-call | flops 8000000000 | bytes 28000000 | tf_op jit(solution)/shard_map/near/pallas_call | solution.py:339
  18.4 0.9 %near.5 = (f32[2,104,512]{2,1,0:T(8,128)S(1)}, f32[8,128]{1,0:T(8,128)S(1)}) custom-call(f32[2,104,512]{2,1,0:T(8,128)S(1)} %get-tuple-element.57.own_ref.refs_0_, bf16[2,400,128]{2,1,0:T(8,128)(2,1)S(1)} %collective-permute-done.5.sib_ref, f32[100,768]{1,0:T(8,128)S(1)} %bitcast.14, f32[1,768]{1,0:T(1,128)S(1)} %broadcast_in_dim.9.area_ref.refs_2_, ...), custom_call_target="tpu_custom_call" | custom-call | flops 10000000 | bytes 35000 | tf_op jit(solution)/shard_map/near/pallas_call | solution.py:339
  19.3 0.4 collective-permute-start.7
  19.7 1.4 %far.3 = (bf16[2,128,512]{2,1,0:T(8,128)(2,1)S(1)}, f32[128,1024]{1,0:T(8,128)S(1)}, f32[104,128]{1,0:T(8,128)S(1)}, f32[8,128]{1,0:T(8,128)S(1)}) custom-call(f32[2,104,512]{2,1,0:T(8,128)S(1)} %get-tuple-element.53.own_ref.refs_0_, f32[2,104,512]{2,1,0:T(8,128)S(1)} %get-tuple-element.69.refs_1_, f32[1,768]{1,0:T(1,128)S(1)} %broadcast_in_dim.9.area_ref.refs_2_, ...), custom_call_target="tpu_custom_call" | custom-call | flops 8000000000 | bytes 28000000 | tf_op jit(solution)/shard_map/far/pallas_call | solution.py:371
  21.1 1.4 %far.4 = (bf16[2,128,512]{2,1,0:T(8,128)(2,1)S(1)}, f32[128,1024]{1,0:T(8,128)S(1)}, f32[104,128]{1,0:T(8,128)S(1)}, f32[8,128]{1,0:T(8,128)S(1)}) custom-call(f32[2,104,512]{2,1,0:T(8,128)S(1)} %get-tuple-element.60.own_ref.refs_0_, f32[2,104,512]{2,1,0:T(8,128)S(1)} %get-tuple-element.65.refs_1_, f32[1,768]{1,0:T(1,128)S(1)} %broadcast_in_dim.9.area_ref.refs_2_, ...), custom_call_target="tpu_custom_call" | custom-call | flops 10000000 | bytes 35000 | tf_op jit(solution)/shard_map/far/pallas_call | solution.py:371
  22.6 0.7 %collective-permute-done.2.far_ref = bf16[2,400,128]{2,1,0:T(8,128)(2,1)S(1)} collective-permute-done((bf16[2,400,128]{2,1,0:T(8,128)(2,1)S(1)}, bf16[2,400,128]{2,1,0:T(8,128)(2,1)S(1)}, u32[]{:S(2)}, u32[]{:S(2)}) %collective-permute-start.2) | collective-permute-done | bytes 204832 | tf_op jit(solution)/shard_map/ppermute | solution.py:384
  23.3 0.7 %collective-permute-start.8 = (bf16[2,400,128]{2,1,0:T(8,128)(2,1)S(1)}, bf16[2,400,128]{2,1,0:T(8,128)(2,1)S(1)}, u32[]{:S(2)}, u32[]{:S(2)}) collective-permute-start(bf16[2,400,128]{2,1,0:T(8,128)(2,1)S(1)} %collective-permute-done.2.far_ref), channel_id=1, source_target_pairs={{0,64},{64,0},{128,192},{192,128},{1,65},{65,1},{129,193},{193,129... | collective-permute-start | bytes 614408 | tf_op jit(solution)/shard_map/ppermute | solution.py:385
  24.0 0.5 direct.1
  24.5 0.6 %collective-permute-done.8.refs_9_ = bf16[2,400,128]{2,1,0:T(8,128)(2,1)S(1)} collective-permute-done((bf16[2,400,128]{2,1,0:T(8,128)(2,1)S(1)}, bf16[2,400,128]{2,1,0:T(8,128)(2,1)S(1)}, u32[]{:S(2)}, u32[]{:S(2)}) %collective-permute-start.8) | collective-permute-done | bytes 204832 | tf_op jit(solution)/shard_map/ppermute | solution.py:385
  25.1 1.8 %far.5 = (bf16[2,128,512]{2,1,0:T(8,128)(2,1)S(1)}, bf16[1024,128]{1,0:T(8,128)(2,1)}) custom-call(f32[2,104,512]{2,1,0:T(8,128)S(1)} %get-tuple-element.57.own_ref.refs_0_, f32[2,104,512]{2,1,0:T(8,128)S(1)} %get-tuple-element.83.refs_1_, f32[1,768]{1,0:T(1,128)S(1)} %broadcast_in_dim.9.area_ref.refs_2_, f32[104,128]{1,0:T(8,128)S(1)} %get-tuple-element.66.refs_3_.coefs, ...), custom_call_target="tpu_custom_call" | custom-call | flops 10000000 | bytes 35000 | tf_op jit(solution)/shard_map/far/pallas_call | solution.py:371
  26.9 12.8 %all-to-all-start = ((bf16[256,4,128]{2,1,0:T(4,128)(2,1)}), bf16[256,4,128]{2,1,0:T(4,128)(2,1)S(1)}, u32[]{:S(2)}, u32[]{:S(2)}) async-start(bf16[256,4,128]{2,1,0:T(4,128)(2,1)} %bitcast.4), calls=%async_computation | async-start | bytes 524288 | tf_op jit(solution)/shard_map/all_to_all | solution.py:412
  39.7 0.1 pad_maximum_fusion.grad_ref
  39.8 4.8 %slope.1 = bf16[4,768,1024]{2,1,0:T(8,128)(2,1)} custom-call(bf16[6,128,512]{2,1,0:T(8,128)(2,1)S(1)} %pad_maximum_fusion.grad_ref, bf16[100,1024]{1,0:T(8,128)(2,1)S(1)} %bitcast.11), custom_call_target="tpu_custom_call" | custom-call | flops 5000000000 | bytes 17500000 | tf_op jit(solution)/shard_map/slope/pallas_call | solution.py:415
  44.6 10.4 %all-to-all-done = bf16[256,4,128]{2,1,0:T(4,128)(2,1)S(1)} async-done(((bf16[256,4,128]{2,1,0:T(4,128)(2,1)}), bf16[256,4,128]{2,1,0:T(4,128)(2,1)S(1)}, u32[]{:S(2)}, u32[]{:S(2)}) %all-to-all-start) | async-done | bytes 262176 | tf_op jit(solution)/shard_map/all_to_all | solution.py:412
  55.1 0.7 %finish.1 = (f32[4,100]{1,0:T(4,128)}, f32[1,100]{1,0:T(1,128)}, f32[1,1]{1,0:T(1,128)}) custom-call(bf16[1024,128]{1,0:T(8,128)(2,1)S(1)} %bitcast.15), custom_call_target="tpu_custom_call" | custom-call | tf_op jit(solution)/shard_map/finish/pallas_call | solution.py:427
  (12 shorter events, 0.0 us)
Async XLA Ops:
  2.9 11.9 %collective-permute-start.1 = (bf16[2,400,128]{2,1,0:T(8,128)(2,1)S(1)}, bf16[2,400,128]{2,1,0:T(8,128)(2,1)S(1)}, u32[]{:S(2)}, u32[]{:S(2)}) collective-permute-start(bf16[2,400,128]{2,1,0:T(8,128)(2,1)S(1)} %get-tuple-element.50), channel_id=1, source_target_pairs={{0,64},{64,0},{128,192},{192,128},{1,65},{65,1},{129,193},{193,129... | collective-permute-start | bytes 614408 | tf_op jit(solution)/shard_map/ppermute | solution.py:385
  6.2 10.8 %collective-permute-start = (bf16[2,400,128]{2,1,0:T(8,128)(2,1)S(1)}, bf16[2,400,128]{2,1,0:T(8,128)(2,1)S(1)}, u32[]{:S(2)}, u32[]{:S(2)}) collective-permute-start(bf16[2,400,128]{2,1,0:T(8,128)(2,1)S(1)} %get-tuple-element.50), channel_id=1, source_target_pairs={{0,128},{64,192},{128,0},{192,64},{1,129},{65,193},{129,1},{193,65... | collective-permute-start | bytes 614408 | tf_op jit(solution)/shard_map/ppermute | solution.py:384
  9.7 5.1 %copy-start.4 = (f32[768]{0:T(1024)S(1)}, f32[768]{0:T(1024)}, u32[]{:S(2)}) copy-start(f32[768]{0:T(1024)} %param.10) | copy-start | bytes 9220
  9.7 6.4 %copy-start.1 = (f32[768,100]{0,1:T(8,128)S(1)}, f32[768,100]{0,1:T(8,128)}, u32[]{:S(2)}) copy-start(f32[768,100]{0,1:T(8,128)} %param.9) | copy-start | bytes 921604
  9.8 6.4 %copy-start.2 = (f32[100]{0:T(128)S(1)}, f32[100]{0:T(128)}, u32[]{:S(2)}) copy-start(f32[100]{0:T(128)} %param.8) | copy-start | bytes 1204
  9.8 6.3 %copy-start.3 = (f32[100]{0:T(128)S(1)}, f32[100]{0:T(128)}, u32[]{:S(2)}) copy-start(f32[100]{0:T(128)} %param.11) | copy-start | bytes 1204
  9.8 7.7 %collective-permute-start.4 = (bf16[2,400,128]{2,1,0:T(8,128)(2,1)S(1)}, bf16[2,400,128]{2,1,0:T(8,128)(2,1)S(1)}, u32[]{:S(2)}, u32[]{:S(2)}) collective-permute-start(bf16[2,400,128]{2,1,0:T(8,128)(2,1)S(1)} %get-tuple-element.59), channel_id=1, source_target_pairs={{0,64},{64,0},{128,192},{192,128},{1,65},{65,1},{129,193},{193,129... | collective-permute-start | bytes 614408 | tf_op jit(solution)/shard_map/ppermute | solution.py:385
  10.2 9.0 %collective-permute-start.3 = (bf16[2,400,128]{2,1,0:T(8,128)(2,1)S(1)}, bf16[2,400,128]{2,1,0:T(8,128)(2,1)S(1)}, u32[]{:S(2)}, u32[]{:S(2)}) collective-permute-start(bf16[2,400,128]{2,1,0:T(8,128)(2,1)S(1)} %get-tuple-element.59), channel_id=1, source_target_pairs={{0,128},{64,192},{128,0},{192,64},{1,129},{65,193},{129,1},{193,65... | collective-permute-start | bytes 614408 | tf_op jit(solution)/shard_map/ppermute | solution.py:384
  14.3 4.0 %collective-permute-start.5 = (bf16[2,400,128]{2,1,0:T(8,128)(2,1)S(1)}, bf16[2,400,128]{2,1,0:T(8,128)(2,1)S(1)}, u32[]{:S(2)}, u32[]{:S(2)}) collective-permute-start(bf16[2,400,128]{2,1,0:T(8,128)(2,1)S(1)} %get-tuple-element.58), channel_id=1, source_target_pairs={{0,64},{64,0},{128,192},{192,128},{1,65},{65,1},{129,193},{193,129... | collective-permute-start | bytes 614408 | tf_op jit(solution)/shard_map/ppermute | solution.py:385
  14.9 8.4 %collective-permute-start.2 = (bf16[2,400,128]{2,1,0:T(8,128)(2,1)S(1)}, bf16[2,400,128]{2,1,0:T(8,128)(2,1)S(1)}, u32[]{:S(2)}, u32[]{:S(2)}) collective-permute-start(bf16[2,400,128]{2,1,0:T(8,128)(2,1)S(1)} %get-tuple-element.58), channel_id=1, source_target_pairs={{0,128},{64,192},{128,0},{192,64},{1,129},{65,193},{129,1},{193,65... | collective-permute-start | bytes 614408 | tf_op jit(solution)/shard_map/ppermute | solution.py:384
  17.0 2.7 %collective-permute-start.6 = (bf16[2,400,128]{2,1,0:T(8,128)(2,1)S(1)}, bf16[2,400,128]{2,1,0:T(8,128)(2,1)S(1)}, u32[]{:S(2)}, u32[]{:S(2)}) collective-permute-start(bf16[2,400,128]{2,1,0:T(8,128)(2,1)S(1)} %collective-permute-done.refs_6_), channel_id=1, source_target_pairs={{0,64},{64,0},{128,192},{192,128},{1,65},{65,1},{129,193},{193,129... | collective-permute-start | bytes 614408 | tf_op jit(solution)/shard_map/ppermute | solution.py:385
  19.3 1.9 %collective-permute-start.7 = (bf16[2,400,128]{2,1,0:T(8,128)(2,1)S(1)}, bf16[2,400,128]{2,1,0:T(8,128)(2,1)S(1)}, u32[]{:S(2)}, u32[]{:S(2)}) collective-permute-start(bf16[2,400,128]{2,1,0:T(8,128)(2,1)S(1)} %collective-permute-done.3.refs_9_), channel_id=1, source_target_pairs={{0,64},{64,0},{128,192},{192,128},{1,65},{65,1},{129,193},{193,129... | collective-permute-start | bytes 614408 | tf_op jit(solution)/shard_map/ppermute | solution.py:385
  23.3 1.8 %collective-permute-start.8 = (bf16[2,400,128]{2,1,0:T(8,128)(2,1)S(1)}, bf16[2,400,128]{2,1,0:T(8,128)(2,1)S(1)}, u32[]{:S(2)}, u32[]{:S(2)}) collective-permute-start(bf16[2,400,128]{2,1,0:T(8,128)(2,1)S(1)} %collective-permute-done.2.far_ref), channel_id=1, source_target_pairs={{0,64},{64,0},{128,192},{192,128},{1,65},{65,1},{129,193},{193,129... | collective-permute-start | bytes 614408 | tf_op jit(solution)/shard_map/ppermute | solution.py:385
  25.1 14.7 %copy-start = (bf16[1024,100]{0,1:T(8,128)(2,1)S(1)}, bf16[1024,100]{0,1:T(8,128)(2,1)}, u32[]{:S(2)}) copy-start(bf16[1024,100]{0,1:T(8,128)(2,1)} %param.7) | copy-start | bytes 614404
  26.9 28.1 %all-to-all-start = ((bf16[256,4,128]{2,1,0:T(4,128)(2,1)}), bf16[256,4,128]{2,1,0:T(4,128)(2,1)S(1)}, u32[]{:S(2)}, u32[]{:S(2)}) async-start(bf16[256,4,128]{2,1,0:T(4,128)(2,1)} %bitcast.4), calls=%async_computation | async-start | bytes 524288 | tf_op jit(solution)/shard_map/all_to_all | solution.py:412

commit v6 on v5

--- a/solution.py
+++ b/solution.py
@@ -22,6 +22,13 @@
 
 def round_up(n, k):
     return -(-n // k) * k
+
+
+def add_length(spread, b, m, n, members, folded):
+    turn = (m - n) % members
+    if folded or turn in (0, members // 2):
+        return spread + b
+    return spread + 2.0 * b if turn < members // 2 else spread
 
 
 def half_turn(a):
@@ -118,10 +125,10 @@
             slopes = [jnp.zeros((8, LANES), F32) for _ in range(members)]
             for m in range(members):
                 mine = own[m] + half_turn(own[m]) if folded else own[m]
-                for other in sib:
+                for n, other in enumerate(sib):
                     a, b = slope_and_length(mine - other)
                     slopes[m] = slopes[m] + a
-                    spread = spread + b
+                    spread = add_length(spread, b, m, n, members, folded)
                 if folded:
                     slopes[m] = slopes[m] + half_turn(slopes[m])
             if folded:
@@ -161,10 +168,10 @@
             for m in range(members):
                 mine = own[m] + half_turn(own[m]) if folded else own[m]
                 slopes = jnp.zeros((8, LANES), F32)
-                for other in remote:
+                for n, other in enumerate(remote):
                     a, b = slope_and_length(mine - other)
                     slopes = slopes + a
-                    spread = spread + b
+                    spread = add_length(spread, b, m, n, members, folded)
                 if folded:
                     slopes = slopes + half_turn(slopes)
                 here = slice(m * LANES, (m + 1) * LANES)
@@ -241,10 +248,10 @@
             for m in range(members):
                 mine = own[m] + half_turn(own[m]) if folded else own[m]
                 slopes = jnp.zeros((8, LANES), F32)
-                for other in remote:
+                for n, other in enumerate(remote):
                     a, b = slope_and_length(mine - other)
                     slopes = slopes + a
-                    spread = spread + b
+                    spread = add_length(spread, b, m, n, members, folded)
                 if folded:
                     slopes = slopes + half_turn(slopes)
                 here = slice(m * LANES, (m + 1) * LANES)

time: 56 us -> 56 us (level)
  transfers between devices with their start and end apart: 10 -> 10, of which waited for: 3 -> 3; matrix products, arithmetic and copies ran while one was open for 0% -> 0% of each run, Pallas kernels for 28% -> 27%
where the time goes in v6:
time: 56 us; the launch traced here: 55.8 us
  starting transfers between devices  23 us (41%)
  Pallas kernels  20 us (36%)
  waiting for transfers between devices  11.8 us (21%)
  between operations  0.79 us (1%)
    all_to_all x1, starting transfers between devices, shards(): lax.all_to_all(packed, ('member', 'point'), split_axis=0, concat_axis=0,...  12.8 us
    all_to_all x1, waiting for transfers between devices, shards(): lax.all_to_all(packed, ('member', 'point'), split_axis=0, concat_axis=0,...  10.4 us
    pallas_call x3, Pallas kernels, forecast(): pl.pallas_call(functools.partial(forecast_kernel, first=first), in_specs=...  6.84 us
    ppermute x6, starting transfers between devices, shards(): beside = lambda a: lax.ppermute(a, 'member', core_swap)  5.96 us
    pallas_call x1, Pallas kernels, shards(): pl.pallas_call(slope_kernel, grid=(points // LANES,), in_specs=[tile((LAN...  4.79 us
    pallas_call x3, Pallas kernels, far(): pl.pallas_call(functools.partial(far_kernel, first=first, before=len(sums...  4.61 us
    ppermute x3, starting transfers between devices, shards(): across = lambda a: lax.ppermute(a, 'member', chip_swap)  4.24 us
    pallas_call x3, Pallas kernels, near(): pl.pallas_call(functools.partial(near_kernel, first=first, members=member...  2.6 us
  transfers between devices with their start and end apart: 10, of which 3 were waited for; matrix products, arithmetic and copies ran while one was open for 0% of the time, Pallas kernels for 27%

profile of v6, /device:TPU:1, one launch (start us, length us, event | category | flops | bytes accessed | tf_op | source)
XLA Modules:
  0.0 55.8 jit_solution(5784525524128366979)
XLA Ops:
  0.6 2.3 %forecast.3 = (bf16[2,4,128,1024]{3,2,1,0:T(8,128)(2,1)S(1)}, f32[2,104,512]{2,1,0:T(8,128)S(1)}, bf16[2,400,128]{2,1,0:T(8,128)(2,1)S(1)}) custom-call(bf16[4,768,1024]{2,1,0:T(8,128)(2,1)} %x_hbm.5, bf16[100,1024]{1,0:T(8,128)(2,1)} %bitcast.8), custom_call_target="tpu_custom_call" | custom-call | flops 10000000 | bytes 35000 | tf_op jit(solution)/shard_map/forecast/pallas_call | solution.py:326
  2.9 3.3 %collective-permute-start.1 = (bf16[2,400,128]{2,1,0:T(8,128)(2,1)S(1)}, bf16[2,400,128]{2,1,0:T(8,128)(2,1)S(1)}, u32[]{:S(2)}, u32[]{:S(2)}) collective-permute-start(bf16[2,400,128]{2,1,0:T(8,128)(2,1)S(1)} %get-tuple-element.50), channel_id=1, source_target_pairs={{0,64},{64,0},{128,192},{192,128},{1,65},{65,1},{129,193},{193,129... | collective-permute-start | bytes 614408 | tf_op jit(solution)/shard_map/ppermute | solution.py:392
  6.2 1.2 %collective-permute-start = (bf16[2,400,128]{2,1,0:T(8,128)(2,1)S(1)}, bf16[2,400,128]{2,1,0:T(8,128)(2,1)S(1)}, u32[]{:S(2)}, u32[]{:S(2)}) collective-permute-start(bf16[2,400,128]{2,1,0:T(8,128)(2,1)S(1)} %get-tuple-element.50), channel_id=1, source_target_pairs={{0,128},{64,192},{128,0},{192,64},{1,129},{65,193},{129,1},{193,65... | collective-permute-start | bytes 614408 | tf_op jit(solution)/shard_map/ppermute | solution.py:391
  7.4 2.3 %forecast.5 = (bf16[2,4,128,1024]{3,2,1,0:T(8,128)(2,1)S(1)}, f32[2,104,512]{2,1,0:T(8,128)S(1)}, bf16[2,400,128]{2,1,0:T(8,128)(2,1)S(1)}) custom-call(bf16[4,768,1024]{2,1,0:T(8,128)(2,1)} %x_hbm.5, bf16[100,1024]{1,0:T(8,128)(2,1)} %bitcast.9), custom_call_target="tpu_custom_call" | custom-call | flops 10000000 | bytes 35000 | tf_op jit(solution)/shard_map/forecast/pallas_call | solution.py:326
  9.7 0.0 copy-start.4
  9.7 0.0 copy-start.1
  9.8 0.0 copy-start.2
  9.8 0.0 copy-start.3
  9.8 0.4 collective-permute-start.4
  10.2 1.8 %collective-permute-start.3 = (bf16[2,400,128]{2,1,0:T(8,128)(2,1)S(1)}, bf16[2,400,128]{2,1,0:T(8,128)(2,1)S(1)}, u32[]{:S(2)}, u32[]{:S(2)}) collective-permute-start(bf16[2,400,128]{2,1,0:T(8,128)(2,1)S(1)} %get-tuple-element.59), channel_id=1, source_target_pairs={{0,128},{64,192},{128,0},{192,64},{1,129},{65,193},{129,1},{193,65... | collective-permute-start | bytes 614408 | tf_op jit(solution)/shard_map/ppermute | solution.py:391
  12.0 2.3 %forecast.4 = (bf16[2,4,128,1024]{3,2,1,0:T(8,128)(2,1)S(1)}, f32[2,104,512]{2,1,0:T(8,128)S(1)}, bf16[2,400,128]{2,1,0:T(8,128)(2,1)S(1)}) custom-call(bf16[4,768,1024]{2,1,0:T(8,128)(2,1)} %x_hbm.5, bf16[100,1024]{1,0:T(8,128)(2,1)} %bitcast.10), custom_call_target="tpu_custom_call" | custom-call | flops 10000000 | bytes 35000 | tf_op jit(solution)/shard_map/forecast/pallas_call | solution.py:326
  14.3 0.5 collective-permute-start.5
  14.9 1.3 %collective-permute-start.2 = (bf16[2,400,128]{2,1,0:T(8,128)(2,1)S(1)}, bf16[2,400,128]{2,1,0:T(8,128)(2,1)S(1)}, u32[]{:S(2)}, u32[]{:S(2)}) collective-permute-start(bf16[2,400,128]{2,1,0:T(8,128)(2,1)S(1)} %get-tuple-element.58), channel_id=1, source_target_pairs={{0,128},{64,192},{128,0},{192,64},{1,129},{65,193},{129,1},{193,65... | collective-permute-start | bytes 614408 | tf_op jit(solution)/shard_map/ppermute | solution.py:391
  16.1 0.9 %near.3 = (f32[2,104,512]{2,1,0:T(8,128)S(1)}, f32[8,128]{1,0:T(8,128)S(1)}, f32[104,128]{1,0:T(8,128)S(1)}) custom-call(f32[2,104,512]{2,1,0:T(8,128)S(1)} %get-tuple-element.53.own_ref.refs_0_, bf16[2,400,128]{2,1,0:T(8,128)(2,1)S(1)} %collective-permute-done.1.sib_ref, f32[100,768]{1,0:T(8,128)S(1)} %bitcast.12, ...), custom_call_target="tpu_custom_call" | custom-call | flops 10000000 | bytes 35000 | tf_op jit(solution)/shard_map/near/pallas_call | solution.py:346
  17.0 0.4 collective-permute-start.6
  17.4 0.0 collective-permute-done.4.sib_ref
  17.4 0.9 %near.4 = (f32[2,104,512]{2,1,0:T(8,128)S(1)}, f32[8,128]{1,0:T(8,128)S(1)}) custom-call(f32[2,104,512]{2,1,0:T(8,128)S(1)} %get-tuple-element.60.own_ref.refs_0_, bf16[2,400,128]{2,1,0:T(8,128)(2,1)S(1)} %collective-permute-done.4.sib_ref, f32[100,768]{1,0:T(8,128)S(1)} %bitcast.13, f32[1,768]{1,0:T(1,128)S(1)} %broadcast_in_dim.9.area_ref.refs_2_, ...), custom_call_target="tpu_custom_call" | custom-call | flops 8000000000 | bytes 28000000 | tf_op jit(solution)/shard_map/near/pallas_call | solution.py:346
  18.3 0.0 collective-permute-done.5.sib_ref
  18.3 0.9 %near.5 = (f32[2,104,512]{2,1,0:T(8,128)S(1)}, f32[8,128]{1,0:T(8,128)S(1)}) custom-call(f32[2,104,512]{2,1,0:T(8,128)S(1)} %get-tuple-element.57.own_ref.refs_0_, bf16[2,400,128]{2,1,0:T(8,128)(2,1)S(1)} %collective-permute-done.5.sib_ref, f32[100,768]{1,0:T(8,128)S(1)} %bitcast.14, f32[1,768]{1,0:T(1,128)S(1)} %broadcast_in_dim.9.area_ref.refs_2_, ...), custom_call_target="tpu_custom_call" | custom-call | flops 10000000 | bytes 35000 | tf_op jit(solution)/shard_map/near/pallas_call | solution.py:346
  19.2 0.5 collective-permute-start.7
  19.7 1.4 %far.3 = (bf16[2,128,512]{2,1,0:T(8,128)(2,1)S(1)}, f32[128,1024]{1,0:T(8,128)S(1)}, f32[104,128]{1,0:T(8,128)S(1)}, f32[8,128]{1,0:T(8,128)S(1)}) custom-call(f32[2,104,512]{2,1,0:T(8,128)S(1)} %get-tuple-element.53.own_ref.refs_0_, f32[2,104,512]{2,1,0:T(8,128)S(1)} %get-tuple-element.69.refs_1_, f32[1,768]{1,0:T(1,128)S(1)} %broadcast_in_dim.9.area_ref.refs_2_, ...), custom_call_target="tpu_custom_call" | custom-call | flops 8000000000 | bytes 28000000 | tf_op jit(solution)/shard_map/far/pallas_call | solution.py:378
  21.1 1.4 %far.4 = (bf16[2,128,512]{2,1,0:T(8,128)(2,1)S(1)}, f32[128,1024]{1,0:T(8,128)S(1)}, f32[104,128]{1,0:T(8,128)S(1)}, f32[8,128]{1,0:T(8,128)S(1)}) custom-call(f32[2,104,512]{2,1,0:T(8,128)S(1)} %get-tuple-element.60.own_ref.refs_0_, f32[2,104,512]{2,1,0:T(8,128)S(1)} %get-tuple-element.65.refs_1_, f32[1,768]{1,0:T(1,128)S(1)} %broadcast_in_dim.9.area_ref.refs_2_, ...), custom_call_target="tpu_custom_call" | custom-call | flops 10000000 | bytes 35000 | tf_op jit(solution)/shard_map/far/pallas_call | solution.py:378
  22.6 0.7 %collective-permute-done.2.far_ref = bf16[2,400,128]{2,1,0:T(8,128)(2,1)S(1)} collective-permute-done((bf16[2,400,128]{2,1,0:T(8,128)(2,1)S(1)}, bf16[2,400,128]{2,1,0:T(8,128)(2,1)S(1)}, u32[]{:S(2)}, u32[]{:S(2)}) %collective-permute-start.2) | collective-permute-done | bytes 204832 | tf_op jit(solution)/shard_map/ppermute | solution.py:391
  23.3 0.7 %collective-permute-start.8 = (bf16[2,400,128]{2,1,0:T(8,128)(2,1)S(1)}, bf16[2,400,128]{2,1,0:T(8,128)(2,1)S(1)}, u32[]{:S(2)}, u32[]{:S(2)}) collective-permute-start(bf16[2,400,128]{2,1,0:T(8,128)(2,1)S(1)} %collective-permute-done.2.far_ref), channel_id=1, source_target_pairs={{0,64},{64,0},{128,192},{192,128},{1,65},{65,1},{129,193},{193,129... | collective-permute-start | bytes 614408 | tf_op jit(solution)/shard_map/ppermute | solution.py:392
  24.0 0.5 direct.1
  24.5 0.6 %collective-permute-done.8.refs_9_ = bf16[2,400,128]{2,1,0:T(8,128)(2,1)S(1)} collective-permute-done((bf16[2,400,128]{2,1,0:T(8,128)(2,1)S(1)}, bf16[2,400,128]{2,1,0:T(8,128)(2,1)S(1)}, u32[]{:S(2)}, u32[]{:S(2)}) %collective-permute-start.8) | collective-permute-done | bytes 204832 | tf_op jit(solution)/shard_map/ppermute | solution.py:392
  25.1 1.8 %far.5 = (bf16[2,128,512]{2,1,0:T(8,128)(2,1)S(1)}, bf16[1024,128]{1,0:T(8,128)(2,1)}) custom-call(f32[2,104,512]{2,1,0:T(8,128)S(1)} %get-tuple-element.57.own_ref.refs_0_, f32[2,104,512]{2,1,0:T(8,128)S(1)} %get-tuple-element.83.refs_1_, f32[1,768]{1,0:T(1,128)S(1)} %broadcast_in_dim.9.area_ref.refs_2_, f32[104,128]{1,0:T(8,128)S(1)} %get-tuple-element.66.refs_3_.coefs, ...), custom_call_target="tpu_custom_call" | custom-call | flops 10000000 | bytes 35000 | tf_op jit(solution)/shard_map/far/pallas_call | solution.py:378
  26.9 12.8 %all-to-all-start = ((bf16[256,4,128]{2,1,0:T(4,128)(2,1)}), bf16[256,4,128]{2,1,0:T(4,128)(2,1)S(1)}, u32[]{:S(2)}, u32[]{:S(2)}) async-start(bf16[256,4,128]{2,1,0:T(4,128)(2,1)} %bitcast.4), calls=%async_computation | async-start | bytes 524288 | tf_op jit(solution)/shard_map/all_to_all | solution.py:419
  39.7 0.1 pad_maximum_fusion.grad_ref
  39.8 4.8 %slope.1 = bf16[4,768,1024]{2,1,0:T(8,128)(2,1)} custom-call(bf16[6,128,512]{2,1,0:T(8,128)(2,1)S(1)} %pad_maximum_fusion.grad_ref, bf16[100,1024]{1,0:T(8,128)(2,1)S(1)} %bitcast.11), custom_call_target="tpu_custom_call" | custom-call | flops 5000000000 | bytes 17500000 | tf_op jit(solution)/shard_map/slope/pallas_call | solution.py:422
  44.6 10.4 %all-to-all-done = bf16[256,4,128]{2,1,0:T(4,128)(2,1)S(1)} async-done(((bf16[256,4,128]{2,1,0:T(4,128)(2,1)}), bf16[256,4,128]{2,1,0:T(4,128)(2,1)S(1)}, u32[]{:S(2)}, u32[]{:S(2)}) %all-to-all-start) | async-done | bytes 262176 | tf_op jit(solution)/shard_map/all_to_all | solution.py:419
  55.0 0.7 %finish.1 = (f32[4,100]{1,0:T(4,128)}, f32[1,100]{1,0:T(1,128)}, f32[1,1]{1,0:T(1,128)}) custom-call(bf16[1024,128]{1,0:T(8,128)(2,1)S(1)} %bitcast.15), custom_call_target="tpu_custom_call" | custom-call | tf_op jit(solution)/shard_map/finish/pallas_call | solution.py:434
  (12 shorter events, 0.0 us)
Async XLA Ops:
  2.9 11.9 %collective-permute-start.1 = (bf16[2,400,128]{2,1,0:T(8,128)(2,1)S(1)}, bf16[2,400,128]{2,1,0:T(8,128)(2,1)S(1)}, u32[]{:S(2)}, u32[]{:S(2)}) collective-permute-start(bf16[2,400,128]{2,1,0:T(8,128)(2,1)S(1)} %get-tuple-element.50), channel_id=1, source_target_pairs={{0,64},{64,0},{128,192},{192,128},{1,65},{65,1},{129,193},{193,129... | collective-permute-start | bytes 614408 | tf_op jit(solution)/shard_map/ppermute | solution.py:392
  6.2 10.7 %collective-permute-start = (bf16[2,400,128]{2,1,0:T(8,128)(2,1)S(1)}, bf16[2,400,128]{2,1,0:T(8,128)(2,1)S(1)}, u32[]{:S(2)}, u32[]{:S(2)}) collective-permute-start(bf16[2,400,128]{2,1,0:T(8,128)(2,1)S(1)} %get-tuple-element.50), channel_id=1, source_target_pairs={{0,128},{64,192},{128,0},{192,64},{1,129},{65,193},{129,1},{193,65... | collective-permute-start | bytes 614408 | tf_op jit(solution)/shard_map/ppermute | solution.py:391
  9.7 5.1 %copy-start.4 = (f32[768]{0:T(1024)S(1)}, f32[768]{0:T(1024)}, u32[]{:S(2)}) copy-start(f32[768]{0:T(1024)} %param.10) | copy-start | bytes 9220
  9.7 6.4 %copy-start.1 = (f32[768,100]{0,1:T(8,128)S(1)}, f32[768,100]{0,1:T(8,128)}, u32[]{:S(2)}) copy-start(f32[768,100]{0,1:T(8,128)} %param.9) | copy-start | bytes 921604
  9.8 6.4 %copy-start.2 = (f32[100]{0:T(128)S(1)}, f32[100]{0:T(128)}, u32[]{:S(2)}) copy-start(f32[100]{0:T(128)} %param.8) | copy-start | bytes 1204
  9.8 6.3 %copy-start.3 = (f32[100]{0:T(128)S(1)}, f32[100]{0:T(128)}, u32[]{:S(2)}) copy-start(f32[100]{0:T(128)} %param.11) | copy-start | bytes 1204
  9.8 7.7 %collective-permute-start.4 = (bf16[2,400,128]{2,1,0:T(8,128)(2,1)S(1)}, bf16[2,400,128]{2,1,0:T(8,128)(2,1)S(1)}, u32[]{:S(2)}, u32[]{:S(2)}) collective-permute-start(bf16[2,400,128]{2,1,0:T(8,128)(2,1)S(1)} %get-tuple-element.59), channel_id=1, source_target_pairs={{0,64},{64,0},{128,192},{192,128},{1,65},{65,1},{129,193},{193,129... | collective-permute-start | bytes 614408 | tf_op jit(solution)/shard_map/ppermute | solution.py:392
  10.2 9.0 %collective-permute-start.3 = (bf16[2,400,128]{2,1,0:T(8,128)(2,1)S(1)}, bf16[2,400,128]{2,1,0:T(8,128)(2,1)S(1)}, u32[]{:S(2)}, u32[]{:S(2)}) collective-permute-start(bf16[2,400,128]{2,1,0:T(8,128)(2,1)S(1)} %get-tuple-element.59), channel_id=1, source_target_pairs={{0,128},{64,192},{128,0},{192,64},{1,129},{65,193},{129,1},{193,65... | collective-permute-start | bytes 614408 | tf_op jit(solution)/shard_map/ppermute | solution.py:391
  14.3 4.0 %collective-permute-start.5 = (bf16[2,400,128]{2,1,0:T(8,128)(2,1)S(1)}, bf16[2,400,128]{2,1,0:T(8,128)(2,1)S(1)}, u32[]{:S(2)}, u32[]{:S(2)}) collective-permute-start(bf16[2,400,128]{2,1,0:T(8,128)(2,1)S(1)} %get-tuple-element.58), channel_id=1, source_target_pairs={{0,64},{64,0},{128,192},{192,128},{1,65},{65,1},{129,193},{193,129... | collective-permute-start | bytes 614408 | tf_op jit(solution)/shard_map/ppermute | solution.py:392
  14.9 8.4 %collective-permute-start.2 = (bf16[2,400,128]{2,1,0:T(8,128)(2,1)S(1)}, bf16[2,400,128]{2,1,0:T(8,128)(2,1)S(1)}, u32[]{:S(2)}, u32[]{:S(2)}) collective-permute-start(bf16[2,400,128]{2,1,0:T(8,128)(2,1)S(1)} %get-tuple-element.58), channel_id=1, source_target_pairs={{0,128},{64,192},{128,0},{192,64},{1,129},{65,193},{129,1},{193,65... | collective-permute-start | bytes 614408 | tf_op jit(solution)/shard_map/ppermute | solution.py:391
  17.0 2.7 %collective-permute-start.6 = (bf16[2,400,128]{2,1,0:T(8,128)(2,1)S(1)}, bf16[2,400,128]{2,1,0:T(8,128)(2,1)S(1)}, u32[]{:S(2)}, u32[]{:S(2)}) collective-permute-start(bf16[2,400,128]{2,1,0:T(8,128)(2,1)S(1)} %collective-permute-done.refs_6_), channel_id=1, source_target_pairs={{0,64},{64,0},{128,192},{192,128},{1,65},{65,1},{129,193},{193,129... | collective-permute-start | bytes 614408 | tf_op jit(solution)/shard_map/ppermute | solution.py:392
  19.2 1.9 %collective-permute-start.7 = (bf16[2,400,128]{2,1,0:T(8,128)(2,1)S(1)}, bf16[2,400,128]{2,1,0:T(8,128)(2,1)S(1)}, u32[]{:S(2)}, u32[]{:S(2)}) collective-permute-start(bf16[2,400,128]{2,1,0:T(8,128)(2,1)S(1)} %collective-permute-done.3.refs_9_), channel_id=1, source_target_pairs={{0,64},{64,0},{128,192},{192,128},{1,65},{65,1},{129,193},{193,129... | collective-permute-start | bytes 614408 | tf_op jit(solution)/shard_map/ppermute | solution.py:392
  23.3 1.8 %collective-permute-start.8 = (bf16[2,400,128]{2,1,0:T(8,128)(2,1)S(1)}, bf16[2,400,128]{2,1,0:T(8,128)(2,1)S(1)}, u32[]{:S(2)}, u32[]{:S(2)}) collective-permute-start(bf16[2,400,128]{2,1,0:T(8,128)(2,1)S(1)} %collective-permute-done.2.far_ref), channel_id=1, source_target_pairs={{0,64},{64,0},{128,192},{192,128},{1,65},{65,1},{129,193},{193,129... | collective-permute-start | bytes 614408 | tf_op jit(solution)/shard_map/ppermute | solution.py:392
  25.1 14.7 %copy-start = (bf16[1024,100]{0,1:T(8,128)(2,1)S(1)}, bf16[1024,100]{0,1:T(8,128)(2,1)}, u32[]{:S(2)}) copy-start(bf16[1024,100]{0,1:T(8,128)(2,1)} %param.7) | copy-start | bytes 614404
  26.9 28.1 %all-to-all-start = ((bf16[256,4,128]{2,1,0:T(4,128)(2,1)}), bf16[256,4,128]{2,1,0:T(4,128)(2,1)S(1)}, u32[]{:S(2)}, u32[]{:S(2)}) async-start(bf16[256,4,128]{2,1,0:T(4,128)(2,1)} %bitcast.4), calls=%async_computation | async-start | bytes 524288 | tf_op jit(solution)/shard_map/all_to_all | solution.py:419
